TPU v7x, 32 devices: a whole 2x2x4 slice. The times are simulated.
32 devices in a mesh: row: 4 (over y, x), col: 8 (over z, core).
Axes of the slice: x: 2, y: 2, z: 4, core: 2. Of those that a mesh axis runs over, the one named last changes fastest.
Arguments:
- density: float32 [2560, 2560], P('row', 'col'), as said below
- pattern: int32 [40, 40], P('row', 'col'), may hold values from 0 to 1, as said below
- weights: float32 [2560], P('row'), may hold values from 0.5 to 5
Outputs:
- purified: float32 [2560, 2560], P('row', 'col')
- checks: float32 [2, 2560], P(None, 'col')
Inputs may be any that keep to these rules, and one draw needn't show every extreme that they name: pattern is symmetric, and every block with |a - b| <= 2 is nonzero; the number of nonzero blocks differs strongly between block rows. density is symmetric and zero outside the blocks that pattern marks.
All inputs are finite; a program needn't handle non-finite values.
Results may differ from a plain program's by a relative error of at most 0.00012.
Values sent between devices are 32-bit elements; how exact they have to be, the bound alone decides.
No kernel may reach another device: no remote copies, remote signals or barrier semaphores. Data moves between devices by JAX's collectives and lax.ppermute only.
A program may use at most 64 MiB of HBM per device.

v0:
```python
import jax
import jax.numpy as jnp
from jax import lax
from jax.sharding import PartitionSpec as P

BLK = 64


def full_dot(first, second):
    return jnp.dot(
        first, second, precision=lax.Precision.HIGHEST, preferred_element_type=jnp.float32
    )


def expand_mask(pattern):
    return jnp.repeat(jnp.repeat(pattern.astype(jnp.float32), BLK, axis=0), BLK, axis=1)


def multiply(left_tile, column, weight_row):
    partial_row = full_dot(weight_row, left_tile)
    result = full_dot(lax.all_gather(left_tile, "col", axis=1, tiled=True), column)
    summed = lax.psum(partial_row, "row")
    full_check = lax.all_gather(summed, "col", axis=1, tiled=True)
    check_row = full_dot(full_check, column)
    return (result, check_row)


def body(density, pattern, weights):
    block_mask = expand_mask(pattern)
    current = density
    weight_row = weights[None, :]
    checks = []
    column = lax.all_gather(current, "row", axis=0, tiled=True)
    square, first_check = multiply(current, column, weight_row)
    square = block_mask * square
    cube_term, second_check = multiply(square, column, weight_row)
    cube_term = block_mask * cube_term
    current = 3.0 * square - 2.0 * cube_term
    checks.append(first_check)
    checks.append(second_check)
    return (current, jnp.concatenate(checks, axis=0))


def solution(mesh):
    in_specs = (P("row", "col"), P("row", "col"), P("row"))
    out_specs = (P("row", "col"), P(None, "col"))
    return jax.shard_map(body, mesh=mesh, in_specs=in_specs, out_specs=out_specs, check_vma=False)
```

profile of v0, /device:TPU:0, one launch (start us, length us, event | category | flops | bytes accessed | tf_op | source)
XLA Modules:
  0.0 223.8 jit_solution(9711572545245477868)
XLA Ops:
  7.2 0.7 all-gather.6.cloned.1.call-update
  7.9 0.0 all-gather.4.cloned.1.call-start
  7.9 0.7 all-gather.4.cloned.1.call-update
  8.6 0.0 all-gather.8.cloned.1.call-start
  8.7 0.7 convert_element_type.3
  9.4 0.1 broadcast_in_dim.7
  9.5 0.1 reshape.24
  9.5 48.1 %all-gather.6.cloned.1.call-done = f32[2560,320]{0,1:T(8,128)} async-done(((f32[640,320]{0,1:T(8,128)}), f32[2560,320]{0,1:T(8,128)}) %all-gather.6.cloned.1.call-update) | async-done | bytes 3276816 | tf_op jit(solution)/shard_map/all_gather | solution.py:33
  57.7 68.6 %all-gather.4.cloned.1.call-done = f32[640,2560]{0,1:T(8,128)} async-done(((f32[640,320]{0,1:T(8,128)}), f32[640,2560]{0,1:T(8,128)}) %all-gather.4.cloned.1.call-update) | async-done | bytes 6553616 | tf_op jit(solution)/shard_map/all_gather | solution.py:21
  126.3 0.1 broadcast_in_dim.8
  126.3 0.9 copy-done.1
  127.2 12.0 %convolution_multiply_fusion.1 = f32[640,320]{0,1:T(8,128)} fusion(f32[640,320]{0,1:T(8,128)S(1)} %bitcast.16, f32[640,2560]{0,1:T(8,128)} %all-gather.4.cloned.1.call-done, f32[2560,320]{0,1:T(8,128)} %all-gather.6.cloned.1.call-done), kind=kOutput, calls=%fused_computation.1 | convolution fusion | flops 6291660800 | bytes 11468800 | tf_op jit(solution)/shard_map/dot_general | solution.py:10
  139.2 0.6 dynamic-slice
  140.5 1.9 fusion.2
  142.4 1.9 fusion.4
  144.3 9.9 %all-reduce.3 = (f32[1,320]{1,0:T(1,128)S(1)}, f32[1,320]{1,0:T(1,128)S(1)}) all-reduce(f32[1,320]{1,0:T(1,128)S(1)} %fusion.4, f32[1,320]{1,0:T(1,128)S(1)} %fusion.2), channel_id=1, replica_groups=mesh['row'=4,'col'=8] {'row'}, use_global_device_ids=true, to_apply=%region_1.0 | all-reduce | flops 640 | bytes 5120 | tf_op jit(solution)/shard_map/psum | solution.py:22
  154.2 0.3 dynamic-update-slice
  154.5 0.3 dynamic-update-slice.1
  154.8 27.3 %all-reduce.2 = (f32[2560]{0:T(1024)S(1)}, f32[2560]{0:T(1024)S(1)}) all-reduce(f32[2560]{0:T(1024)S(1)} %dynamic-update-slice.1, f32[2560]{0:T(1024)S(1)} %dynamic-update-slice), channel_id=1, replica_groups=mesh['row'=4,'col'=8] {'col'}, use_global_device_ids=true, to_apply=%add.1 | all-reduce | flops 5120 | bytes 40960 | tf_op jit(solution)/shard_map/reshape.10
  182.2 2.7 %fusion.3 = f32[1,320]{1,0:T(1,128)S(1)} fusion(f32[2560,1]{0,1:T(1,128)S(1)} %reshape.42, f32[2560,320]{0,1:T(8,128)S(1)} %copy-done), kind=kOutput, calls=%fused_computation.6 | convolution fusion | flops 9830400 | bytes 3288320 | tf_op jit(solution)/shard_map/dot_general | solution.py:10
  184.8 2.7 %fusion.5 = f32[1,320]{1,0:T(1,128)S(1)} fusion(f32[2560,1]{0,1:T(1,128)S(1)} %reshape.46, f32[2560,320]{0,1:T(8,128)S(1)} %copy-done), kind=kOutput, calls=%fused_computation.8 | convolution fusion | flops 9830400 | bytes 3288320 | tf_op jit(solution)/shard_map/dot_general | solution.py:10
  187.5 0.6 pad_maximum_fusion
  188.1 17.2 %all-gather.8.cloned.1.call-done = f32[640,2560]{0,1:T(8,128)} async-done(((f32[640,320]{0,1:T(8,128)}), f32[640,2560]{0,1:T(8,128)}) %all-gather.8.cloned.1.call-update) | async-done | bytes 6553616 | tf_op jit(solution)/shard_map/all_gather | solution.py:21
  205.3 11.9 %fusion.1 = f32[640,320]{0,1:T(8,128)} fusion(f32[640,320]{0,1:T(8,128)} %bitcast.17, f32[640,2560]{0,1:T(8,128)} %all-gather.8.cloned.1.call-done, f32[2560,320]{0,1:T(8,128)S(1)} %copy-done, f32[640,320]{0,1:T(8,128)} %convolution_multiply_fusion.1), kind=kOutput, calls=%fused_computation.3 | convolution fusion | flops 6292275200 | bytes 12288000 | tf_op jit(solution)/shard_map/dot_general | solution.py:10
  (16 shorter events, 0.1 us)
Async XLA Ops:
  7.2 50.5 %all-gather.6.cloned.1.call-start = ((), (), s32[]{:S(2)}) async-start(), calls=%async_computation.1 | async-start | bytes 4096000 | tf_op jit(solution)/shard_map/all_gather | solution.py:33
  7.9 118.4 %all-gather.4.cloned.1.call-start = ((), (), s32[]{:S(2)}) async-start(), calls=%async_computation | async-start | bytes 7372800 | tf_op jit(solution)/shard_map/all_gather | solution.py:21
  8.6 196.7 %all-gather.8.cloned.1.call-start = ((), (), s32[]{:S(2)}) async-start(), calls=%async_computation.2 | async-start | bytes 7372800 | tf_op jit(solution)/shard_map/all_gather | solution.py:21
  126.3 0.9 copy-start.1
  127.2 12.0 %copy-start.2 = (f32[640]{0:T(1024)S(1)}, f32[640]{0:T(1024)}, u32[]{:S(2)}) copy-start(f32[640]{0:T(1024)} %param.5) | copy-start | bytes 7684
  127.2 12.0 %copy-start.3 = (u32[32]{0:T(128)S(1)}, u32[32]{0:T(128)}, u32[]{:S(2)}) copy-start(u32[32]{0:T(128)} %constant.7) | copy-start | bytes 388
  127.2 54.9 %copy-start = (f32[2560,320]{0,1:T(8,128)S(1)}, f32[2560,320]{0,1:T(8,128)}, u32[]{:S(2)}) copy-start(f32[2560,320]{0,1:T(8,128)} %all-gather.6.cloned.1.call-done) | copy-start | bytes 9830404
Sparse Core Ops, SparseCore 0:
  9.8 47.7 all-gather.5
  59.3 66.9 all-gather.3
  139.3 65.9 all-gather.7
where the time goes:
time: 224 us
  waiting for transfers between devices  135 us (60%)
  blocking collectives  37.2 us (17%)
  matrix products  33 us (15%)
  between operations  14.5 us (6%)
  local copies, waits for them, and re-layouts  2.25 us (1%)
    all_gather x2, waiting for transfers between devices, multiply(): lax.all_gather(left_tile, 'col', axis=1, tiled=True)  85.8 us
    all_gather x1, waiting for transfers between devices, body(): column = lax.all_gather(current, 'row', axis=0, tiled=True)  48.1 us
    dot_general x6, matrix products, full_dot(): jnp.dot(first, second, precision=lax.Precision.HIGHEST, preferred_element...  33 us
    another operation x1, blocking collectives  27.3 us
    psum x1, blocking collectives, multiply(): summed = lax.psum(partial_row, 'row')  9.87 us
  transfers between devices with their start and end apart: 3, of which 3 were waited for; matrix products, arithmetic and copies ran while one was open for 5% of the time, Pallas kernels for 0%

commit v1 on v0

v1 whole, which is shorter than its diff:
```python
import jax
import jax.numpy as jnp
from jax import lax
from jax.sharding import PartitionSpec as P

BLK = 64


def dot(first, second, contract=((1,), (0,))):
    return lax.dot_general(
        first, second, (contract, ((), ())), precision=lax.Precision.HIGH, preferred_element_type=jnp.float32
    )


def expand_mask(pattern):
    return jnp.repeat(jnp.repeat(pattern.astype(jnp.float32), BLK, axis=0), BLK, axis=1)


def make_body(panels, columns):
    assert columns == 2 * panels and panels & (panels - 1) == 0

    def flat(r, z, core):
        return r * columns + 2 * z + core

    def send(value, target):
        pairs = []
        for r in range(panels):
            for z in range(panels):
                to = target(r, z)
                if to is not None:
                    pairs += [(flat(r, z, core), flat(*to, core)) for core in (0, 1)]
        return lax.ppermute(value, ("row", "col"), pairs)

    def swap_core(value):
        return lax.ppermute(value, "col", [(c, c ^ 1) for c in range(columns)])

    def ring(step):
        return lambda r, z: (r, (z + step) % panels)

    def others_ring(step):
        def target(r, z):
            if z == r:
                return None
            line = [q for q in range(panels) if q != r]
            return (r, line[(line.index(z) + step) % len(line)])

        return target

    def across(m):
        return lambda r, z: (r ^ m, z)

    def to_diagonal(m):
        return lambda r, z: (r ^ m, z) if r ^ m == z else None

    def row_sum(value):
        m = 1
        while m < panels:
            value = value + send(value, across(m))
            m *= 2
        return value

    def gather_ring(value, ring_of, count):
        got = {0: value}
        for j in range(1, count // 2 + 1):
            got[j] = send(got[j - 1], ring_of(1))
        for j in range(count - 1, count // 2, -1):
            got[j] = send(got[(j + 1) % count], ring_of(-1))
        return got

    def body(density, pattern, weights):
        r = lax.axis_index("row")
        c = lax.axis_index("col")
        z, core = c // 2, c % 2
        half = density.shape[1]
        block_mask = expand_mask(pattern)
        line_pattern = lax.all_gather(pattern, "col", axis=0)
        diagonal_mask = expand_mask(lax.dynamic_index_in_dim(line_pattern, 2 * r + core, 0, keepdims=False))

        def own_rows(value):
            mine = lax.dynamic_slice_in_dim(value, core * half, half, 0)
            given = lax.dynamic_slice_in_dim(value, (1 - core) * half, half, 0)
            return mine, swap_core(given)

        def finish(kept_and_given):
            return kept_and_given[:, :half] + swap_core(kept_and_given[:, half:])

        left = gather_ring(density, ring, panels)
        own = jnp.concatenate(own_rows(density), axis=1)
        right = jnp.stack([own] + [send(own, across(m)) for m in range(1, panels)])

        def right_of(k):
            return lax.dynamic_index_in_dim(right, r ^ k, 0, keepdims=False)

        product = sum(dot(left[j], right_of((z - j) % panels)) for j in (0, 1, 3, 2) + tuple(range(4, panels)))
        product = finish(product)
        square = block_mask * product

        weight_row = weights[None, :]
        sums = row_sum(jnp.sum(jnp.stack([product, square]) * weights[None, :, None], axis=1))
        first_check, column_sums = sums[:1], sums[1]
        all_sums = lax.all_gather(column_sums, "col", axis=0).reshape(panels, 2, half)
        all_sums = lax.dynamic_index_in_dim(all_sums, core, 1, keepdims=False)
        ordered = jnp.take(all_sums, r ^ jnp.arange(panels), axis=0)
        second_partial = jnp.sum(right * ordered[:, :, None], axis=(0, 1))[None, :]
        second_check = finish(second_partial)

        others = gather_ring(square, others_ring, panels - 1)
        mine, theirs = own_rows(square)
        rows = jnp.where(core == 0, jnp.concatenate([mine, theirs], axis=1), jnp.concatenate([theirs, mine], axis=1))
        down = [send(rows, to_diagonal(m)) for m in range(1, panels)]

        def own_part(value, which):
            return lax.dynamic_slice_in_dim(value, which * half, half, 0)

        def diagonal(which):
            return sum(dot(left[j], own_part(left[j], which), ((1,), (1,))) for j in range(panels))

        diagonal_square = diagonal_mask * (diagonal(core) + swap_core(diagonal(1 - core)))

        place = z - (z > r).astype(z.dtype)

        def on_diagonal():
            return sum(dot(down[m - 1], right[m], ((0,), (0,))) for m in range(1, panels))

        def off_diagonal():
            total = dot(diagonal_square, right_of(r))
            for j in range(1, panels - 1):
                q = (place - j) % (panels - 1)
                total = total + dot(others[j], right_of(q + (q >= r).astype(q.dtype)))
            return total

        cube = dot(square, right_of(z)) + lax.cond(z == r, on_diagonal, off_diagonal)
        cube_term = block_mask * finish(cube)
        return 3.0 * square - 2.0 * cube_term, jnp.concatenate([first_check, second_check], axis=0)

    return body


def solution(mesh):
    in_specs = (P("row", "col"), P("row", "col"), P("row"))
    out_specs = (P("row", "col"), P(None, "col"))
    body = make_body(mesh.shape["row"], mesh.shape["col"])
    return jax.shard_map(body, mesh=mesh, in_specs=in_specs, out_specs=out_specs, check_vma=False)
```

time: 224 us -> 172 us (0.77)
  waiting for transfers between devices: 135 us -> 35.2 us
  starting transfers between devices: 0.11 us -> 23.6 us
  between operations: 14.5 us -> 1.02 us
  matrix products: 33 us -> 45.5 us
  local copies, waits for them, and re-layouts: 2.25 us -> 13.6 us
  other arithmetic: 1.35 us -> 11.2 us
  blocking collectives: 37.2 us -> 40.7 us
    all_gather x3 -> x0, waiting for transfers between devices: 134 us -> none  [the longest x2 85.8 us: multiply(): lax.all_gather(left_tile, 'col', axis=1, tiled=True)]
    all_gather x0 -> x2, blocking collectives: none -> 40.7 us  [the longest x1 26.5 us: body(): lax.all_gather(column_sums, 'col', axis=0).reshape(panels, 2, half)]
    ppermute x0 -> x19, waiting for transfers between devices: none -> 35.2 us  [the longest x13 34.1 us: send(): return lax.ppermute(value, ('row', 'col'), pairs)]
    another operation x1 -> x0, blocking collectives: 27.3 us -> none
    ppermute x0 -> x19, starting transfers between devices: none -> 23.6 us  [the longest x13 21.9 us: send(): return lax.ppermute(value, ('row', 'col'), pairs)]
    dot_general x6 -> x16, matrix products: 33 us -> 45.5 us  [dot(): lax.dot_general(first, second, (contract, ((), ())), precision=lax.Precis...]
    psum x1 -> x0, blocking collectives: 9.87 us -> none  [multiply(): summed = lax.psum(partial_row, 'row')]
    another operation x0 -> x3, other arithmetic: none -> 4.44 us  [the longest x1 2.4 us: body(): jnp.stack([product, square]) * weights[None, :, None]]
  transfers between devices with their start and end apart: 3 -> 19, of which waited for: 3 -> 7; matrix products, arithmetic and copies ran while one was open for 5% -> 26% of each run, Pallas kernels for 0% -> 0%
where the time goes in v1:
time: 172 us; the launch traced here: 171 us
  matrix products  45.5 us (26%)
  blocking collectives  40.7 us (24%)
  waiting for transfers between devices  35.2 us (20%)
  starting transfers between devices  23.6 us (14%)
  local copies, waits for them, and re-layouts  13.6 us (8%)
  other arithmetic  11.2 us (7%)
    dot_general x16, matrix products, dot(): lax.dot_general(first, second, (contract, ((), ())), precision=lax.Precis...  45.5 us
    ppermute x13, waiting for transfers between devices, send(): return lax.ppermute(value, ('row', 'col'), pairs)  34.1 us
    all_gather x1, blocking collectives, body(): lax.all_gather(column_sums, 'col', axis=0).reshape(panels, 2, half)  26.5 us
    ppermute x13, starting transfers between devices, send(): return lax.ppermute(value, ('row', 'col'), pairs)  21.9 us
    all_gather x1, blocking collectives, body(): line_pattern = lax.all_gather(pattern, 'col', axis=0)  14.2 us
    unnamed x40, local copies, waits for them, and re-layouts  4.91 us
  transfers between devices with their start and end apart: 19, of which 7 were waited for; matrix products, arithmetic and copies ran while one was open for 26% of the time, Pallas kernels for 0%

profile of v1, /device:TPU:0, one launch (start us, length us, event | category | flops | bytes accessed | tf_op | source)
XLA Modules:
  0.0 170.9 jit_solution(5728910178423099838)
XLA Ops:
  3.0 2.6 %collective-permute-start.4 = (f32[640,320]{0,1:T(8,128)}, f32[640,320]{0,1:T(8,128)}, u32[]{:S(2)}, u32[]{:S(2)}) collective-permute-start(f32[640,320]{0,1:T(8,128)} %param.5), channel_id=1, source_target_pairs={{0,2},{1,3},{2,4},{3,5},{4,6},{5,7},{6,0},{7,1},{8,10},{9,11},{10,... | collective-permute-start | bytes 2457608 | tf_op jit(solution)/shard_map/ppermute | solution.py:32
  11.2 2.8 %collective-permute-start.5 = (f32[640,320]{0,1:T(8,128)}, f32[640,320]{0,1:T(8,128)}, u32[]{:S(2)}, u32[]{:S(2)}) collective-permute-start(f32[640,320]{0,1:T(8,128)} %param.5), channel_id=1, source_target_pairs={{0,6},{1,7},{2,0},{3,1},{4,2},{5,3},{6,4},{7,5},{8,14},{9,15},{10,... | collective-permute-start | bytes 2457608 | tf_op jit(solution)/shard_map/ppermute | solution.py:32
  14.1 3.2 %convolution_bitcast_fusion.3 = f32[640,320]{0,1:T(8,128)} fusion(f32[320,320]{0,1:T(8,128)} %copy-done.13, f32[640,320]{0,1:T(8,128)} %param.5), kind=kOutput, calls=%fused_computation.25 | convolution fusion | flops 393216000 | bytes 2048000 | tf_op jit(solution)/shard_map/dot_general | solution.py:10
  19.6 7.5 %collective-permute-done.4 = f32[640,320]{0,1:T(8,128)} collective-permute-done((f32[640,320]{0,1:T(8,128)}, f32[640,320]{0,1:T(8,128)}, u32[]{:S(2)}, u32[]{:S(2)}) %collective-permute-start.4) | collective-permute-done | bytes 819232 | tf_op jit(solution)/shard_map/ppermute | solution.py:32
  30.6 16.4 %collective-permute-done.3 = f32[320,640]{1,0:T(8,128)S(1)} collective-permute-done((f32[320,640]{1,0:T(8,128)}, f32[320,640]{1,0:T(8,128)S(1)}, u32[]{:S(2)}, u32[]{:S(2)}) %collective-permute-start.3) | collective-permute-done | bytes 819232 | tf_op jit(solution)/shard_map/ppermute | solution.py:32
  49.8 2.8 %fusion.21 = f32[640,640]{1,0:T(8,128)S(1)} fusion(f32[640,320]{0,1:T(8,128)} %param.5, f32[4,320,640]{2,1,0:T(8,128)S(1)} %pad_maximum_fusion, s32[]{:T(128)S(6)} %select_n.130), kind=kOutput, calls=%fused_computation.44 | convolution fusion | flops 786432000 | bytes 3276804 | tf_op jit(solution)/shard_map/dot_general | solution.py:10
  52.6 2.8 %fusion.19 = f32[640,640]{1,0:T(8,128)S(1)} fusion(f32[640,320]{0,1:T(8,128)} %collective-permute-done.4, f32[4,320,640]{2,1,0:T(8,128)S(1)} %pad_maximum_fusion, s32[]{:T(128)S(6)} %select_n.132), kind=kOutput, calls=%fused_computation.42 | convolution fusion | flops 786432000 | bytes 3276804 | tf_op jit(solution)/shard_map/dot_general | solution.py:10
  55.5 2.8 %fusion.17 = f32[640,640]{1,0:T(8,128)S(1)} fusion(f32[640,320]{0,1:T(8,128)} %collective-permute-done.5, f32[4,320,640]{2,1,0:T(8,128)S(1)} %pad_maximum_fusion, s32[]{:T(128)S(6)} %select_n.134), kind=kOutput, calls=%fused_computation.40 | convolution fusion | flops 786432000 | bytes 3276804 | tf_op jit(solution)/shard_map/dot_general | solution.py:10
  58.3 3.5 %collective-permute-done.6 = f32[640,320]{0,1:T(8,128)S(1)} collective-permute-done((f32[640,320]{0,1:T(8,128)}, f32[640,320]{0,1:T(8,128)S(1)}, u32[]{:S(2)}, u32[]{:S(2)}) %collective-permute-start.6) | collective-permute-done | bytes 819232 | tf_op jit(solution)/shard_map/ppermute | solution.py:32
  64.8 2.5 %fusion.28 = f32[320,640]{1,0:T(8,128)S(1)} fusion(f32[640,320]{0,1:T(8,128)} %collective-permute-done.5, s32[]{:T(128)S(6)} %select_n.127), kind=kOutput, calls=%fused_computation.51 | convolution fusion | flops 393216000 | bytes 2129924 | tf_op jit(solution)/shard_map/dot_general | solution.py:10
  67.3 2.5 %convolution_add_fusion.2 = f32[320,640]{1,0:T(8,128)S(1)} fusion(f32[320,640]{1,0:T(8,128)S(1)} %fusion.51, f32[640,320]{0,1:T(8,128)} %collective-permute-done.4, s32[]{:T(128)S(6)} %select_n.127), kind=kOutput, calls=%fused_computation.29 | convolution fusion | flops 393420800 | bytes 2949124 | tf_op jit(solution)/shard_map/dot_general | solution.py:10
  72.8 14.2 %all-gather.1 = s32[8,10,5]{1,2,0:T(8,128)S(1)} all-gather(s32[1,10,5]{1,2,0:T(8,128)S(1)} %bitcast.104), channel_id=2, replica_groups=mesh['row'=4,'col'=8] {'col'}, dimensions={0}, use_global_device_ids=true | all-gather | bytes 1800 | tf_op jit(solution)/shard_map/all_gather | solution.py:76
  94.3 3.6 %convolution_bitcast_fusion.2 = f32[640,320]{0,1:T(8,128)} fusion(f32[640,320]{0,1:T(8,128)} %collective-permute-done.4, s32[]{:T(128)S(6)} %select_n.126), kind=kOutput, calls=%fused_computation.24 | convolution fusion | flops 393216000 | bytes 2129924 | tf_op jit(solution)/shard_map/dot_general | solution.py:10
  100.9 4.3 %collective-permute-start.17 = (f32[2,320]{1,0:T(2,128)S(1)}, f32[2,320]{1,0:T(2,128)S(1)}, u32[]{:S(2)}, u32[]{:S(2)}) collective-permute-start(f32[2,320]{1,0:T(2,128)S(1)} %add.229), channel_id=1, source_target_pairs={{0,16},{1,17},{2,18},{3,19},{4,20},{5,21},{6,22},{7,23},{8,24},{9,... | collective-permute-start | bytes 7688 | tf_op jit(solution)/shard_map/ppermute | solution.py:32
  106.3 2.4 %copy.35 = f32[320,640]{1,0:T(8,128)} copy(f32[320,640]{0,1:T(8,128)} %maximum_select_fusion) | data formatting | bytes 1638400 | tf_op jit(solution)/shard_map/jit(_where)/select_n | solution.py:109
  112.8 3.5 %convolution_bitcast_fusion = f32[640,320]{0,1:T(8,128)} fusion(f32[640,320]{0,1:T(8,128)} %collective-permute-done.5, s32[]{:T(128)S(6)} %select_n.126), kind=kOutput, calls=%fused_computation.22 | convolution fusion | flops 393216000 | bytes 2129924 | tf_op jit(solution)/shard_map/dot_general | solution.py:10
  118.3 26.5 %all-gather.2 = f32[8,1,320]{2,1,0:T(1,128)S(1)} all-gather(f32[1,1,320]{2,1,0:T(1,128)S(1)} %get-tuple-element.211), channel_id=1, replica_groups=mesh['row'=4,'col'=8] {'col'}, dimensions={0}, use_global_device_ids=true | all-gather | bytes 11520 | tf_op jit(solution)/shard_map/all_gather | solution.py:101
  145.5 3.1 %collective-permute-done.13 = f32[320,640]{1,0:T(8,128)} collective-permute-done((f32[320,640]{1,0:T(8,128)}, f32[320,640]{1,0:T(8,128)}, u32[]{:S(2)}, u32[]{:S(2)}) %collective-permute-start.13) | collective-permute-done | bytes 819232 | tf_op jit(solution)/shard_map/ppermute | solution.py:32
  148.6 12.9 %conditional.1 = (f32[640,640]{0,1:T(8,128)}) conditional(s32[]{:T(128)} %convert_element_type.29, (s32[]{:T(128)}, s32[]{:T(128)}, s32[8,10,5]{1,2,0:T(8,128)S(1)}, f32[640,320]{0,1:T(8,128)}, f32[640,320]{0,1:T(8,128)}, /*index=5*/f32[640,320]{0,1:T(8,128)}, f32[640,320]{0,1:T(8,128)}, f32[640,320]{0,1:T(8,128)}, f32[4,320,640]{2,1,0:T(8,128)S(1)}, ...), branch_computations={%region_0.1_spmd, %region_1.2_spmd} | conditional | flops 2361139200 | bytes 22937664 | solution.py:132
  148.6 3.1 %fusion.49 = f32[640,640]{1,0:T(8,128)S(1)} fusion(f32[320,640]{1,0:T(8,128)} %get-tuple-element.144, f32[320,640]{1,0:T(8,128)} %get-tuple-element.145), kind=kOutput, calls=%fused_computation.86 | convolution fusion | flops 786432000 | bytes 3276800 | tf_op jit(solution)/shard_map/cond/branch_1_fun/dot_general | solution.py:10
  151.8 2.9 %fusion.50 = f32[640,640]{1,0:T(8,128)S(1)} fusion(f32[320,640]{1,0:T(8,128)} %get-tuple-element.146, f32[320,640]{1,0:T(8,128)S(1)} %copy-done.5), kind=kOutput, calls=%fused_computation.87 | convolution fusion | flops 786432000 | bytes 3276800 | tf_op jit(solution)/shard_map/cond/branch_1_fun/dot_general | solution.py:10
  154.7 4.1 %add_add_fusion = f32[640,640]{1,0:T(8,128)} fusion(f32[640,640]{1,0:T(8,128)S(1)} %fusion.49, f32[640,640]{1,0:T(8,128)S(1)} %fusion.50, f32[320,640]{1,0:T(8,128)} %get-tuple-element.148, f32[320,640]{1,0:T(8,128)S(1)} %copy-done.2), kind=kOutput, calls=%fused_computation.15 | convolution fusion | flops 787251200 | bytes 6553600 | tf_op jit(solution)/shard_map/cond/branch_1_fun/dot_general | solution.py:10
  158.8 2.7 %copy.46 = f32[640,640]{0,1:T(8,128)} copy(f32[640,640]{1,0:T(8,128)} %add_add_fusion) | data formatting | bytes 3276800 | tf_op jit(solution)/shard_map/cond | solution.py:132
  161.6 3.5 %convolution_add_fusion = f32[640,640]{0,1:T(8,128)S(1)} fusion(f32[640,640]{0,1:T(8,128)} %get-tuple-element.203, f32[640,320]{0,1:T(8,128)} %get-tuple-element.205, f32[4,320,640]{2,1,0:T(8,128)S(1)} %pad_maximum_fusion, s32[]{:T(128)S(6)} %select_n.137), kind=kOutput, calls=%fused_computation.21 | convolution fusion | flops 786841600 | bytes 4915204 | tf_op jit(solution)/shard_map/dot_general | solution.py:10
  (108 shorter events, 46.3 us)
Async XLA Ops:
  2.5 3.4 %collective-permute-start = (f32[320,320]{1,0:T(8,128)S(1)}, f32[320,320]{1,0:T(8,128)S(1)}, u32[]{:S(2)}, u32[]{:S(2)}) collective-permute-start(f32[320,320]{1,0:T(8,128)S(1)} %copy.50), channel_id=1, source_target_pairs={{0,1},{1,0},{2,3},{3,2},{4,5},{5,4},{6,7},{7,6},{8,9},{9,8},{10,11... | collective-permute-start | bytes 1228808 | tf_op jit(solution)/shard_map/ppermute | solution.py:35
  3.0 24.1 %collective-permute-start.4 = (f32[640,320]{0,1:T(8,128)}, f32[640,320]{0,1:T(8,128)}, u32[]{:S(2)}, u32[]{:S(2)}) collective-permute-start(f32[640,320]{0,1:T(8,128)} %param.5), channel_id=1, source_target_pairs={{0,2},{1,3},{2,4},{3,5},{4,6},{5,7},{6,0},{7,1},{8,10},{9,11},{10,... | collective-permute-start | bytes 2457608 | tf_op jit(solution)/shard_map/ppermute | solution.py:32
  7.7 20.5 %collective-permute-start.2 = (f32[320,640]{1,0:T(8,128)}, f32[320,640]{1,0:T(8,128)S(1)}, u32[]{:S(2)}, u32[]{:S(2)}) collective-permute-start(f32[320,640]{1,0:T(8,128)} %pad_maximum_fusion.1), channel_id=1, source_target_pairs={{0,16},{1,17},{2,18},{3,19},{4,20},{5,21},{6,22},{7,23},{8,24},{9,... | collective-permute-start | bytes 2457608 | tf_op jit(solution)/shard_map/ppermute | solution.py:32
  9.3 21.3 %collective-permute-start.1 = (f32[320,640]{1,0:T(8,128)}, f32[320,640]{1,0:T(8,128)S(1)}, u32[]{:S(2)}, u32[]{:S(2)}) collective-permute-start(f32[320,640]{1,0:T(8,128)} %pad_maximum_fusion.1), channel_id=1, source_target_pairs={{0,8},{1,9},{2,10},{3,11},{4,12},{5,13},{6,14},{7,15},{8,0},{9,1},... | collective-permute-start | bytes 2457608 | tf_op jit(solution)/shard_map/ppermute | solution.py:32
  10.8 36.2 %collective-permute-start.3 = (f32[320,640]{1,0:T(8,128)}, f32[320,640]{1,0:T(8,128)S(1)}, u32[]{:S(2)}, u32[]{:S(2)}) collective-permute-start(f32[320,640]{1,0:T(8,128)} %pad_maximum_fusion.1), channel_id=1, source_target_pairs={{0,24},{1,25},{2,26},{3,27},{4,28},{5,29},{6,30},{7,31},{8,16},{9,... | collective-permute-start | bytes 2457608 | tf_op jit(solution)/shard_map/ppermute | solution.py:32
  11.2 44.3 %collective-permute-start.5 = (f32[640,320]{0,1:T(8,128)}, f32[640,320]{0,1:T(8,128)}, u32[]{:S(2)}, u32[]{:S(2)}) collective-permute-start(f32[640,320]{0,1:T(8,128)} %param.5), channel_id=1, source_target_pairs={{0,6},{1,7},{2,0},{3,1},{4,2},{5,3},{6,4},{7,5},{8,14},{9,15},{10,... | collective-permute-start | bytes 2457608 | tf_op jit(solution)/shard_map/ppermute | solution.py:32
  19.6 33.1 %copy-start.8 = (f32[1,320,640]{2,1,0:T(8,128)}, f32[1,320,640]{2,1,0:T(8,128)S(1)}, u32[]{:S(2)}) copy-start(f32[1,320,640]{2,1,0:T(8,128)S(1)} %fusion.76) | copy-start | bytes 2457604
  27.1 34.8 %collective-permute-start.6 = (f32[640,320]{0,1:T(8,128)}, f32[640,320]{0,1:T(8,128)S(1)}, u32[]{:S(2)}, u32[]{:S(2)}) collective-permute-start(f32[640,320]{0,1:T(8,128)} %collective-permute-done.4), channel_id=1, source_target_pairs={{0,2},{1,3},{2,4},{3,5},{4,6},{5,7},{6,0},{7,1},{8,10},{9,11},{10,... | collective-permute-start | bytes 2457608 | tf_op jit(solution)/shard_map/ppermute | solution.py:32
  28.3 18.7 %copy-start.3 = (f32[320,640]{1,0:T(8,128)}, f32[320,640]{1,0:T(8,128)S(1)}, u32[]{:S(2)}) copy-start(f32[320,640]{1,0:T(8,128)S(1)} %collective-permute-done.2) | copy-start | bytes 2457604
  30.6 16.4 %copy-start.6 = (f32[320,640]{1,0:T(8,128)}, f32[320,640]{1,0:T(8,128)S(1)}, u32[]{:S(2)}) copy-start(f32[320,640]{1,0:T(8,128)S(1)} %collective-permute-done.1) | copy-start | bytes 2457604
  61.8 7.9 %copy-start.10 = (f32[640,320]{0,1:T(8,128)}, f32[640,320]{0,1:T(8,128)S(1)}, u32[]{:S(2)}) copy-start(f32[640,320]{0,1:T(8,128)S(1)} %collective-permute-done.6) | copy-start | bytes 2457604
  64.8 22.2 %collective-permute-start.7 = (f32[640,320]{0,1:T(8,128)}, f32[640,320]{0,1:T(8,128)}, u32[]{:S(2)}, u32[]{:S(2)}) collective-permute-start(f32[640,320]{0,1:T(8,128)} %slice.38), channel_id=1, source_target_pairs={{0,1},{1,0},{2,3},{3,2},{4,5},{5,4},{6,7},{7,6},{8,9},{9,8},{10,11... | collective-permute-start | bytes 2457608 | tf_op jit(solution)/shard_map/ppermute | solution.py:35
  71.9 38.2 %collective-permute-start.8 = (f32[640,320]{0,1:T(8,128)}, f32[640,320]{0,1:T(8,128)}, u32[]{:S(2)}, u32[]{:S(2)}) collective-permute-start(f32[640,320]{0,1:T(8,128)} %fusion.12), channel_id=1, source_target_pairs={{0,1},{1,0},{2,3},{3,2},{4,5},{5,4},{6,7},{7,6},{8,9},{9,8},{10,11... | collective-permute-start | bytes 2457608 | tf_op jit(solution)/shard_map/ppermute | solution.py:35
  91.0 14.3 %collective-permute-start.11 = (f32[320,320]{0,1:T(8,128)S(1)}, f32[320,320]{0,1:T(8,128)S(1)}, u32[]{:S(2)}, u32[]{:S(2)}) collective-permute-start(f32[320,320]{0,1:T(8,128)S(1)} %get-tuple-element.207), channel_id=1, source_target_pairs={{0,1},{1,0},{2,3},{3,2},{4,5},{5,4},{6,7},{7,6},{8,9},{9,8},{10,11... | collective-permute-start | bytes 1228808 | tf_op jit(solution)/shard_map/ppermute | solution.py:35
  92.7 8.2 %collective-permute-start.16 = (f32[2,320]{1,0:T(2,128)S(1)}, f32[2,320]{1,0:T(2,128)S(1)}, u32[]{:S(2)}, u32[]{:S(2)}) collective-permute-start(f32[2,320]{1,0:T(2,128)S(1)} %fusion.10), channel_id=1, source_target_pairs={{0,8},{1,9},{2,10},{3,11},{4,12},{5,13},{6,14},{7,15},{8,0},{9,1},... | collective-permute-start | bytes 7688 | tf_op jit(solution)/shard_map/ppermute | solution.py:32
  97.8 47.6 %collective-permute-start.10 = (f32[640,320]{0,1:T(8,128)}, f32[640,320]{0,1:T(8,128)}, u32[]{:S(2)}, u32[]{:S(2)}) collective-permute-start(f32[640,320]{0,1:T(8,128)} %get-tuple-element.205), channel_id=1, source_target_pairs={{2,6},{3,7},{4,2},{5,3},{6,4},{7,5},{8,14},{9,15},{12,8},{13,9},{1... | collective-permute-start | bytes 2457608 | tf_op jit(solution)/shard_map/ppermute | solution.py:32
  99.4 46.1 %collective-permute-start.9 = (f32[640,320]{0,1:T(8,128)}, f32[640,320]{0,1:T(8,128)}, u32[]{:S(2)}, u32[]{:S(2)}) collective-permute-start(f32[640,320]{0,1:T(8,128)} %get-tuple-element.205), channel_id=1, source_target_pairs={{2,4},{3,5},{4,6},{5,7},{6,2},{7,3},{8,12},{9,13},{12,14},{13,15},... | collective-permute-start | bytes 2457608 | tf_op jit(solution)/shard_map/ppermute | solution.py:32
  100.9 10.5 %collective-permute-start.17 = (f32[2,320]{1,0:T(2,128)S(1)}, f32[2,320]{1,0:T(2,128)S(1)}, u32[]{:S(2)}, u32[]{:S(2)}) collective-permute-start(f32[2,320]{1,0:T(2,128)S(1)} %add.229), channel_id=1, source_target_pairs={{0,16},{1,17},{2,18},{3,19},{4,20},{5,21},{6,22},{7,23},{8,24},{9,... | collective-permute-start | bytes 7688 | tf_op jit(solution)/shard_map/ppermute | solution.py:32
  108.7 7.5 %copy-start.11 = (f32[640,320]{0,1:T(8,128)S(1)}, f32[640,320]{0,1:T(8,128)}, u32[]{:S(2)}) copy-start(f32[640,320]{0,1:T(8,128)} %copy-done.10) | copy-start | bytes 2457604
  108.7 36.7 %collective-permute-start.14 = (f32[320,640]{1,0:T(8,128)}, f32[320,640]{1,0:T(8,128)}, u32[]{:S(2)}, u32[]{:S(2)}) collective-permute-start(f32[320,640]{1,0:T(8,128)} %copy.35), channel_id=1, source_target_pairs={{6,30},{7,31},{12,20},{13,21},{18,10},{19,11},{24,0},{25,1}} | collective-permute-start | bytes 2457608 | tf_op jit(solution)/shard_map/ppermute | solution.py:32
  110.2 38.5 %collective-permute-start.13 = (f32[320,640]{1,0:T(8,128)}, f32[320,640]{1,0:T(8,128)}, u32[]{:S(2)}, u32[]{:S(2)}) collective-permute-start(f32[320,640]{1,0:T(8,128)} %copy.35), channel_id=1, source_target_pairs={{4,20},{5,21},{14,30},{15,31},{16,0},{17,1},{26,10},{27,11}} | collective-permute-start | bytes 2457608 | tf_op jit(solution)/shard_map/ppermute | solution.py:32
  111.5 37.2 %collective-permute-start.12 = (f32[320,640]{1,0:T(8,128)}, f32[320,640]{1,0:T(8,128)}, u32[]{:S(2)}, u32[]{:S(2)}) collective-permute-start(f32[320,640]{1,0:T(8,128)} %copy.35), channel_id=1, source_target_pairs={{2,10},{3,11},{8,0},{9,1},{22,30},{23,31},{28,20},{29,21}} | collective-permute-start | bytes 2457608 | tf_op jit(solution)/shard_map/ppermute | solution.py:32
  165.2 3.5 %collective-permute-start.15 = (f32[640,320]{0,1:T(8,128)S(1)}, f32[640,320]{0,1:T(8,128)S(1)}, u32[]{:S(2)}, u32[]{:S(2)}) collective-permute-start(f32[640,320]{0,1:T(8,128)S(1)} %slice.40), channel_id=1, source_target_pairs={{0,1},{1,0},{2,3},{3,2},{4,5},{5,4},{6,7},{7,6},{8,9},{9,8},{10,11... | collective-permute-start | bytes 2457608 | tf_op jit(solution)/shard_map/ppermute | solution.py:35
  166.9 1.2 collective-permute-start.18
  (15 other events, 41.5 us)

commit v2 on v1

v2 whole, which is shorter than its diff:
```python
import functools

import jax
import jax.numpy as jnp
from jax import lax
from jax.experimental import pallas as pl
from jax.experimental.pallas import tpu as pltpu
from jax.sharding import PartitionSpec as P

BLK = 64
ROW_BY_COLUMN = ((1,), (0,))
ROW_BY_ROW = ((1,), (1,))


def expand_mask(pattern):
    return jnp.repeat(jnp.repeat(pattern.astype(jnp.float32), BLK, axis=0), BLK, axis=1)


def split(value):
    high = value.astype(jnp.bfloat16)
    return high, (value - high.astype(jnp.float32)).astype(jnp.bfloat16)


def dot(first, second, contract=ROW_BY_COLUMN):
    def one(a, b):
        return lax.dot_general(a, b, (contract, ((), ())), preferred_element_type=jnp.float32)

    return one(first[0], second[0]) + (one(first[0], second[1]) + one(first[1], second[0]))


def call(kernel, outs, scalars, *arrays, flops=0):
    moved = sum(a.size * a.dtype.itemsize for a in arrays)
    return pl.pallas_call(
        kernel,
        out_shape=outs,
        in_specs=[pl.BlockSpec(memory_space=pltpu.SMEM)] + [pl.BlockSpec(memory_space=pltpu.VMEM)] * len(arrays),
        out_specs=jax.tree.map(lambda _: pl.BlockSpec(memory_space=pltpu.VMEM), outs),
        compiler_params=pltpu.CompilerParams(vmem_limit_bytes=32 * 1024 * 1024),
        cost_estimate=pl.CostEstimate(flops=flops, bytes_accessed=moved, transcendentals=0),
    )(jnp.stack([jnp.asarray(s, jnp.int32) for s in scalars]), *arrays)


def shape(*dims, dtype=jnp.float32):
    return jax.ShapeDtypeStruct(dims, dtype)


def split_kernel(ids, mine, theirs, *refs):
    tiles, (kept_high, kept_low, given_high, given_low) = refs[:-4], refs[-4:]
    half = mine.shape[1]

    def store(place, kept, given):
        kept_high[place], kept_low[place] = split(kept)
        given_high[place], given_low[place] = split(given)

    store(ids[0], mine[...], theirs[...])
    for m, tile in enumerate(tiles):
        store(ids[m + 1], tile[:, :half], tile[:, half:])


def add_products(ids, first_id, lefts, sides, starts, outs):
    height, half = outs[0].shape

    def step(i, carry):
        rows = pl.ds(pl.multiple_of(i * half, half), half)
        totals = [start[rows, :] if start is not None else None for start in starts]
        for j, left in enumerate(lefts):
            parts = split(left[rows, :])
            for s, (high, low) in enumerate(sides):
                k = ids[first_id + j]
                term = dot(parts, (high[k], low[k]))
                totals[s] = term if totals[s] is None else totals[s] + term
        for out, total in zip(outs, totals):
            out[rows, :] = total
        return carry

    lax.fori_loop(0, height // half, step, 0)


def products_kernel(count, sides, started, ids, *refs):
    parts, refs = refs[: 2 * sides], refs[2 * sides :]
    lefts, refs = refs[:count], refs[count:]
    starts, outs = (refs[:sides], refs[sides:]) if started else ([None] * sides, refs)
    add_products(ids, 0, lefts, [parts[2 * s : 2 * s + 2] for s in range(sides)], starts, outs)


def products(ids, lefts, sides, starts=None):
    height, half = lefts[0].shape
    kernel = functools.partial(products_kernel, len(lefts), len(sides), starts is not None)
    flops = 6 * height * half * half * len(lefts) * len(sides)
    args = [part for side in sides for part in side] + list(lefts) + list(starts or [])
    return call(kernel, [shape(height, half)] * len(sides), ids, *args, flops=flops)


def last_kernel(others, downs, ids, high, low, *refs):
    on_line, on_plane = refs[:others], refs[others : others + downs]
    start, out = refs[others + downs :]

    @pl.when(ids[0] == 0)
    def _():
        add_products(ids, 1, on_line, [(high, low)], [start], [out])

    @pl.when(ids[0] == 1)
    def _():
        add_products(ids, 1 + others, on_plane, [(high, low)], [start], [out])


def square_kernel(ids, kept, received, mask, weights, square, given, sums):
    half = kept.shape[1]
    product = kept[...] + received[...]
    square[...] = product * mask[...]
    column = weights[...]
    sums[...] = jnp.zeros_like(sums)
    sums[0:1, :] = jnp.sum(product * column, axis=0, keepdims=True)
    sums[1:2, :] = jnp.sum(square[...] * column, axis=0, keepdims=True)
    given[...] = square[pl.ds(pl.multiple_of((1 - ids[0]) * half, half), half), :]


def turn_kernel(ids, square, theirs, out):
    half = square.shape[1]
    own = pl.ds(pl.multiple_of(ids[0] * half, half), half)
    other = pl.ds(pl.multiple_of((1 - ids[0]) * half, half), half)
    out[own, :] = square[own, :].T
    out[other, :] = theirs[...].T


def diagonal_kernel(ids, *refs):
    lefts, (given, kept) = refs[:-2], refs[-2:]
    height, half = given.shape
    for out, which in ((given, 1 - ids[0]), (kept, ids[0])):
        wanted = pl.ds(pl.multiple_of(which * half, half), half)

        def step(i, carry):
            rows = pl.ds(pl.multiple_of(i * half, half), half)
            out[rows, :] = sum(dot(split(left[rows, :]), split(left[wanted, :]), ROW_BY_ROW) for left in lefts)
            return carry

        lax.fori_loop(0, height // half, step, 0)


def early_kernel(ids, *refs):
    parts, (square, kept, received, mask), outs, diagonal = refs[:4], refs[4:8], refs[8:10], refs[10]
    diagonal[...] = (kept[...] + received[...]) * mask[...]
    add_products(ids, 0, [square, diagonal], [parts[:2], parts[2:]], [None, None], outs)


def check_kernel(ids, *refs):
    parts, rows, (kept, given) = refs[:4], refs[4:-2], refs[-2:]
    for out, (high, low) in ((kept, parts[:2]), (given, parts[2:])):
        out[...] = sum(dot(split(row[...]), (high[ids[j]], low[ids[j]])) for j, row in enumerate(rows))


def make_body(panels, columns):
    assert columns == 2 * panels and panels & (panels - 1) == 0

    def flat(r, z, core):
        return r * columns + 2 * z + core

    def send(value, target):
        pairs = []
        for r in range(panels):
            for z in range(panels):
                to = target(r, z)
                if to is not None:
                    pairs += [(flat(r, z, core), flat(*to, core)) for core in (0, 1)]
        return lax.ppermute(value, ("row", "col"), pairs)

    def swap_core(value):
        return lax.ppermute(value, "col", [(c, c ^ 1) for c in range(columns)])

    def ring(step):
        return lambda r, z: (r, (z + step) % panels)

    def others_ring(step):
        def target(r, z):
            if z == r:
                return None
            line = [q for q in range(panels) if q != r]
            return (r, line[(line.index(z) + step) % len(line)])

        return target

    def across(m):
        return lambda r, z: (r ^ m, z)

    def to_diagonal(m):
        return lambda r, z: (r ^ m, z) if r ^ m == z else None

    def from_diagonal(m):
        return lambda r, z: (r, r ^ m) if r == z else None

    def row_sum(value):
        m = 1
        while m < panels:
            value = value + send(value, across(m))
            m *= 2
        return value

    def gather_ring(value, ring_of, count):
        got = {0: value}
        got[1] = send(value, ring_of(1))
        for j in range(count - 1, count // 2, -1):
            got[j] = send(got[(j + 1) % count], ring_of(-1))
        for j in range(2, count // 2 + 1):
            got[j] = send(got[j - 1], ring_of(1))
        return got

    def body(density, pattern, weights):
        r = lax.axis_index("row")
        c = lax.axis_index("col")
        z, core = c // 2, c % 2
        height, half = density.shape
        block_mask = expand_mask(pattern)

        left = gather_ring(density, ring, panels)
        mine = lax.dynamic_slice_in_dim(density, core * half, half, 0)
        theirs = swap_core(lax.dynamic_slice_in_dim(density, (1 - core) * half, half, 0))
        own = jnp.concatenate([mine, theirs], axis=1)
        own_later, pattern_later, _ = lax.optimization_barrier((own, pattern, left[1]))
        tiles = [send(own if m & (m - 1) == 0 else own_later, across(m)) for m in range(1, panels)]
        diagonal_pattern = sum(send(pattern_later, from_diagonal(m)) for m in range(1, panels))
        diagonal_mask = expand_mask(diagonal_pattern)

        part = shape(panels, half, half, dtype=jnp.bfloat16)
        right = call(split_kernel, [part] * 4, [r ^ m for m in range(panels)], mine, theirs, *tiles)
        kept, given = right[:2], right[2:]

        last = panels // 2
        early = [j for j in range(panels) if j != last]
        starts = products([(z - j) % panels for j in early], [left[j] for j in early], [kept, given])
        at = [(z - last) % panels]
        given_sum = products(at, [left[last]], [given], starts[1:])[0]
        kept_sum = products(at, [left[last]], [kept], starts[:1])[0]
        received = swap_core(given_sum)
        square, quarter, sums = call(
            square_kernel,
            [shape(height, half), shape(half, half), shape(8, half)],
            [core],
            kept_sum,
            received,
            block_mask,
            weights[:, None],
        )

        others = gather_ring(square, others_ring, panels - 1)
        rows = call(turn_kernel, shape(height, half), [core], square, swap_core(quarter))
        down = [send(rows, to_diagonal(m)) for m in range(1, panels)]

        sums = row_sum(sums)
        all_sums = gather_ring(sums, ring, panels)
        check = call(
            check_kernel,
            [shape(8, half)] * 2,
            [(z - j) % panels for j in range(panels)],
            *right,
            *[all_sums[j] for j in range(panels)],
        )
        second_check = check[0] + swap_core(check[1])

        diagonal_given, diagonal_kept = call(
            diagonal_kernel,
            [shape(height, half)] * 2,
            [core],
            *[left[j] for j in range(panels)],
            flops=12 * height * half * half * panels,
        )
        cube = call(
            lambda *refs: early_kernel(*refs),
            [shape(height, half)] * 2 + [shape(height, half)],
            [z, r],
            *right,
            square,
            diagonal_kept,
            swap_core(diagonal_given),
            diagonal_mask,
            flops=24 * height * half * half,
        )

        place = z - (z > r).astype(z.dtype)
        ids = [(z == r).astype(jnp.int32)]
        for j in range(1, panels - 1):
            q = (place - j) % (panels - 1)
            ids.append(q + (q >= r).astype(q.dtype))
        ids += [r ^ m for m in range(1, panels)]
        on_line = [others[j] for j in range(1, panels - 1)]

        def finish(side, start):
            kernel = functools.partial(last_kernel, len(on_line), len(down))
            flops = 6 * height * half * half * len(on_line)
            return call(kernel, shape(height, half), ids, *side, *on_line, *down, start, flops=flops)

        given_cube = finish(given, cube[1])
        kept_cube = finish(kept, cube[0])
        cube_term = block_mask * (kept_cube + swap_core(given_cube))
        checks = jnp.concatenate([sums[:1], second_check[1:2]], axis=0)
        return 3.0 * square - 2.0 * cube_term, checks

    return body


def solution(mesh):
    in_specs = (P("row", "col"), P("row", "col"), P("row"))
    out_specs = (P("row", "col"), P(None, "col"))
    body = make_body(mesh.shape["row"], mesh.shape["col"])
    return jax.shard_map(body, mesh=mesh, in_specs=in_specs, out_specs=out_specs, check_vma=False)
```

time: 172 us -> 229 us (1.33)
  local copies, waits for them, and re-layouts: 13.6 us -> 102 us
  matrix products: 45.5 us -> 0 us
  blocking collectives: 40.7 us -> 0 us
  Pallas kernels: 0 us -> 33.1 us
  waiting for transfers between devices: 35.2 us -> 54.7 us
  starting transfers between devices: 23.6 us -> 32.1 us
  other arithmetic: 11.2 us -> 4.32 us
    unnamed x40 -> x122, local copies, waits for them, and re-layouts: 4.91 us -> 57 us
    dot_general x16 -> x0, matrix products: 45.5 us -> none  [dot(): lax.dot_general(first, second, (contract, ((), ())), precision=lax.Precis...]
    all_gather x2 -> x0, blocking collectives: 40.7 us -> none  [the longest x1 26.5 us: body(): lax.all_gather(column_sums, 'col', axis=0).reshape(panels, 2, half)]
    pallas_call x0 -> x11, Pallas kernels: none -> 33.1 us  [call(): pl.pallas_call(kernel, out_shape=outs, in_specs=[pl.BlockSpec(memory_spac...]
    ppermute x0 -> x11, local copies, waits for them, and re-layouts: none -> 26.1 us  [the longest x8 19.6 us: send(): return lax.ppermute(value, ('row', 'col'), pairs)]
    ppermute x13 -> x19, waiting for transfers between devices: 34.1 us -> 53.6 us  [send(): return lax.ppermute(value, ('row', 'col'), pairs)]
    pallas_call x0 -> x5, local copies, waits for them, and re-layouts: none -> 11 us  [call(): pl.pallas_call(kernel, out_shape=outs, in_specs=[pl.BlockSpec(memory_spac...]
    ppermute x13 -> x19, starting transfers between devices: 21.9 us -> 31.5 us  [send(): return lax.ppermute(value, ('row', 'col'), pairs)]
  transfers between devices with their start and end apart: 19 -> 25, of which waited for: 7 -> 9; matrix products, arithmetic and copies ran while one was open for 26% -> 16% of each run, Pallas kernels for 0% -> 12%
where the time goes in v2:
time: 229 us; the launch traced here: 227 us
  local copies, waits for them, and re-layouts  102 us (45%)
  waiting for transfers between devices  54.7 us (24%)
  Pallas kernels  33.1 us (14%)
  starting transfers between devices  32.1 us (14%)
  other arithmetic  4.32 us (2%)
    unnamed x122, local copies, waits for them, and re-layouts  57 us
    ppermute x19, waiting for transfers between devices, send(): return lax.ppermute(value, ('row', 'col'), pairs)  53.6 us
    pallas_call x11, Pallas kernels, call(): pl.pallas_call(kernel, out_shape=outs, in_specs=[pl.BlockSpec(memory_spac...  33.1 us
    ppermute x19, starting transfers between devices, send(): return lax.ppermute(value, ('row', 'col'), pairs)  31.5 us
    ppermute x8, local copies, waits for them, and re-layouts, send(): return lax.ppermute(value, ('row', 'col'), pairs)  19.6 us
    pallas_call x5, local copies, waits for them, and re-layouts, call(): pl.pallas_call(kernel, out_shape=outs, in_specs=[pl.BlockSpec(memory_spac...  11 us
    ppermute x3, local copies, waits for them, and re-layouts, swap_core(): return lax.ppermute(value, 'col', [(c, c ^ 1) for c in range(columns)])  6.48 us
    reshape x2, local copies, waits for them, and re-layouts, expand_mask(): jnp.repeat(jnp.repeat(pattern.astype(jnp.float32), BLK, axis=0), BLK, axi...  4.93 us
  transfers between devices with their start and end apart: 25, of which 9 were waited for; matrix products, arithmetic and copies ran while one was open for 16% of the time, Pallas kernels for 12%

profile of v2, /device:TPU:0, one launch (start us, length us, event | category | flops | bytes accessed | tf_op | source)
XLA Modules:
  0.0 226.9 jit_solution(7107349835785796921)
XLA Ops:
  0.6 3.1 %collective-permute-start.3 = (f32[640,320]{0,1:T(8,128)}, f32[640,320]{0,1:T(8,128)}, u32[]{:S(2)}, u32[]{:S(2)}) collective-permute-start(f32[640,320]{0,1:T(8,128)} %param.3), channel_id=1, source_target_pairs={{0,2},{1,3},{2,4},{3,5},{4,6},{5,7},{6,0},{7,1},{8,10},{9,11},{10,... | collective-permute-start | bytes 2457608 | tf_op jit(solution)/shard_map/ppermute | solution.py:165
  12.6 12.6 %collective-permute-done.3 = f32[640,320]{0,1:T(8,128)} collective-permute-done((f32[640,320]{0,1:T(8,128)}, f32[640,320]{0,1:T(8,128)}, u32[]{:S(2)}, u32[]{:S(2)}) %collective-permute-start.3) | collective-permute-done | bytes 819232 | tf_op jit(solution)/shard_map/ppermute | solution.py:165
  25.2 2.7 %collective-permute-start.4 = (f32[320,640]{1,0:T(8,128)}, f32[320,640]{1,0:T(8,128)S(1)}, u32[]{:S(2)}, u32[]{:S(2)}) collective-permute-start(f32[320,640]{1,0:T(8,128)} %pad_maximum_fusion), channel_id=1, source_target_pairs={{0,24},{1,25},{2,26},{3,27},{4,28},{5,29},{6,30},{7,31},{8,16},{9,... | collective-permute-start | bytes 2457608 | tf_op jit(solution)/shard_map/ppermute | solution.py:165
  30.4 12.2 %collective-permute-done.6 = f32[640,320]{0,1:T(8,128)} collective-permute-done((f32[640,320]{0,1:T(8,128)}, f32[640,320]{0,1:T(8,128)}, u32[]{:S(2)}, u32[]{:S(2)}) %collective-permute-start.6) | collective-permute-done | bytes 819232 | tf_op jit(solution)/shard_map/ppermute | solution.py:165
  42.6 2.5 %copy.29.refs_6_.refs_3_ = f32[640,320]{1,0:T(8,128)} copy(f32[640,320]{0,1:T(8,128)} %collective-permute-done.6) | data formatting | bytes 1638400 | tf_op jit(solution)/shard_map/ppermute | solution.py:165
  46.0 2.9 %collective-permute-done.2.refs_1_ = f32[320,640]{1,0:T(8,128)S(1)} collective-permute-done((f32[320,640]{1,0:T(8,128)}, f32[320,640]{1,0:T(8,128)S(1)}, u32[]{:S(2)}, u32[]{:S(2)}) %collective-permute-start.2) | collective-permute-done | bytes 819232 | tf_op jit(solution)/shard_map/ppermute | solution.py:165
  58.9 6.3 %shard_map.51 = (f32[640,320]{1,0:T(8,128)S(1)}, f32[640,320]{1,0:T(8,128)S(1)}) custom-call(s32[3]{0:T(128)S(1)} %pad_add_fusion.1.ids, bf16[4,320,320]{2,1,0:T(8,128)(2,1)S(1)} %get-tuple-element.20.refs_0_.refs_1_.high, bf16[4,320,320]{2,1,0:T(8,128)(2,1)S(1)} %get-tuple-element.21.refs_1_.refs_2_.low, ...), custom_call_target="tpu_custom_call" | custom-call | flops 2359296000 | bytes 5734400 | tf_op jit(solution)/shard_map/pallas_call | solution.py:33
  75.5 2.5 %copy.32 = f32[640,320]{0,1:T(8,128)} copy(f32[640,320]{1,0:T(8,128)} %copy-done.23) | data formatting | bytes 1638400 | tf_op jit(solution)/shard_map/pallas_call | solution.py:33
  81.6 7.9 %shard_map.56 = (f32[640,320]{1,0:T(8,128)S(1)}, f32[640,320]{1,0:T(8,128)S(1)}) custom-call(s32[1]{0:T(128)} %bitcast.ids, f32[640,320]{1,0:T(8,128)S(1)} %copy-done.27, f32[640,320]{1,0:T(8,128)S(1)} %copy-done.42, f32[640,320]{1,0:T(8,128)S(1)} %copy-done.10, f32[640,320]{1,0:T(8,128)S(1)} %copy-done.44), custom_call_target="tpu_custom_call" | custom-call | flops 3145728000 | bytes 3276800 | tf_op jit(solution)/shard_map/pallas_call | solution.py:33
  91.5 2.5 %copy.45 = f32[640,320]{0,1:T(8,128)} copy(f32[640,320]{1,0:T(8,128)} %copy-done.45) | data formatting | bytes 1638400 | tf_op jit(solution)/shard_map/pallas_call | solution.py:33
  95.6 2.5 %copy.34.mask = f32[640,320]{1,0:T(8,128)} copy(f32[640,320]{0,1:T(8,128)} %bitcast.19) | data formatting | bytes 1638400 | tf_op jit(solution)/shard_map/reshape | solution.py:16
  108.8 3.5 %collective-permute-start.15 = (s32[10,5]{0,1:T(8,128)S(1)}, s32[10,5]{0,1:T(8,128)S(1)}, u32[]{:S(2)}, u32[]{:S(2)}) collective-permute-start(s32[10,5]{0,1:T(8,128)S(1)} %copy-done.58), channel_id=1, source_target_pairs={{0,2},{1,3},{10,8},{11,9},{20,22},{21,23},{30,28},{31,29}} | collective-permute-start | bytes 608 | tf_op jit(solution)/shard_map/ppermute | solution.py:165
  112.3 4.2 %collective-permute-start.16 = (s32[10,5]{0,1:T(8,128)S(1)}, s32[10,5]{0,1:T(8,128)S(1)}, u32[]{:S(2)}, u32[]{:S(2)}) collective-permute-start(s32[10,5]{0,1:T(8,128)S(1)} %copy-done.58), channel_id=1, source_target_pairs={{0,4},{1,5},{10,14},{11,15},{20,16},{21,17},{30,26},{31,27}} | collective-permute-start | bytes 608 | tf_op jit(solution)/shard_map/ppermute | solution.py:165
  131.9 2.5 %copy.47.refs_8_ = f32[640,320]{1,0:T(8,128)} copy(f32[640,320]{0,1:T(8,128)} %bitcast.20) | data formatting | bytes 1638400 | tf_op jit(solution)/shard_map/reshape | solution.py:16
  142.8 4.6 %shard_map.57 = (f32[640,320]{1,0:T(8,128)S(1)}, f32[640,320]{1,0:T(8,128)S(1)}, f32[640,320]{1,0:T(8,128)}) custom-call(s32[2]{0:T(128)S(1)} %pad_add_fusion.2.refs_0_, bf16[4,320,320]{2,1,0:T(8,128)(2,1)S(1)} %get-tuple-element.20.refs_0_.refs_1_.high, bf16[4,320,320]{2,1,0:T(8,128)(2,1)S(1)} %get-tuple-element.21.refs_1_.refs_2_.low, ...), custom_call_target="tpu_custom_call" | custom-call | flops 1572864000 | bytes 6553600 | tf_op jit(solution)/shard_map/pallas_call | solution.py:33
  149.3 2.5 %copy.48.refs_0_ = f32[640,320]{1,0:T(8,128)} copy(f32[640,320]{0,1:T(8,128)} %collective-permute-done.8) | data formatting | bytes 1638400 | tf_op jit(solution)/shard_map/ppermute | solution.py:165
  156.7 11.4 %collective-permute-done.12 = f32[640,320]{0,1:T(8,128)} collective-permute-done((f32[640,320]{0,1:T(8,128)}, f32[640,320]{0,1:T(8,128)}, u32[]{:S(2)}, u32[]{:S(2)}) %collective-permute-start.12) | collective-permute-done | bytes 819232 | tf_op jit(solution)/shard_map/ppermute | solution.py:165
  168.1 2.5 %copy.51.refs_3_ = f32[640,320]{1,0:T(8,128)} copy(f32[640,320]{0,1:T(8,128)} %collective-permute-done.12) | data formatting | bytes 1638400 | tf_op jit(solution)/shard_map/ppermute | solution.py:165
  182.6 3.6 %shard_map.59 = f32[640,320]{1,0:T(8,128)S(1)} custom-call(s32[6]{0:T(128)S(1)} %stack.90.ids, bf16[4,320,320]{2,1,0:T(8,128)(2,1)S(1)} %copy-done.2, bf16[4,320,320]{2,1,0:T(8,128)(2,1)S(1)} %copy-done.7, f32[640,320]{1,0:T(8,128)S(1)} %copy-done.13, f32[640,320]{1,0:T(8,128)S(1)} %copy-done.15, f32[640,320]{1,0:T(8,128)S(1)} %copy-done.17, ...), custom_call_target="tpu_custom_call" | custom-call | flops 786432000 | bytes 6553600 | tf_op jit(solution)/shard_map/pallas_call | solution.py:33
  189.5 3.7 %collective-permute-done.19 = f32[8,320]{1,0:T(8,128)S(1)} collective-permute-done((f32[8,320]{1,0:T(8,128)S(1)}, f32[8,320]{1,0:T(8,128)S(1)}, u32[]{:S(2)}, u32[]{:S(2)}) %collective-permute-start.19) | collective-permute-done | bytes 10272 | tf_op jit(solution)/shard_map/ppermute | solution.py:165
  193.2 3.7 %collective-permute-done.20 = f32[8,320]{1,0:T(8,128)S(1)} collective-permute-done((f32[8,320]{1,0:T(8,128)S(1)}, f32[8,320]{1,0:T(8,128)S(1)}, u32[]{:S(2)}, u32[]{:S(2)}) %collective-permute-start.20) | collective-permute-done | bytes 10272 | tf_op jit(solution)/shard_map/ppermute | solution.py:165
  197.6 3.2 %collective-permute-start.23 = (f32[8,320]{1,0:T(8,128)S(1)}, f32[8,320]{1,0:T(8,128)S(1)}, u32[]{:S(2)}, u32[]{:S(2)}) collective-permute-start(f32[8,320]{1,0:T(8,128)S(1)} %add.77.refs_4_), channel_id=1, source_target_pairs={{0,6},{1,7},{2,0},{3,1},{4,2},{5,3},{6,4},{7,5},{8,14},{9,15},{10,... | collective-permute-start | bytes 30728 | tf_op jit(solution)/shard_map/ppermute | solution.py:165
  202.5 5.4 %collective-permute-done.22.refs_6_ = f32[8,320]{1,0:T(8,128)S(1)} collective-permute-done((f32[8,320]{1,0:T(8,128)S(1)}, f32[8,320]{1,0:T(8,128)S(1)}, u32[]{:S(2)}, u32[]{:S(2)}) %collective-permute-start.22) | collective-permute-done | bytes 10272 | tf_op jit(solution)/shard_map/ppermute | solution.py:165
  216.1 3.6 %shard_map.58 = f32[640,320]{1,0:T(8,128)S(1)} custom-call(s32[6]{0:T(128)S(1)} %stack.90.ids, bf16[4,320,320]{2,1,0:T(8,128)(2,1)S(1)} %get-tuple-element.20.refs_0_.refs_1_.high, bf16[4,320,320]{2,1,0:T(8,128)(2,1)S(1)} %get-tuple-element.21.refs_1_.refs_2_.low, f32[640,320]{1,0:T(8,128)S(1)} %copy-done.14, f32[640,320]{1,0:T(8,128)S(1)} %copy-done.16, ...), custom_call_target="tpu_custom_call" | custom-call | flops 786432000 | bytes 6553600 | tf_op jit(solution)/shard_map/pallas_call | solution.py:33
  (199 shorter events, 114.1 us)
Async XLA Ops:
  0.6 24.5 %collective-permute-start.3 = (f32[640,320]{0,1:T(8,128)}, f32[640,320]{0,1:T(8,128)}, u32[]{:S(2)}, u32[]{:S(2)}) collective-permute-start(f32[640,320]{0,1:T(8,128)} %param.3), channel_id=1, source_target_pairs={{0,2},{1,3},{2,4},{3,5},{4,6},{5,7},{6,0},{7,1},{8,10},{9,11},{10,... | collective-permute-start | bytes 2457608 | tf_op jit(solution)/shard_map/ppermute | solution.py:165
  6.2 2.0 collective-permute-start
  6.2 36.4 %collective-permute-start.6 = (f32[640,320]{0,1:T(8,128)}, f32[640,320]{0,1:T(8,128)}, u32[]{:S(2)}, u32[]{:S(2)}) collective-permute-start(f32[640,320]{0,1:T(8,128)} %param.3), channel_id=1, source_target_pairs={{0,6},{1,7},{2,0},{3,1},{4,2},{5,3},{6,4},{7,5},{8,14},{9,15},{10,... | collective-permute-start | bytes 2457608 | tf_op jit(solution)/shard_map/ppermute | solution.py:165
  9.3 35.8 %collective-permute-start.1 = (f32[320,640]{1,0:T(8,128)}, f32[320,640]{1,0:T(8,128)S(1)}, u32[]{:S(2)}, u32[]{:S(2)}) collective-permute-start(f32[320,640]{1,0:T(8,128)} %pad_maximum_fusion), channel_id=1, source_target_pairs={{0,8},{1,9},{2,10},{3,11},{4,12},{5,13},{6,14},{7,15},{8,0},{9,1},... | collective-permute-start | bytes 2457608 | tf_op jit(solution)/shard_map/ppermute | solution.py:165
  11.0 37.9 %collective-permute-start.2 = (f32[320,640]{1,0:T(8,128)}, f32[320,640]{1,0:T(8,128)S(1)}, u32[]{:S(2)}, u32[]{:S(2)}) collective-permute-start(f32[320,640]{1,0:T(8,128)} %pad_maximum_fusion), channel_id=1, source_target_pairs={{0,16},{1,17},{2,18},{3,19},{4,20},{5,21},{6,22},{7,23},{8,24},{9,... | collective-permute-start | bytes 2457608 | tf_op jit(solution)/shard_map/ppermute | solution.py:165
  25.2 24.7 %collective-permute-start.4 = (f32[320,640]{1,0:T(8,128)}, f32[320,640]{1,0:T(8,128)S(1)}, u32[]{:S(2)}, u32[]{:S(2)}) collective-permute-start(f32[320,640]{1,0:T(8,128)} %pad_maximum_fusion), channel_id=1, source_target_pairs={{0,24},{1,25},{2,26},{3,27},{4,28},{5,29},{6,30},{7,31},{8,16},{9,... | collective-permute-start | bytes 2457608 | tf_op jit(solution)/shard_map/ppermute | solution.py:165
  27.9 39.4 %collective-permute-start.5 = (f32[640,320]{0,1:T(8,128)}, f32[640,320]{0,1:T(8,128)}, u32[]{:S(2)}, u32[]{:S(2)}) collective-permute-start(f32[640,320]{0,1:T(8,128)} %collective-permute-done.3), channel_id=1, source_target_pairs={{0,2},{1,3},{2,4},{3,5},{4,6},{5,7},{6,0},{7,1},{8,10},{9,11},{10,... | collective-permute-start | bytes 2457608 | tf_op jit(solution)/shard_map/ppermute | solution.py:165
  78.0 23.6 %collective-permute-start.7 = (f32[640,320]{0,1:T(8,128)}, f32[640,320]{0,1:T(8,128)}, u32[]{:S(2)}, u32[]{:S(2)}) collective-permute-start(f32[640,320]{0,1:T(8,128)} %copy.32), channel_id=1, source_target_pairs={{0,1},{1,0},{2,3},{3,2},{4,5},{5,4},{6,7},{7,6},{8,9},{9,8},{10,11... | collective-permute-start | bytes 2457608 | tf_op jit(solution)/shard_map/ppermute | solution.py:168
  94.0 35.3 %collective-permute-start.14 = (f32[640,320]{0,1:T(8,128)}, f32[640,320]{0,1:T(8,128)}, u32[]{:S(2)}, u32[]{:S(2)}) collective-permute-start(f32[640,320]{0,1:T(8,128)} %copy.45), channel_id=1, source_target_pairs={{0,1},{1,0},{2,3},{3,2},{4,5},{5,4},{6,7},{7,6},{8,9},{9,8},{10,11... | collective-permute-start | bytes 2457608 | tf_op jit(solution)/shard_map/ppermute | solution.py:168
  108.8 10.8 %collective-permute-start.10 = (f32[320,320]{1,0:T(8,128)}, f32[320,320]{1,0:T(8,128)S(1)}, u32[]{:S(2)}, u32[]{:S(2)}) collective-permute-start(f32[320,320]{1,0:T(8,128)} %get-tuple-element.27), channel_id=1, source_target_pairs={{0,1},{1,0},{2,3},{3,2},{4,5},{5,4},{6,7},{7,6},{8,9},{9,8},{10,11... | collective-permute-start | bytes 1228808 | tf_op jit(solution)/shard_map/ppermute | solution.py:168
  108.8 16.2 %collective-permute-start.15 = (s32[10,5]{0,1:T(8,128)S(1)}, s32[10,5]{0,1:T(8,128)S(1)}, u32[]{:S(2)}, u32[]{:S(2)}) collective-permute-start(s32[10,5]{0,1:T(8,128)S(1)} %copy-done.58), channel_id=1, source_target_pairs={{0,2},{1,3},{10,8},{11,9},{20,22},{21,23},{30,28},{31,29}} | collective-permute-start | bytes 608 | tf_op jit(solution)/shard_map/ppermute | solution.py:165
  112.3 14.3 %collective-permute-start.16 = (s32[10,5]{0,1:T(8,128)S(1)}, s32[10,5]{0,1:T(8,128)S(1)}, u32[]{:S(2)}, u32[]{:S(2)}) collective-permute-start(s32[10,5]{0,1:T(8,128)S(1)} %copy-done.58), channel_id=1, source_target_pairs={{0,4},{1,5},{10,14},{11,15},{20,16},{21,17},{30,26},{31,27}} | collective-permute-start | bytes 608 | tf_op jit(solution)/shard_map/ppermute | solution.py:165
  116.5 11.5 %collective-permute-start.17 = (s32[10,5]{0,1:T(8,128)S(1)}, s32[10,5]{0,1:T(8,128)S(1)}, u32[]{:S(2)}, u32[]{:S(2)}) collective-permute-start(s32[10,5]{0,1:T(8,128)S(1)} %copy-done.58), channel_id=1, source_target_pairs={{0,6},{1,7},{10,12},{11,13},{20,18},{21,19},{30,24},{31,25}} | collective-permute-start | bytes 608 | tf_op jit(solution)/shard_map/ppermute | solution.py:165
  119.7 29.7 %collective-permute-start.8 = (f32[640,320]{0,1:T(8,128)}, f32[640,320]{0,1:T(8,128)}, u32[]{:S(2)}, u32[]{:S(2)}) collective-permute-start(f32[640,320]{0,1:T(8,128)} %copy.36), channel_id=1, source_target_pairs={{2,4},{3,5},{4,6},{5,7},{6,2},{7,3},{8,12},{9,13},{12,14},{13,15},... | collective-permute-start | bytes 2457608 | tf_op jit(solution)/shard_map/ppermute | solution.py:165
  125.1 26.7 %collective-permute-start.9 = (f32[640,320]{0,1:T(8,128)}, f32[640,320]{0,1:T(8,128)}, u32[]{:S(2)}, u32[]{:S(2)}) collective-permute-start(f32[640,320]{0,1:T(8,128)} %copy.36), channel_id=1, source_target_pairs={{2,6},{3,7},{4,2},{5,3},{6,4},{7,5},{8,14},{9,15},{12,8},{13,9},{1... | collective-permute-start | bytes 2457608 | tf_op jit(solution)/shard_map/ppermute | solution.py:165
  126.6 27.6 %collective-permute-start.11 = (f32[640,320]{0,1:T(8,128)}, f32[640,320]{0,1:T(8,128)}, u32[]{:S(2)}, u32[]{:S(2)}) collective-permute-start(f32[640,320]{0,1:T(8,128)} %copy.38), channel_id=1, source_target_pairs={{2,10},{3,11},{8,0},{9,1},{22,30},{23,31},{28,20},{29,21}} | collective-permute-start | bytes 2457608 | tf_op jit(solution)/shard_map/ppermute | solution.py:165
  127.9 40.1 %collective-permute-start.12 = (f32[640,320]{0,1:T(8,128)}, f32[640,320]{0,1:T(8,128)}, u32[]{:S(2)}, u32[]{:S(2)}) collective-permute-start(f32[640,320]{0,1:T(8,128)} %copy.38), channel_id=1, source_target_pairs={{4,20},{5,21},{14,30},{15,31},{16,0},{17,1},{26,10},{27,11}} | collective-permute-start | bytes 2457608 | tf_op jit(solution)/shard_map/ppermute | solution.py:165
  129.2 41.3 %collective-permute-start.13 = (f32[640,320]{0,1:T(8,128)}, f32[640,320]{0,1:T(8,128)}, u32[]{:S(2)}, u32[]{:S(2)}) collective-permute-start(f32[640,320]{0,1:T(8,128)} %copy.38), channel_id=1, source_target_pairs={{6,30},{7,31},{12,20},{13,21},{18,10},{19,11},{24,0},{25,1}} | collective-permute-start | bytes 2457608 | tf_op jit(solution)/shard_map/ppermute | solution.py:165
  189.5 31.1 %collective-permute-start.18 = (f32[640,320]{0,1:T(8,128)}, f32[640,320]{0,1:T(8,128)}, u32[]{:S(2)}, u32[]{:S(2)}) collective-permute-start(f32[640,320]{0,1:T(8,128)} %copy.58), channel_id=1, source_target_pairs={{0,1},{1,0},{2,3},{3,2},{4,5},{5,4},{6,7},{7,6},{8,9},{9,8},{10,11... | collective-permute-start | bytes 2457608 | tf_op jit(solution)/shard_map/ppermute | solution.py:168
  189.5 3.7 %collective-permute-start.19 = (f32[8,320]{1,0:T(8,128)S(1)}, f32[8,320]{1,0:T(8,128)S(1)}, u32[]{:S(2)}, u32[]{:S(2)}) collective-permute-start(f32[8,320]{1,0:T(8,128)S(1)} %get-tuple-element.33), channel_id=1, source_target_pairs={{0,8},{1,9},{2,10},{3,11},{4,12},{5,13},{6,14},{7,15},{8,0},{9,1},... | collective-permute-start | bytes 30728 | tf_op jit(solution)/shard_map/ppermute | solution.py:165
  193.2 3.7 %collective-permute-start.20 = (f32[8,320]{1,0:T(8,128)S(1)}, f32[8,320]{1,0:T(8,128)S(1)}, u32[]{:S(2)}, u32[]{:S(2)}) collective-permute-start(f32[8,320]{1,0:T(8,128)S(1)} %add.76), channel_id=1, source_target_pairs={{0,16},{1,17},{2,18},{3,19},{4,20},{5,21},{6,22},{7,23},{8,24},{9,... | collective-permute-start | bytes 30728 | tf_op jit(solution)/shard_map/ppermute | solution.py:165
  196.9 5.5 %collective-permute-start.21 = (f32[8,320]{1,0:T(8,128)S(1)}, f32[8,320]{1,0:T(8,128)S(1)}, u32[]{:S(2)}, u32[]{:S(2)}) collective-permute-start(f32[8,320]{1,0:T(8,128)S(1)} %add.77.refs_4_), channel_id=1, source_target_pairs={{0,2},{1,3},{2,4},{3,5},{4,6},{5,7},{6,0},{7,1},{8,10},{9,11},{10,... | collective-permute-start | bytes 30728 | tf_op jit(solution)/shard_map/ppermute | solution.py:165
  197.6 4.9 %collective-permute-start.23 = (f32[8,320]{1,0:T(8,128)S(1)}, f32[8,320]{1,0:T(8,128)S(1)}, u32[]{:S(2)}, u32[]{:S(2)}) collective-permute-start(f32[8,320]{1,0:T(8,128)S(1)} %add.77.refs_4_), channel_id=1, source_target_pairs={{0,6},{1,7},{2,0},{3,1},{4,2},{5,3},{6,4},{7,5},{8,14},{9,15},{10,... | collective-permute-start | bytes 30728 | tf_op jit(solution)/shard_map/ppermute | solution.py:165
  202.4 5.5 %collective-permute-start.22 = (f32[8,320]{1,0:T(8,128)S(1)}, f32[8,320]{1,0:T(8,128)S(1)}, u32[]{:S(2)}, u32[]{:S(2)}) collective-permute-start(f32[8,320]{1,0:T(8,128)S(1)} %collective-permute-done.21.refs_5_), channel_id=1, source_target_pairs={{0,2},{1,3},{2,4},{3,5},{4,6},{5,7},{6,0},{7,1},{8,10},{9,11},{10,... | collective-permute-start | bytes 30728 | tf_op jit(solution)/shard_map/ppermute | solution.py:165
  (61 other events, 113.0 us)

commit v3 on v0

v3 whole, which is shorter than its diff:
```python
import functools

import jax
import jax.numpy as jnp
from jax import lax
from jax.experimental import pallas as pl
from jax.experimental.pallas import tpu as pltpu
from jax.sharding import PartitionSpec as P

BLK = 64
ROWS, LANES = 8, 128
VMEM_BYTES = 24 * 1024 * 1024
ROW_BY_COLUMN = ((1,), (0,))
ROW_BY_ROW = ((1,), (1,))
COLUMN_BY_COLUMN = ((0,), (0,))

CORE, DOWN, ROW, COLUMN, BACK, LISTS = range(6)


def parts(value):
    high = value.astype(jnp.bfloat16)
    return high, (value - high.astype(jnp.float32)).astype(jnp.bfloat16)


def first(value, axis):
    high, low = parts(value)
    return jnp.concatenate([high, high, low], axis=axis)


def second(value, axis):
    high, low = parts(value)
    return jnp.concatenate([high, low, high], axis=axis)


def dot(a, b, contract=ROW_BY_COLUMN):
    return lax.dot_general(a, b, (contract, ((), ())), preferred_element_type=jnp.float32)


def call(kernel, outs, ids, *arrays, placed=0, scratch=()):
    copied = len(arrays) - placed
    held = [pltpu.VMEM(a.shape, a.dtype) for a in arrays[:copied]]
    n_outs = len(jax.tree.leaves(outs))

    def body(ids_ref, *refs):
        sources, rest, own = refs[:copied], refs[copied : len(arrays) + n_outs], refs[len(arrays) + n_outs :]
        targets, sems, own = own[:copied], own[copied], own[copied + 1 :]
        copies = [pltpu.make_async_copy(a, b, sems.at[i]) for i, (a, b) in enumerate(zip(sources, targets))]
        for copy in copies:
            copy.start()
        for copy in copies:
            copy.wait()
        kernel(ids_ref, *targets, *rest, *own)

    return pl.pallas_call(
        body,
        out_shape=outs,
        in_specs=[pl.BlockSpec(memory_space=pltpu.SMEM)] + [pl.BlockSpec(memory_space=pl.ANY)] * len(arrays),
        scratch_shapes=held + [pltpu.SemaphoreType.DMA((max(copied, 1),))] + list(scratch),
        compiler_params=pltpu.CompilerParams(vmem_limit_bytes=VMEM_BYTES),
    )(ids, *arrays)


def shape(*dims, dtype=jnp.float32):
    return jax.ShapeDtypeStruct(dims, dtype)


def after(value, *earlier):
    return lax.optimization_barrier((value, *earlier))[0]


def in_half(value, which):
    half = value.shape[1] // 2
    return jnp.where(which == 0, value[:, :half], value[:, half:])


def ones(count, wide, entry):
    dims = [wide, wide]
    dims[entry] = count * BLK
    entries = lax.broadcasted_iota(jnp.int32, dims, entry)
    return (entries // BLK == lax.broadcasted_iota(jnp.int32, dims, 1 - entry)).astype(jnp.bfloat16)


def spread(blocks, half, height):
    rows = dot(ones(half // BLK, blocks.shape[0], 0), blocks.astype(jnp.bfloat16))
    return dot(rows.astype(jnp.bfloat16), ones(height // BLK, blocks.shape[1], 1))


def pack_kernel(core, tile, pattern, packed, mine, other, blocks):
    half, (high, wide) = tile.shape[0], pattern.shape
    packed[:half, :] = tile[...]
    packed[half:, :] = jnp.zeros((ROWS, tile.shape[1]), jnp.float32)

    def unit(rows, columns):
        same = lax.broadcasted_iota(jnp.int32, (rows, columns), 0) == lax.broadcasted_iota(jnp.int32, (rows, columns), 1)
        return same.astype(jnp.bfloat16)

    turned = dot(unit(ROWS, wide), pattern[...].astype(jnp.float32).astype(jnp.bfloat16), ROW_BY_ROW)
    blocks[...] = dot(turned.astype(jnp.bfloat16), unit(high, LANES))
    packed[half:, :LANES] = blocks[...]
    mine[...] = in_half(tile[...], core[0])
    other[:half, :] = in_half(tile[...], 1 - core[0])
    other[half:, :] = jnp.zeros((ROWS, half), jnp.float32)
    other[half:, :LANES] = blocks[...]


def split_kernel(ids, *refs):
    tiles, (kept, given) = refs[:-2], refs[-2:]
    half = kept.shape[1]
    for m, tile in enumerate(tiles):
        kept[ids[LISTS + m]] = first(tile[:, :half], 1)
        given[ids[LISTS + m]] = first(tile[:, half:], 1)


def held_parts(count, half):
    return [pltpu.VMEM((count, half, 3 * half), jnp.bfloat16), pltpu.SemaphoreType.DMA((count,))]


def fetch(sources, held, sems):
    copies = [pltpu.make_async_copy(source, held.at[t], sems.at[t]) for t, source in enumerate(sources)]
    for copy in copies:
        copy.start()
    for copy in copies:
        copy.wait()


def sums_of_products(places, lefts, starts, rights, held, sems):
    half, count = held.shape[1], len(lefts)
    fetch([right.at[place] for right in rights for place in places], held, sems)
    totals = [None if start is None else start[...] for start in starts]
    for j, left in enumerate(lefts):
        value = second(left[:half, :], 0)
        for s in range(len(rights)):
            term = dot(held[s * count + j], value)
            totals[s] = term if totals[s] is None else totals[s] + term
    return totals


def early_products_kernel(early, line_at, ids, *refs):
    count = len(early)
    lefts, rights, outs, (held, sems) = refs[:count], refs[count : count + 2], refs[count + 2 : count + 4], refs[count + 4 :]
    places = [ids[line_at + j] for j in early]
    for out, total in zip(outs, sums_of_products(places, lefts, [None, None], rights, held, sems)):
        out[...] = total


def last_product_kernel(place, ids, left, start_kept, start_given, right_kept, right_given, kept, given, held, sems):
    height = kept.shape[1]
    starts = [start_kept, start_given]
    kept_sum, given_sum = sums_of_products([ids[place]], [left], starts, [right_kept, right_given], held, sems)
    kept[...] = kept_sum
    given[:, :height] = given_sum
    given[:, height:] = in_half(kept_sum, 1 - ids[CORE])


def square_kernel(ids, kept, given, received, blocks, their_blocks, weights, *outs):
    half, height = kept.shape
    square, sums, outs = outs[0], outs[1], outs[2:]
    product = kept[...] + received[:, :height]
    square[...] = product * spread(blocks[...], half, height)
    row = first(jnp.broadcast_to(weights[...], (ROWS, height)), 1)
    sums[...] = jnp.zeros_like(sums)
    sums[0:1, :] = dot(row, second(product, 1), ROW_BY_ROW)[0:1, :]
    other = in_half(given[:, :height], ids[CORE]) + received[:, height:]
    other = (other * in_half(spread(their_blocks[...], half, height), ids[CORE])).T
    own = in_half(square[...], ids[CORE]).T
    for step, out in enumerate(outs):

        @pl.when(ids[DOWN] != step)
        def _():
            out[...] = square[...]

        @pl.when(ids[DOWN] == step)
        def _():
            out[:, :half] = jnp.where(ids[CORE] == 0, own, other)
            out[:, half:] = jnp.where(ids[CORE] == 0, other, own)


def last_kernel(count, place, ids, start, weights, right, *refs):
    sources, out, held, held_sems, tiles, sems = refs[:count], *refs[count:]
    half, height = start.shape

    def copies(t):
        k = jnp.maximum(ids[place + t], 0)
        yield pltpu.make_async_copy(right.at[k], held.at[t], held_sems.at[t])
        yield pltpu.make_async_copy(sources[t], tiles.at[t], sems.at[t])

    for t in range(count):
        for copy in copies(t):
            copy.start()
    out[:half, :] = start[...]
    for t in range(count):
        for copy in copies(t):
            copy.wait()

        @pl.when(ids[place + t] >= 0)
        def _():
            out[:half, :] += dot(held[t], second(tiles[t], 0))

    row = first(jnp.broadcast_to(weights[...], (ROWS, height)), 1)
    out[half:, :] = jnp.zeros((ROWS, height), jnp.float32)
    out[half + 1 : half + 2, :half] = dot(row, second(out[:half, :], 1), ROW_BY_ROW)[1:2, :]


def diagonal_early_kernel(ids, *refs):
    lefts, out = refs[:-1], refs[-1]
    for j, left in enumerate(lefts):
        tile = left[: out.shape[0] // 2, :]
        term = dot(first(tile, 0), second(tile, 0), COLUMN_BY_COLUMN)
        out[...] = term if j == 0 else out[...] + term


def diagonal_kernel(last, ids, start, left, *refs):
    patterns, (given, kept, blocks, whole) = refs[:-4], refs[-4:]
    half = given.shape[0]
    tile = left[:half, :]
    whole[...] = start[...] + dot(first(tile, 0), second(tile, 0), COLUMN_BY_COLUMN)
    given[...] = whole[pl.ds(pl.multiple_of((1 - ids[CORE]) * half, half), half), :]
    kept[...] = whole[pl.ds(pl.multiple_of(ids[CORE] * half, half), half), :]
    blocks[...] = jnp.zeros_like(blocks)
    for j, pattern in enumerate(patterns):

        @pl.when(ids[BACK] == j + 1)
        def _():
            blocks[...] = pattern[...]


def early_kernel(ids, square, kept, received, blocks, *refs):
    rights, outs, (held, sems) = refs[:2], refs[2:4], refs[4:]
    fetch([right.at[place] for right in rights for place in (ids[COLUMN], ids[ROW])], held, sems)
    own = second(square[...], 0)
    diagonal = second((kept[...] + received[...]) * spread(blocks[...], *kept.shape), 0)
    for s, out in enumerate(outs):
        out[...] = dot(held[2 * s], own) + dot(held[2 * s + 1], diagonal)


def purify_kernel(ids, square, kept, received, blocks, out):
    half, height = square.shape
    cube = kept[:half, :] + received[:half, :]
    out[...] = 3.0 * square[...] - 2.0 * (spread(blocks[...], half, height) * cube)


def in_steps(edges):
    sent, got, count = {}, {}, 0
    for source, target in edges:
        count = max(count, sum(e[0] == source for e in edges), sum(e[1] == target for e in edges))
    for source, target in edges:
        free = next(i for i in range(count) if (source, i) not in sent)
        other = next(i for i in range(count) if (target, i) not in got)
        if free != other:
            path, node, at_target, step = [], target, True, free
            while (node, step) in (got if at_target else sent):
                partner = (got if at_target else sent)[node, step]
                path.append((partner, node, step) if at_target else (node, partner, step))
                node, at_target, step = partner, not at_target, free + other - step
            for u, v, step in path:
                del sent[u, step], got[v, step]
            for u, v, step in path:
                sent[u, free + other - step], got[v, free + other - step] = v, u
        sent[source, free], got[target, free] = target, source
    return count, sent, got


def make_body(panels, columns):
    assert columns == 2 * panels and panels & (panels - 1) == 0
    chips = [(r, z) for r in range(panels) for z in range(panels)]

    edges = [((r, z), (r, q)) for r, z in chips for q in range(panels) if z != r and q != r and q != z]
    edges += [((r, z), (z, z)) for r, z in chips if z != r]
    steps, sent, got = in_steps(edges)
    down_step = [[-1] * panels for _ in range(panels)]
    tile_got = [[[-1] * steps for _ in range(panels)] for _ in range(panels)]
    for ((r, z), step), target in sent.items():
        if target[0] != r:
            down_step[r][z] = step
    for ((r, z), step), source in got.items():
        tile_got[r][z][step] = source[1] if source[0] == r else source[0]

    def send(value, target):
        pairs = []
        for r, z in chips:
            to = target(r, z)
            if to is not None:
                pairs += [(r * columns + 2 * z + core, to[0] * columns + 2 * to[1] + core) for core in (0, 1)]
        return lax.ppermute(value, ("row", "col"), pairs)

    def swap_core(value):
        return lax.ppermute(value, "col", [(c, c ^ 1) for c in range(columns)])

    def ring(step):
        return lambda r, z: (r, (z + step) % panels)

    def across(m):
        return lambda r, z: (r ^ m, z)

    def step_target(step, r, z):
        return sent.get(((r, z), step))

    powers = [1 << i for i in range(panels.bit_length() - 1)]

    def body(density, pattern, weights):
        r = lax.axis_index("row")
        c = lax.axis_index("col")
        z, core = c // 2, c % 2
        tile = density.T
        half, height = tile.shape

        scalars = [core, jnp.asarray(down_step)[r, z], r, z, (z - r) % panels]
        scalars += [r ^ m for m in range(panels)] + [(z - j) % panels for j in range(panels)]
        scalars += list(jnp.asarray(tile_got)[r, z])
        ids = jnp.stack([jnp.asarray(s, jnp.int32) for s in scalars])
        line_at, steps_at = LISTS + panels, LISTS + 2 * panels

        packed, mine, other, blocks = call(
            pack_kernel,
            [shape(half + ROWS, height), shape(half, half), shape(half + ROWS, half), shape(ROWS, LANES)],
            jnp.asarray(core, jnp.int32)[None],
            tile,
            pattern,
        )
        left = {0: packed, 1: send(packed, ring(1))}
        theirs = swap_core(other)
        own = jnp.concatenate([mine, theirs[:half]], axis=1)
        their_blocks = theirs[half:, :LANES]
        tiles = {m: send(own, across(m)) for m in powers}
        nearest = [tiles[m] for m in powers]
        own_later = after(own, *nearest)
        tiles = [own] + [tiles[m] if m in powers else send(own_later, across(m)) for m in range(1, panels)]
        last = panels // 2 + 1
        for j in range(2, last):
            left[j] = send(left[j - 1], ring(1))
        for j in range(panels - 1, last - 1, -1):
            left[j] = send(after(packed, *nearest) if j == panels - 1 else left[j + 1], ring(-1))

        part = shape(panels, half, 3 * half, dtype=jnp.bfloat16)
        kept, given = call(split_kernel, [part] * 2, ids, *tiles)

        early = [j for j in range(panels) if j != last]
        starts = call(
            functools.partial(early_products_kernel, early, line_at),
            [shape(half, height)] * 2,
            ids,
            *[left[j] for j in early],
            kept,
            given,
            placed=2,
            scratch=held_parts(2 * len(early), half),
        )
        diagonal_start = call(diagonal_early_kernel, shape(height, height), ids, *[left[j] for j in early])
        kept_sum, given_sum = call(
            functools.partial(last_product_kernel, line_at + last),
            [shape(half, height), shape(half, height + half)],
            ids,
            left[last],
            *starts,
            kept,
            given,
            placed=2,
            scratch=held_parts(2, half),
        )
        square, sums, *rows = call(
            square_kernel,
            [shape(half, height), shape(ROWS, half)] + [shape(half, height)] * steps,
            ids,
            kept_sum,
            given_sum,
            swap_core(given_sum),
            blocks,
            their_blocks,
            weights[None, :],
        )

        arrived = [send(rows[step], functools.partial(step_target, step)) for step in range(steps)]
        diagonal_given, diagonal_kept, diagonal_blocks = call(
            functools.partial(diagonal_kernel, last),
            [shape(half, height)] * 2 + [shape(ROWS, LANES)],
            ids,
            after(diagonal_start, rows[0]),
            left[last],
            *[left[j][half:, :LANES] for j in range(1, panels)],
            scratch=[pltpu.VMEM((2 * half, height), jnp.float32)],
        )
        cube = call(
            early_kernel,
            [shape(half, height)] * 2,
            ids,
            square,
            diagonal_kept,
            swap_core(diagonal_given),
            diagonal_blocks,
            kept,
            given,
            placed=2,
            scratch=held_parts(4, half),
        )

        held = [pltpu.VMEM((steps, half, height), jnp.float32), pltpu.SemaphoreType.DMA((steps,))]

        def finish(side, start):
            kernel = functools.partial(last_kernel, steps, steps_at)
            scratch = held_parts(steps, half) + held
            arrays = [start, weights[None, :], side, *arrived]
            return call(kernel, shape(half + ROWS, height), ids, *arrays, placed=steps + 1, scratch=scratch)

        given_cube = finish(given, cube[1])
        kept_cube = finish(kept, cube[0])
        received = swap_core(given_cube)
        sums = sums + kept_cube[half:, :half] + received[half:, :half]
        for m in powers:
            sums = sums + send(sums, across(m))
        purified = call(purify_kernel, shape(half, height), ids, square, kept_cube, received, blocks)
        return purified.T, sums[:2]

    return body


def solution(mesh):
    in_specs = (P("row", "col"), P("row", "col"), P("row"))
    out_specs = (P("row", "col"), P(None, "col"))
    body = make_body(mesh.shape["row"], mesh.shape["col"])
    return jax.shard_map(body, mesh=mesh, in_specs=in_specs, out_specs=out_specs, check_vma=False)
```

time: 224 us -> 139 us (0.62)
  waiting for transfers between devices: 135 us -> 66.4 us
  blocking collectives: 37.2 us -> 0 us
  Pallas kernels: 0 us -> 35.2 us
  matrix products: 33 us -> 0 us
  starting transfers between devices: 0.11 us -> 21.1 us
  between operations: 14.5 us -> 0.86 us
  local copies, waits for them, and re-layouts: 2.25 us -> 12.8 us
    all_gather x3 -> x0, waiting for transfers between devices: 134 us -> none  [the longest x2 85.8 us: multiply(): lax.all_gather(left_tile, 'col', axis=1, tiled=True)]
    ppermute x0 -> x15, waiting for transfers between devices: none -> 66.4 us  [the longest x11 66.4 us: send(): return lax.ppermute(value, ('row', 'col'), pairs)]
    pallas_call x0 -> x11, Pallas kernels: none -> 35.2 us  [call(): pl.pallas_call(body, out_shape=outs, in_specs=[pl.BlockSpec(memory_space=...]
    dot_general x6 -> x0, matrix products: 33 us -> none  [full_dot(): jnp.dot(first, second, precision=lax.Precision.HIGHEST, preferred_element...]
    another operation x1 -> x0, blocking collectives: 27.3 us -> none
    ppermute x0 -> x15, starting transfers between devices: none -> 21.1 us  [the longest x11 19.9 us: send(): return lax.ppermute(value, ('row', 'col'), pairs)]
    psum x1 -> x0, blocking collectives: 9.87 us -> none  [multiply(): summed = lax.psum(partial_row, 'row')]
    unnamed x14 -> x15, local copies, waits for them, and re-layouts: 2.03 us -> 6.82 us
  transfers between devices with their start and end apart: 3 -> 15, of which waited for: 3 -> 8; matrix products, arithmetic and copies ran while one was open for 5% -> 5% of each run, Pallas kernels for 0% -> 17%
where the time goes in v3:
time: 139 us; the launch traced here: 138 us
  waiting for transfers between devices  66.4 us (48%)
  Pallas kernels  35.2 us (25%)
  starting transfers between devices  21.1 us (15%)
  local copies, waits for them, and re-layouts  12.8 us (9%)
  other arithmetic  1.68 us (1%)
    ppermute x11, waiting for transfers between devices, send(): return lax.ppermute(value, ('row', 'col'), pairs)  66.4 us
    pallas_call x11, Pallas kernels, call(): pl.pallas_call(body, out_shape=outs, in_specs=[pl.BlockSpec(memory_space=...  35.2 us
    ppermute x11, starting transfers between devices, send(): return lax.ppermute(value, ('row', 'col'), pairs)  19.9 us
    unnamed x15, local copies, waits for them, and re-layouts  6.82 us
  transfers between devices with their start and end apart: 15, of which 8 were waited for; matrix products, arithmetic and copies ran while one was open for 5% of the time, Pallas kernels for 17%

profile of v3, /device:TPU:0, one launch (start us, length us, event | category | flops | bytes accessed | tf_op | source)
XLA Modules:
  0.0 138.1 jit_solution(17387399665265133140)
XLA Ops:
  3.5 2.6 %collective-permute-start.4 = (f32[328,640]{1,0:T(8,128)S(1)}, f32[328,640]{1,0:T(8,128)S(1)}, u32[]{:S(2)}, u32[]{:S(2)}) collective-permute-start(f32[328,640]{1,0:T(8,128)S(1)} %get-tuple-element.28.refs_0_), channel_id=1, source_target_pairs={{0,2},{1,3},{2,4},{3,5},{4,6},{5,7},{6,0},{7,1},{8,10},{9,11},{10,... | collective-permute-start | bytes 2519048 | tf_op jit(solution)/shard_map/ppermute | solution.py:284
  8.1 1.8 %collective-permute-start.2 = (f32[320,640]{1,0:T(8,128)}, f32[320,640]{1,0:T(8,128)S(1)}, u32[]{:S(2)}, u32[]{:S(2)}) collective-permute-start(f32[320,640]{1,0:T(8,128)} %pad_maximum_fusion.refs_0_), channel_id=1, source_target_pairs={{0,16},{1,17},{2,18},{3,19},{4,20},{5,21},{6,22},{7,23},{8,24},{9,... | collective-permute-start | bytes 2457608 | tf_op jit(solution)/shard_map/ppermute | solution.py:284
  9.8 1.5 %collective-permute-start.1 = (f32[320,640]{1,0:T(8,128)}, f32[320,640]{1,0:T(8,128)S(1)}, u32[]{:S(2)}, u32[]{:S(2)}) collective-permute-start(f32[320,640]{1,0:T(8,128)} %pad_maximum_fusion.refs_0_), channel_id=1, source_target_pairs={{0,8},{1,9},{2,10},{3,11},{4,12},{5,13},{6,14},{7,15},{8,0},{9,1},... | collective-permute-start | bytes 2457608 | tf_op jit(solution)/shard_map/ppermute | solution.py:284
  11.3 16.2 %collective-permute-done.4.refs_1_ = f32[328,640]{1,0:T(8,128)S(1)} collective-permute-done((f32[328,640]{1,0:T(8,128)S(1)}, f32[328,640]{1,0:T(8,128)S(1)}, u32[]{:S(2)}, u32[]{:S(2)}) %collective-permute-start.4) | collective-permute-done | bytes 839712 | tf_op jit(solution)/shard_map/ppermute | solution.py:284
  30.9 3.6 %collective-permute-start.3 = (f32[328,640]{1,0:T(8,128)S(1)}, f32[328,640]{1,0:T(8,128)S(1)}, u32[]{:S(2)}, u32[]{:S(2)}) collective-permute-start(f32[328,640]{1,0:T(8,128)S(1)} %get-tuple-element.28.refs_0_), channel_id=1, source_target_pairs={{0,6},{1,7},{2,0},{3,1},{4,2},{5,3},{6,4},{7,5},{8,14},{9,15},{10,... | collective-permute-start | bytes 2519048 | tf_op jit(solution)/shard_map/ppermute | solution.py:284
  34.5 2.1 %collective-permute-start.6 = (f32[320,640]{1,0:T(8,128)}, f32[320,640]{1,0:T(8,128)}, u32[]{:S(2)}, u32[]{:S(2)}) collective-permute-start(f32[320,640]{1,0:T(8,128)} %pad_maximum_fusion.refs_0_), channel_id=1, source_target_pairs={{0,24},{1,25},{2,26},{3,27},{4,28},{5,29},{6,30},{7,31},{8,16},{9,... | collective-permute-start | bytes 2457608 | tf_op jit(solution)/shard_map/ppermute | solution.py:284
  36.7 1.3 dynamic_slice.6
  39.4 2.6 %stack.48.ids_ref = s32[16]{0:T(128)S(1)} concatenate(s32[1]{0:T(128)} %bitcast.ids_ref, s32[1]{0:T(128)} %bitcast.1, s32[1]{0:T(128)} %bitcast.2, s32[1]{0:T(128)} %bitcast.3, s32[1]{0:T(128)} %bitcast.4, s32[1]{0:T(128)} %bitcast.2, s32[1]{0:T(128)} %bitcast.5, s32[1]{0:T(128)} %bitcast.6, s32[1]{0:T(128)} %bitcast.7, s32[1]{0:T(128)} %bitcast.8, s32[1]{0:T(128)} %bitcast.9, ...), dimensions={0} | concatenate | bytes 128 | tf_op jit(solution)/shard_map/stack | solution.py:310
  42.0 12.7 %collective-permute-done.6.refs_3_ = f32[320,640]{1,0:T(8,128)} collective-permute-done((f32[320,640]{1,0:T(8,128)}, f32[320,640]{1,0:T(8,128)}, u32[]{:S(2)}, u32[]{:S(2)}) %collective-permute-start.6) | collective-permute-done | bytes 819232 | tf_op jit(solution)/shard_map/ppermute | solution.py:284
  56.9 2.9 %shard_map.69 = (bf16[4,320,960]{2,1,0:T(8,128)(2,1)S(1)}, bf16[4,320,960]{2,1,0:T(8,128)(2,1)S(1)}) custom-call(s32[16]{0:T(128)S(1)} %stack.48.ids_ref, f32[320,640]{1,0:T(8,128)} %pad_maximum_fusion.refs_0_, f32[320,640]{1,0:T(8,128)S(1)} %copy-done.3, f32[320,640]{1,0:T(8,128)S(1)} %copy-done.1, f32[320,640]{1,0:T(8,128)} %collective-permute-done.6.refs_3_), custom_call_target="tpu_custom_call" | custom-call | tf_op jit(solution)/shard_map/pallas_call | solution.py:54
  59.9 5.5 %shard_map.70 = (f32[320,640]{1,0:T(8,128)S(1)}, f32[320,640]{1,0:T(8,128)S(1)}) custom-call(s32[16]{0:T(128)S(1)} %stack.48.ids_ref, f32[328,640]{1,0:T(8,128)S(1)} %get-tuple-element.28.refs_0_, f32[328,640]{1,0:T(8,128)S(1)} %collective-permute-done.4.refs_1_, f32[328,640]{1,0:T(8,128)S(1)} %collective-permute-done.5.refs_2_, ...), custom_call_target="tpu_custom_call" | custom-call | tf_op jit(solution)/shard_map/pallas_call | solution.py:54
  65.3 2.4 %collective-permute-done.3.refs_0_.refs_1_ = f32[328,640]{1,0:T(8,128)S(1)} collective-permute-done((f32[328,640]{1,0:T(8,128)S(1)}, f32[328,640]{1,0:T(8,128)S(1)}, u32[]{:S(2)}, u32[]{:S(2)}) %collective-permute-start.3) | collective-permute-done | bytes 839712 | tf_op jit(solution)/shard_map/ppermute | solution.py:284
  67.7 2.5 %shard_map.71 = (f32[320,640]{1,0:T(8,128)S(1)}, f32[320,960]{1,0:T(8,128)S(1)}) custom-call(s32[16]{0:T(128)S(1)} %stack.48.ids_ref, f32[328,640]{1,0:T(8,128)S(1)} %collective-permute-done.3.refs_0_.refs_1_, f32[320,640]{1,0:T(8,128)S(1)} %get-tuple-element.32.refs_1_, f32[320,640]{1,0:T(8,128)S(1)} %get-tuple-element.33.refs_2_, ...), custom_call_target="tpu_custom_call" | custom-call | tf_op jit(solution)/shard_map/pallas_call | solution.py:54
  71.1 4.2 %shard_map.73.refs_0_ = f32[640,640]{1,0:T(8,128)S(1)} custom-call(s32[16]{0:T(128)S(1)} %stack.48.ids_ref, f32[328,640]{1,0:T(8,128)S(1)} %get-tuple-element.28.refs_0_, f32[328,640]{1,0:T(8,128)S(1)} %collective-permute-done.4.refs_1_, f32[328,640]{1,0:T(8,128)S(1)} %collective-permute-done.5.refs_2_), custom_call_target="tpu_custom_call" | custom-call | tf_op jit(solution)/shard_map/pallas_call | solution.py:54
  75.3 2.4 %shard_map.72 = (f32[320,640]{1,0:T(8,128)S(1)}, f32[8,320]{1,0:T(8,128)S(1)}, f32[320,640]{1,0:T(8,128)S(1)}, f32[320,640]{1,0:T(8,128)S(1)}, f32[320,640]{1,0:T(8,128)S(1)}) custom-call(s32[16]{0:T(128)S(1)} %stack.48.ids_ref, f32[320,640]{1,0:T(8,128)S(1)} %get-tuple-element.34.refs_0_, f32[320,960]{1,0:T(8,128)S(1)} %get-tuple-element.35.refs_1_, ...), custom_call_target="tpu_custom_call" | custom-call | tf_op jit(solution)/shard_map/pallas_call | solution.py:54
  77.7 2.3 %shard_map.74 = (f32[320,640]{1,0:T(8,128)S(1)}, f32[320,640]{1,0:T(8,128)S(1)}, f32[8,128]{1,0:T(8,128)S(1)}) custom-call(s32[16]{0:T(128)S(1)} %stack.48.ids_ref, f32[640,640]{1,0:T(8,128)S(1)} %shard_map.73.refs_0_, f32[328,640]{1,0:T(8,128)S(1)} %collective-permute-done.3.refs_0_.refs_1_, f32[8,128]{1,0:T(8,128)S(1)} %slice.37.refs_2_, ...), custom_call_target="tpu_custom_call" | custom-call | tf_op jit(solution)/shard_map/pallas_call | solution.py:54
  81.8 1.3 collective-permute-start.11
  84.4 4.3 %shard_map.75 = (f32[320,640]{1,0:T(8,128)S(1)}, f32[320,640]{1,0:T(8,128)S(1)}) custom-call(s32[16]{0:T(128)S(1)} %stack.48.ids_ref, f32[320,640]{1,0:T(8,128)S(1)} %get-tuple-element.37.refs_0_, f32[320,640]{1,0:T(8,128)S(1)} %get-tuple-element.40.refs_1_, f32[320,640]{1,0:T(8,128)S(1)} %collective-permute-done.8.refs_2_, ...), custom_call_target="tpu_custom_call" | custom-call | tf_op jit(solution)/shard_map/pallas_call | solution.py:54
  88.7 31.4 %collective-permute-done.10.refs_4_ = f32[320,640]{1,0:T(8,128)S(1)} collective-permute-done((f32[320,640]{1,0:T(8,128)S(1)}, f32[320,640]{1,0:T(8,128)S(1)}, u32[]{:S(2)}, u32[]{:S(2)}) %collective-permute-start.10) | collective-permute-done | bytes 819232 | tf_op jit(solution)/shard_map/ppermute | solution.py:284
  120.2 4.2 %shard_map.77 = f32[328,640]{1,0:T(8,128)S(1)} custom-call(s32[16]{0:T(128)S(1)} %stack.48.ids_ref, f32[320,640]{1,0:T(8,128)S(1)} %get-tuple-element.46.refs_0_, f32[1,640]{1,0:T(1,128)S(1)} %broadcast_in_dim.2.refs_5_.refs_1_, bf16[4,320,960]{2,1,0:T(8,128)(2,1)S(1)} %get-tuple-element.31.refs_4_.refs_5_.refs_2_, ...), custom_call_target="tpu_custom_call" | custom-call | tf_op jit(solution)/shard_map/pallas_call | solution.py:54
  124.5 4.3 %shard_map.76.refs_1_ = f32[328,640]{1,0:T(8,128)S(1)} custom-call(s32[16]{0:T(128)S(1)} %stack.48.ids_ref, f32[320,640]{1,0:T(8,128)S(1)} %get-tuple-element.43.refs_0_, f32[1,640]{1,0:T(1,128)S(1)} %broadcast_in_dim.2.refs_5_.refs_1_, bf16[4,320,960]{2,1,0:T(8,128)(2,1)S(1)} %get-tuple-element.30.refs_3_.refs_4_.refs_2_, ...), custom_call_target="tpu_custom_call" | custom-call | tf_op jit(solution)/shard_map/pallas_call | solution.py:54
  128.8 3.4 %collective-permute-start.13 = (f32[8,320]{1,0:T(8,128)S(1)}, f32[8,320]{1,0:T(8,128)S(1)}, u32[]{:S(2)}, u32[]{:S(2)}) collective-permute-start(f32[8,320]{1,0:T(8,128)S(1)} %slice_add_fusion), channel_id=1, source_target_pairs={{0,8},{1,9},{2,10},{3,11},{4,12},{5,13},{6,14},{7,15},{8,0},{9,1},... | collective-permute-start | bytes 30728 | tf_op jit(solution)/shard_map/ppermute | solution.py:284
  132.1 1.7 %collective-permute-done.13 = f32[8,320]{1,0:T(8,128)S(1)} collective-permute-done((f32[8,320]{1,0:T(8,128)S(1)}, f32[8,320]{1,0:T(8,128)S(1)}, u32[]{:S(2)}, u32[]{:S(2)}) %collective-permute-start.13) | collective-permute-done | bytes 10272 | tf_op jit(solution)/shard_map/ppermute | solution.py:284
  134.9 2.2 %shard_map.78 = f32[320,640]{1,0:T(8,128)} custom-call(s32[16]{0:T(128)S(1)} %stack.48.ids_ref, f32[320,640]{1,0:T(8,128)S(1)} %get-tuple-element.37.refs_0_, f32[328,640]{1,0:T(8,128)S(1)} %shard_map.76.refs_1_, f32[328,640]{1,0:T(8,128)S(1)} %collective-permute-done.12.refs_2_, f32[8,128]{1,0:T(8,128)S(1)} %get-tuple-element.36.refs_3_), custom_call_target="tpu_custom_call" | custom-call | tf_op jit(solution)/shard_map/pallas_call | solution.py:54
  (46 shorter events, 17.9 us)
Async XLA Ops:
  1.4 1.1 copy-start.4
  3.0 3.2 %collective-permute-start = (f32[328,320]{1,0:T(8,128)S(1)}, f32[328,320]{1,0:T(8,128)S(1)}, u32[]{:S(2)}, u32[]{:S(2)}) collective-permute-start(f32[328,320]{1,0:T(8,128)S(1)} %get-tuple-element.27), channel_id=1, source_target_pairs={{0,1},{1,0},{2,3},{3,2},{4,5},{5,4},{6,7},{7,6},{8,9},{9,8},{10,11... | collective-permute-start | bytes 1259528 | tf_op jit(solution)/shard_map/ppermute | solution.py:287
  3.5 24.0 %collective-permute-start.4 = (f32[328,640]{1,0:T(8,128)S(1)}, f32[328,640]{1,0:T(8,128)S(1)}, u32[]{:S(2)}, u32[]{:S(2)}) collective-permute-start(f32[328,640]{1,0:T(8,128)S(1)} %get-tuple-element.28.refs_0_), channel_id=1, source_target_pairs={{0,2},{1,3},{2,4},{3,5},{4,6},{5,7},{6,0},{7,1},{8,10},{9,11},{10,... | collective-permute-start | bytes 2519048 | tf_op jit(solution)/shard_map/ppermute | solution.py:284
  6.2 0.8 copy-start.5
  8.1 20.5 %collective-permute-start.2 = (f32[320,640]{1,0:T(8,128)}, f32[320,640]{1,0:T(8,128)S(1)}, u32[]{:S(2)}, u32[]{:S(2)}) collective-permute-start(f32[320,640]{1,0:T(8,128)} %pad_maximum_fusion.refs_0_), channel_id=1, source_target_pairs={{0,16},{1,17},{2,18},{3,19},{4,20},{5,21},{6,22},{7,23},{8,24},{9,... | collective-permute-start | bytes 2457608 | tf_op jit(solution)/shard_map/ppermute | solution.py:284
  9.8 20.2 %collective-permute-start.1 = (f32[320,640]{1,0:T(8,128)}, f32[320,640]{1,0:T(8,128)S(1)}, u32[]{:S(2)}, u32[]{:S(2)}) collective-permute-start(f32[320,640]{1,0:T(8,128)} %pad_maximum_fusion.refs_0_), channel_id=1, source_target_pairs={{0,8},{1,9},{2,10},{3,11},{4,12},{5,13},{6,14},{7,15},{8,0},{9,1},... | collective-permute-start | bytes 2457608 | tf_op jit(solution)/shard_map/ppermute | solution.py:284
  27.5 32.4 %collective-permute-start.5 = (f32[328,640]{1,0:T(8,128)S(1)}, f32[328,640]{1,0:T(8,128)S(1)}, u32[]{:S(2)}, u32[]{:S(2)}) collective-permute-start(f32[328,640]{1,0:T(8,128)S(1)} %collective-permute-done.4.refs_1_), channel_id=1, source_target_pairs={{0,2},{1,3},{2,4},{3,5},{4,6},{5,7},{6,0},{7,1},{8,10},{9,11},{10,... | collective-permute-start | bytes 2519048 | tf_op jit(solution)/shard_map/ppermute | solution.py:284
  28.6 0.9 copy-start
  30.0 0.9 copy-start.2
  30.9 36.8 %collective-permute-start.3 = (f32[328,640]{1,0:T(8,128)S(1)}, f32[328,640]{1,0:T(8,128)S(1)}, u32[]{:S(2)}, u32[]{:S(2)}) collective-permute-start(f32[328,640]{1,0:T(8,128)S(1)} %get-tuple-element.28.refs_0_), channel_id=1, source_target_pairs={{0,6},{1,7},{2,0},{3,1},{4,2},{5,3},{6,4},{7,5},{8,14},{9,15},{10,... | collective-permute-start | bytes 2519048 | tf_op jit(solution)/shard_map/ppermute | solution.py:284
  34.5 20.1 %collective-permute-start.6 = (f32[320,640]{1,0:T(8,128)}, f32[320,640]{1,0:T(8,128)}, u32[]{:S(2)}, u32[]{:S(2)}) collective-permute-start(f32[320,640]{1,0:T(8,128)} %pad_maximum_fusion.refs_0_), channel_id=1, source_target_pairs={{0,24},{1,25},{2,26},{3,27},{4,28},{5,29},{6,30},{7,31},{8,16},{9,... | collective-permute-start | bytes 2457608 | tf_op jit(solution)/shard_map/ppermute | solution.py:284
  54.6 1.1 copy-start.1
  55.8 1.1 copy-start.3
  67.7 2.6 %copy-start.6 = (f32[640]{0:T(1024)S(1)}, f32[640]{0:T(1024)}, u32[]{:S(2)}) copy-start(f32[640]{0:T(1024)} %param.7) | copy-start | bytes 7684
  70.3 5.0 %collective-permute-start.7 = (f32[320,960]{1,0:T(8,128)S(1)}, f32[320,960]{1,0:T(8,128)S(1)}, u32[]{:S(2)}, u32[]{:S(2)}) collective-permute-start(f32[320,960]{1,0:T(8,128)S(1)} %get-tuple-element.35.refs_1_), channel_id=1, source_target_pairs={{0,1},{1,0},{2,3},{3,2},{4,5},{5,4},{6,7},{7,6},{8,9},{9,8},{10,11... | collective-permute-start | bytes 3686408 | tf_op jit(solution)/shard_map/ppermute | solution.py:287
  80.0 4.4 %collective-permute-start.8 = (f32[320,640]{1,0:T(8,128)S(1)}, f32[320,640]{1,0:T(8,128)S(1)}, u32[]{:S(2)}, u32[]{:S(2)}) collective-permute-start(f32[320,640]{1,0:T(8,128)S(1)} %get-tuple-element.41), channel_id=1, source_target_pairs={{0,1},{1,0},{2,3},{3,2},{4,5},{5,4},{6,7},{7,6},{8,9},{9,8},{10,11... | collective-permute-start | bytes 2457608 | tf_op jit(solution)/shard_map/ppermute | solution.py:287
  80.5 39.6 %collective-permute-start.10 = (f32[320,640]{1,0:T(8,128)S(1)}, f32[320,640]{1,0:T(8,128)S(1)}, u32[]{:S(2)}, u32[]{:S(2)}) collective-permute-start(f32[320,640]{1,0:T(8,128)S(1)} %get-tuple-element.44), channel_id=1, source_target_pairs={{2,6},{3,7},{4,2},{5,3},{6,4},{7,5},{8,12},{9,13},{12,20},{13,21},... | collective-permute-start | bytes 2457608 | tf_op jit(solution)/shard_map/ppermute | solution.py:284
  81.8 38.3 %collective-permute-start.11 = (f32[320,640]{1,0:T(8,128)S(1)}, f32[320,640]{1,0:T(8,128)S(1)}, u32[]{:S(2)}, u32[]{:S(2)}) collective-permute-start(f32[320,640]{1,0:T(8,128)S(1)} %get-tuple-element.45), channel_id=1, source_target_pairs={{2,4},{3,5},{4,6},{5,7},{6,2},{7,3},{8,14},{9,15},{12,8},{13,9},{1... | collective-permute-start | bytes 2457608 | tf_op jit(solution)/shard_map/ppermute | solution.py:284
  83.1 37.0 %collective-permute-start.9 = (f32[320,640]{1,0:T(8,128)S(1)}, f32[320,640]{1,0:T(8,128)S(1)}, u32[]{:S(2)}, u32[]{:S(2)}) collective-permute-start(f32[320,640]{1,0:T(8,128)S(1)} %get-tuple-element.38), channel_id=1, source_target_pairs={{2,10},{3,11},{4,20},{5,21},{6,30},{7,31},{8,0},{9,1},{12,14},{13,... | collective-permute-start | bytes 2457608 | tf_op jit(solution)/shard_map/ppermute | solution.py:284
  124.4 4.3 %collective-permute-start.12 = (f32[328,640]{1,0:T(8,128)S(1)}, f32[328,640]{1,0:T(8,128)S(1)}, u32[]{:S(2)}, u32[]{:S(2)}) collective-permute-start(f32[328,640]{1,0:T(8,128)S(1)} %shard_map.77), channel_id=1, source_target_pairs={{0,1},{1,0},{2,3},{3,2},{4,5},{5,4},{6,7},{7,6},{8,9},{9,8},{10,11... | collective-permute-start | bytes 2519048 | tf_op jit(solution)/shard_map/ppermute | solution.py:287
  128.8 5.0 %collective-permute-start.13 = (f32[8,320]{1,0:T(8,128)S(1)}, f32[8,320]{1,0:T(8,128)S(1)}, u32[]{:S(2)}, u32[]{:S(2)}) collective-permute-start(f32[8,320]{1,0:T(8,128)S(1)} %slice_add_fusion), channel_id=1, source_target_pairs={{0,8},{1,9},{2,10},{3,11},{4,12},{5,13},{6,14},{7,15},{8,0},{9,1},... | collective-permute-start | bytes 30728 | tf_op jit(solution)/shard_map/ppermute | solution.py:284
  133.8 3.7 %collective-permute-start.14 = (f32[8,320]{1,0:T(8,128)S(1)}, f32[8,320]{1,0:T(8,128)S(1)}, u32[]{:S(2)}, u32[]{:S(2)}) collective-permute-start(f32[8,320]{1,0:T(8,128)S(1)} %add.53), channel_id=1, source_target_pairs={{0,16},{1,17},{2,18},{3,19},{4,20},{5,21},{6,22},{7,23},{8,24},{9,... | collective-permute-start | bytes 30728 | tf_op jit(solution)/shard_map/ppermute | solution.py:284

commit v4 on v3

--- a/solution.py
+++ b/solution.py
@@ -37,14 +37,24 @@
 
 
 def call(kernel, outs, ids, *arrays, placed=0, scratch=()):
-    copied = len(arrays) - placed
-    held = [pltpu.VMEM(a.shape, a.dtype) for a in arrays[:copied]]
+    pieces, held, homes = [], [], []
+    for array in arrays[: len(arrays) - placed]:
+        array = array if isinstance(array, list) else [array]
+        rows = [a.shape[0] for a in array]
+        homes += [(len(held), sum(rows[:i]), n, len(array) > 1) for i, n in enumerate(rows)]
+        held.append(pltpu.VMEM((sum(rows), *array[0].shape[1:]), array[0].dtype))
+        pieces += array
+    arrays = pieces + list(arrays[len(arrays) - placed :])
+    copied = len(pieces)
     n_outs = len(jax.tree.leaves(outs))
 
     def body(ids_ref, *refs):
         sources, rest, own = refs[:copied], refs[copied : len(arrays) + n_outs], refs[len(arrays) + n_outs :]
-        targets, sems, own = own[:copied], own[copied], own[copied + 1 :]
-        copies = [pltpu.make_async_copy(a, b, sems.at[i]) for i, (a, b) in enumerate(zip(sources, targets))]
+        targets, sems, own = own[: len(held)], own[len(held)], own[len(held) + 1 :]
+        copies = []
+        for i, (source, (home, start, n, part)) in enumerate(zip(sources, homes)):
+            target = targets[home].at[start : start + n] if part else targets[home]
+            copies.append(pltpu.make_async_copy(source, target, sems.at[i]))
         for copy in copies:
             copy.start()
         for copy in copies:
@@ -86,7 +96,7 @@
 
 
 def pack_kernel(core, tile, pattern, packed, mine, other, blocks):
-    half, (high, wide) = tile.shape[0], pattern.shape
+    half, (wide, high) = tile.shape[0], pattern.shape
     packed[:half, :] = tile[...]
     packed[half:, :] = jnp.zeros((ROWS, tile.shape[1]), jnp.float32)
 
@@ -94,8 +104,8 @@
         same = lax.broadcasted_iota(jnp.int32, (rows, columns), 0) == lax.broadcasted_iota(jnp.int32, (rows, columns), 1)
         return same.astype(jnp.bfloat16)
 
-    turned = dot(unit(ROWS, wide), pattern[...].astype(jnp.float32).astype(jnp.bfloat16), ROW_BY_ROW)
-    blocks[...] = dot(turned.astype(jnp.bfloat16), unit(high, LANES))
+    rows = dot(unit(ROWS, wide), pattern[...].astype(jnp.float32).astype(jnp.bfloat16))
+    blocks[...] = dot(rows.astype(jnp.bfloat16), unit(high, LANES))
     packed[half:, :LANES] = blocks[...]
     mine[...] = in_half(tile[...], core[0])
     other[:half, :] = in_half(tile[...], 1 - core[0])
@@ -152,15 +162,14 @@
     given[:, height:] = in_half(kept_sum, 1 - ids[CORE])
 
 
-def square_kernel(ids, kept, given, received, blocks, their_blocks, weights, *outs):
+def square_kernel(ids, kept, given, received, blocks, theirs, *refs):
     half, height = kept.shape
-    square, sums, outs = outs[0], outs[1], outs[2:]
-    product = kept[...] + received[:, :height]
-    square[...] = product * spread(blocks[...], half, height)
-    row = first(jnp.broadcast_to(weights[...], (ROWS, height)), 1)
-    sums[...] = jnp.zeros_like(sums)
-    sums[0:1, :] = dot(row, second(product, 1), ROW_BY_ROW)[0:1, :]
+    square, outs, (their_blocks, sem) = refs[0], refs[1:-2], refs[-2:]
+    copy = pltpu.make_async_copy(theirs.at[half:, :LANES], their_blocks, sem)
+    copy.start()
+    square[...] = (kept[...] + received[:, :height]) * spread(blocks[...], half, height)
     other = in_half(given[:, :height], ids[CORE]) + received[:, height:]
+    copy.wait()
     other = (other * in_half(spread(their_blocks[...], half, height), ids[CORE])).T
     own = in_half(square[...], ids[CORE]).T
     for step, out in enumerate(outs):
@@ -175,8 +184,22 @@
             out[:, half:] = jnp.where(ids[CORE] == 0, other, own)
 
 
-def last_kernel(count, place, ids, start, weights, right, *refs):
-    sources, out, held, held_sems, tiles, sems = refs[:count], *refs[count:]
+def check_sums(weights, value):
+    column = jnp.sum(value * weights[...], axis=1, keepdims=True)
+    return jnp.broadcast_to(column, (value.shape[0], LANES)).T[:ROWS, :]
+
+
+def in_row(value, row):
+    return jnp.where(lax.broadcasted_iota(jnp.int32, value.shape, 0) == row, value, 0.0)
+
+
+def last_kernel(count, place, is_kept, ids, start, weights, *refs):
+    if is_kept:
+        square, blocks, *refs = refs
+    right, *refs = refs
+    if not is_kept:
+        theirs, *refs = refs
+    sources, out, held, held_sems, tiles, sems, *refs = refs[:count], *refs[count:]
     half, height = start.shape
 
     def copies(t):
@@ -184,6 +207,11 @@
         yield pltpu.make_async_copy(right.at[k], held.at[t], held_sems.at[t])
         yield pltpu.make_async_copy(sources[t], tiles.at[t], sems.at[t])
 
+    if not is_kept:
+        blocks, sem = refs
+        copy = pltpu.make_async_copy(theirs.at[half:, :LANES], blocks, sem)
+        copy.start()
+        copy.wait()
     for t in range(count):
         for copy in copies(t):
             copy.start()
@@ -196,9 +224,10 @@
         def _():
             out[:half, :] += dot(held[t], second(tiles[t], 0))
 
-    row = first(jnp.broadcast_to(weights[...], (ROWS, height)), 1)
     out[half:, :] = jnp.zeros((ROWS, height), jnp.float32)
-    out[half + 1 : half + 2, :half] = dot(row, second(out[:half, :], 1), ROW_BY_ROW)[1:2, :]
+    out[half:, :half] = in_row(check_sums(weights, out[:half, :]), 1)
+    cube_term = spread(blocks[...], half, height) * out[:half, :]
+    out[:half, :] = 3.0 * square[...] - 2.0 * cube_term if is_kept else -2.0 * cube_term
 
 
 def diagonal_early_kernel(ids, *refs):
@@ -209,34 +238,34 @@
         out[...] = term if j == 0 else out[...] + term
 
 
-def diagonal_kernel(last, ids, start, left, *refs):
-    patterns, (given, kept, blocks, whole) = refs[:-4], refs[-4:]
+def diagonal_kernel(ids, start, left, *refs):
+    tiles, (given, kept, blocks, whole, held, sem) = refs[:-6], refs[-6:]
     half = given.shape[0]
+    held[...] = jnp.zeros_like(held)
+    for j, source in enumerate(tiles):
+
+        @pl.when(ids[BACK] == j + 1)
+        def _():
+            copy = pltpu.make_async_copy(source.at[half:, :LANES], held, sem)
+            copy.start()
+            copy.wait()
+
+    blocks[...] = held[...]
     tile = left[:half, :]
     whole[...] = start[...] + dot(first(tile, 0), second(tile, 0), COLUMN_BY_COLUMN)
     given[...] = whole[pl.ds(pl.multiple_of((1 - ids[CORE]) * half, half), half), :]
     kept[...] = whole[pl.ds(pl.multiple_of(ids[CORE] * half, half), half), :]
-    blocks[...] = jnp.zeros_like(blocks)
-    for j, pattern in enumerate(patterns):
-
-        @pl.when(ids[BACK] == j + 1)
-        def _():
-            blocks[...] = pattern[...]
-
-
-def early_kernel(ids, square, kept, received, blocks, *refs):
-    rights, outs, (held, sems) = refs[:2], refs[2:4], refs[4:]
+
+
+def early_kernel(ids, square, kept, received, blocks, kept_sum, received_sum, weights, *refs):
+    rights, outs, (sums, held, sems) = refs[:2], refs[2:4], refs[4:]
+    height = square.shape[1]
     fetch([right.at[place] for right in rights for place in (ids[COLUMN], ids[ROW])], held, sems)
     own = second(square[...], 0)
     diagonal = second((kept[...] + received[...]) * spread(blocks[...], *kept.shape), 0)
     for s, out in enumerate(outs):
         out[...] = dot(held[2 * s], own) + dot(held[2 * s + 1], diagonal)
-
-
-def purify_kernel(ids, square, kept, received, blocks, out):
-    half, height = square.shape
-    cube = kept[:half, :] + received[:half, :]
-    out[...] = 3.0 * square[...] - 2.0 * (spread(blocks[...], half, height) * cube)
+    sums[...] = in_row(check_sums(weights, kept_sum[...] + received_sum[:, :height]), 0)
 
 
 def in_steps(edges):
@@ -315,21 +344,19 @@
             [shape(half + ROWS, height), shape(half, half), shape(half + ROWS, half), shape(ROWS, LANES)],
             jnp.asarray(core, jnp.int32)[None],
             tile,
-            pattern,
+            pattern.T,
         )
         left = {0: packed, 1: send(packed, ring(1))}
         theirs = swap_core(other)
         own = jnp.concatenate([mine, theirs[:half]], axis=1)
-        their_blocks = theirs[half:, :LANES]
         tiles = {m: send(own, across(m)) for m in powers}
-        nearest = [tiles[m] for m in powers]
-        own_later = after(own, *nearest)
+        own_later = after(own, *[tiles[m] for m in powers])
         tiles = [own] + [tiles[m] if m in powers else send(own_later, across(m)) for m in range(1, panels)]
         last = panels // 2 + 1
         for j in range(2, last):
             left[j] = send(left[j - 1], ring(1))
         for j in range(panels - 1, last - 1, -1):
-            left[j] = send(after(packed, *nearest) if j == panels - 1 else left[j + 1], ring(-1))
+            left[j] = send(after(packed, own) if j == panels - 1 else left[j + 1], ring(-1))
 
         part = shape(panels, half, 3 * half, dtype=jnp.bfloat16)
         kept, given = call(split_kernel, [part] * 2, ids, *tiles)
@@ -351,42 +378,53 @@
             [shape(half, height), shape(half, height + half)],
             ids,
             left[last],
-            *starts,
+            after(starts[0], diagonal_start),
+            starts[1],
             kept,
             given,
             placed=2,
             scratch=held_parts(2, half),
         )
-        square, sums, *rows = call(
+        diagonal_given, diagonal_kept, diagonal_blocks = call(
+            diagonal_kernel,
+            [shape(half, height)] * 2 + [shape(ROWS, LANES)],
+            ids,
+            diagonal_start,
+            left[last],
+            *[left[j] for j in range(1, panels)],
+            placed=panels - 1,
+            scratch=[
+                pltpu.VMEM((height, height), jnp.float32),
+                pltpu.VMEM((ROWS, LANES), jnp.float32),
+                pltpu.SemaphoreType.DMA,
+            ],
+        )
+        received = swap_core(given_sum)
+        square, *rows = call(
             square_kernel,
-            [shape(half, height), shape(ROWS, half)] + [shape(half, height)] * steps,
-            ids,
-            kept_sum,
+            [shape(half, height)] * (1 + steps),
+            ids,
+            after(kept_sum, diagonal_given),
             given_sum,
-            swap_core(given_sum),
+            received,
             blocks,
-            their_blocks,
-            weights[None, :],
+            theirs,
+            placed=1,
+            scratch=[pltpu.VMEM((ROWS, LANES), jnp.float32), pltpu.SemaphoreType.DMA],
         )
 
         arrived = [send(rows[step], functools.partial(step_target, step)) for step in range(steps)]
-        diagonal_given, diagonal_kept, diagonal_blocks = call(
-            functools.partial(diagonal_kernel, last),
-            [shape(half, height)] * 2 + [shape(ROWS, LANES)],
-            ids,
-            after(diagonal_start, rows[0]),
-            left[last],
-            *[left[j][half:, :LANES] for j in range(1, panels)],
-            scratch=[pltpu.VMEM((2 * half, height), jnp.float32)],
-        )
-        cube = call(
+        *cube, sums = call(
             early_kernel,
-            [shape(half, height)] * 2,
+            [shape(half, height)] * 2 + [shape(ROWS, half)],
             ids,
             square,
             diagonal_kept,
             swap_core(diagonal_given),
             diagonal_blocks,
+            kept_sum,
+            received,
+            weights[None, :],
             kept,
             given,
             placed=2,
@@ -395,20 +433,39 @@
 
         held = [pltpu.VMEM((steps, half, height), jnp.float32), pltpu.SemaphoreType.DMA((steps,))]
 
-        def finish(side, start):
-            kernel = functools.partial(last_kernel, steps, steps_at)
-            scratch = held_parts(steps, half) + held
-            arrays = [start, weights[None, :], side, *arrived]
-            return call(kernel, shape(half + ROWS, height), ids, *arrays, placed=steps + 1, scratch=scratch)
-
-        given_cube = finish(given, cube[1])
-        kept_cube = finish(kept, cube[0])
+        kernel = functools.partial(last_kernel, steps, steps_at)
+        out = shape(half + ROWS, height)
+        scratch = held_parts(steps, half) + held
+        given_cube = call(
+            functools.partial(kernel, False),
+            out,
+            ids,
+            cube[1],
+            weights[None, :],
+            given,
+            theirs,
+            *arrived,
+            placed=steps + 2,
+            scratch=scratch + [pltpu.VMEM((ROWS, LANES), jnp.float32), pltpu.SemaphoreType.DMA],
+        )
+        kept_cube = call(
+            functools.partial(kernel, True),
+            out,
+            ids,
+            cube[0],
+            weights[None, :],
+            square,
+            blocks,
+            kept,
+            *arrived,
+            placed=steps + 1,
+            scratch=scratch,
+        )
         received = swap_core(given_cube)
         sums = sums + kept_cube[half:, :half] + received[half:, :half]
         for m in powers:
             sums = sums + send(sums, across(m))
-        purified = call(purify_kernel, shape(half, height), ids, square, kept_cube, received, blocks)
-        return purified.T, sums[:2]
+        return (kept_cube[:half] + received[:half]).T, sums[:2]
 
     return body
 

time: 139 us -> 134 us (0.964)
  local copies, waits for them, and re-layouts: 12.8 us -> 8.93 us
  starting transfers between devices: 21.1 us -> 17.6 us
    ppermute x11, starting transfers between devices: 19.9 us -> 16.4 us  [send(): return lax.ppermute(value, ('row', 'col'), pairs)]
    unnamed x15 -> x14, local copies, waits for them, and re-layouts: 6.82 us -> 3.66 us
    pallas_call x11 -> x10, Pallas kernels: 35.2 us -> 35.7 us  [call(): pl.pallas_call(body, out_shape=outs, in_specs=[pl.BlockSpec(memory_space=...]
  transfers between devices with their start and end apart: 15 -> 15, of which waited for: 8 -> 8; matrix products, arithmetic and copies ran while one was open for 5% -> 6% of each run, Pallas kernels for 17% -> 21%
where the time goes in v4:
time: 134 us; the launch traced here: 133 us
  waiting for transfers between devices  67.7 us (51%)
  Pallas kernels  35.7 us (27%)
  starting transfers between devices  17.6 us (13%)
  local copies, waits for them, and re-layouts  8.93 us (7%)
  other arithmetic  2.68 us (2%)
    ppermute x11, waiting for transfers between devices, send(): return lax.ppermute(value, ('row', 'col'), pairs)  67.4 us
    pallas_call x10, Pallas kernels, call(): pl.pallas_call(body, out_shape=outs, in_specs=[pl.BlockSpec(memory_space=...  35.7 us
    ppermute x11, starting transfers between devices, send(): return lax.ppermute(value, ('row', 'col'), pairs)  16.4 us
    unnamed x14, local copies, waits for them, and re-layouts  3.66 us
  transfers between devices with their start and end apart: 15, of which 8 were waited for; matrix products, arithmetic and copies ran while one was open for 6% of the time, Pallas kernels for 21%

profile of v4, /device:TPU:0, one launch (start us, length us, event | category | flops | bytes accessed | tf_op | source)
XLA Modules:
  0.0 133.4 jit_solution(2772618208360020716)
XLA Ops:
  2.5 1.3 shard_map.68
  4.3 2.6 %collective-permute-start.2 = (f32[328,640]{1,0:T(8,128)}, f32[328,640]{1,0:T(8,128)S(1)}, u32[]{:S(2)}, u32[]{:S(2)}) collective-permute-start(f32[328,640]{1,0:T(8,128)} %get-tuple-element.29.refs_0_), channel_id=1, source_target_pairs={{0,2},{1,3},{2,4},{3,5},{4,6},{5,7},{6,0},{7,1},{8,10},{9,11},{10,... | collective-permute-start | bytes 2519048 | tf_op jit(solution)/shard_map/ppermute | solution.py:313
  8.1 1.7 %collective-permute-start.4 = (f32[320,640]{1,0:T(8,128)}, f32[320,640]{1,0:T(8,128)S(1)}, u32[]{:S(2)}, u32[]{:S(2)}) collective-permute-start(f32[320,640]{1,0:T(8,128)} %pad_maximum_fusion.refs_0_), channel_id=1, source_target_pairs={{0,8},{1,9},{2,10},{3,11},{4,12},{5,13},{6,14},{7,15},{8,0},{9,1},... | collective-permute-start | bytes 2457608 | tf_op jit(solution)/shard_map/ppermute | solution.py:313
  9.8 1.5 %collective-permute-start.5 = (f32[320,640]{1,0:T(8,128)}, f32[320,640]{1,0:T(8,128)S(1)}, u32[]{:S(2)}, u32[]{:S(2)}) collective-permute-start(f32[320,640]{1,0:T(8,128)} %pad_maximum_fusion.refs_0_), channel_id=1, source_target_pairs={{0,16},{1,17},{2,18},{3,19},{4,20},{5,21},{6,22},{7,23},{8,24},{9,... | collective-permute-start | bytes 2457608 | tf_op jit(solution)/shard_map/ppermute | solution.py:313
  11.3 17.1 %collective-permute-done.2.refs_1_.refs_2_ = f32[328,640]{1,0:T(8,128)S(1)} collective-permute-done((f32[328,640]{1,0:T(8,128)}, f32[328,640]{1,0:T(8,128)S(1)}, u32[]{:S(2)}, u32[]{:S(2)}) %collective-permute-start.2) | collective-permute-done | bytes 839712 | tf_op jit(solution)/shard_map/ppermute | solution.py:313
  28.5 3.8 %collective-permute-start.1 = (f32[328,640]{1,0:T(8,128)}, f32[328,640]{1,0:T(8,128)S(1)}, u32[]{:S(2)}, u32[]{:S(2)}) collective-permute-start(f32[328,640]{1,0:T(8,128)} %get-tuple-element.29.refs_0_), channel_id=1, source_target_pairs={{0,6},{1,7},{2,0},{3,1},{4,2},{5,3},{6,4},{7,5},{8,14},{9,15},{10,... | collective-permute-start | bytes 2519048 | tf_op jit(solution)/shard_map/ppermute | solution.py:313
  34.1 2.4 %collective-permute-start.6 = (f32[320,640]{1,0:T(8,128)}, f32[320,640]{1,0:T(8,128)}, u32[]{:S(2)}, u32[]{:S(2)}) collective-permute-start(f32[320,640]{1,0:T(8,128)} %pad_maximum_fusion.refs_0_), channel_id=1, source_target_pairs={{0,24},{1,25},{2,26},{3,27},{4,28},{5,29},{6,30},{7,31},{8,16},{9,... | collective-permute-start | bytes 2457608 | tf_op jit(solution)/shard_map/ppermute | solution.py:313
  36.6 1.3 %dynamic_slice.6 = s32[1,1]{1,0:T(1,128)} dynamic-slice(s32[4,4]{1,0:T(4,128)} %constant.70.clone, s32[]{:T(128)S(6)} %select_n.40, s32[]{:T(128)S(6)} %select_n.42), dynamic_slice_sizes={1,1} | dynamic-slice | bytes 12 | tf_op jit(solution)/shard_map/dynamic_slice | solution.py:336
  39.3 2.6 %stack.48.ids_ref = s32[16]{0:T(128)S(1)} concatenate(s32[1]{0:T(128)} %bitcast.ids_ref, s32[1]{0:T(128)} %bitcast.1, s32[1]{0:T(128)} %bitcast.2, s32[1]{0:T(128)} %bitcast.3, s32[1]{0:T(128)} %bitcast.4, s32[1]{0:T(128)} %bitcast.2, s32[1]{0:T(128)} %bitcast.5, s32[1]{0:T(128)} %bitcast.6, s32[1]{0:T(128)} %bitcast.7, s32[1]{0:T(128)} %bitcast.8, s32[1]{0:T(128)} %bitcast.9, ...), dimensions={0} | concatenate | bytes 128 | tf_op jit(solution)/shard_map/stack | solution.py:339
  41.8 10.0 %collective-permute-done.3.refs_2_.refs_3_ = f32[328,640]{1,0:T(8,128)S(1)} collective-permute-done((f32[328,640]{1,0:T(8,128)S(1)}, f32[328,640]{1,0:T(8,128)S(1)}, u32[]{:S(2)}, u32[]{:S(2)}) %collective-permute-start.3) | collective-permute-done | bytes 839712 | tf_op jit(solution)/shard_map/ppermute | solution.py:313
  51.8 5.0 %shard_map.71.refs_0_ = f32[640,640]{1,0:T(8,128)S(1)} custom-call(s32[16]{0:T(128)S(1)} %stack.48.ids_ref, f32[328,640]{1,0:T(8,128)} %get-tuple-element.29.refs_0_, f32[328,640]{1,0:T(8,128)S(1)} %collective-permute-done.2.refs_1_.refs_2_, f32[328,640]{1,0:T(8,128)S(1)} %collective-permute-done.3.refs_2_.refs_3_), custom_call_target="tpu_custom_call" | custom-call | tf_op jit(solution)/shard_map/pallas_call | solution.py:64
  56.9 2.9 %shard_map.69 = (bf16[4,320,960]{2,1,0:T(8,128)(2,1)S(1)}, bf16[4,320,960]{2,1,0:T(8,128)(2,1)S(1)}) custom-call(s32[16]{0:T(128)S(1)} %stack.48.ids_ref, f32[320,640]{1,0:T(8,128)} %pad_maximum_fusion.refs_0_, f32[320,640]{1,0:T(8,128)S(1)} %copy-done.1, f32[320,640]{1,0:T(8,128)S(1)} %copy-done.3, f32[320,640]{1,0:T(8,128)} %collective-permute-done.6.refs_3_), custom_call_target="tpu_custom_call" | custom-call | tf_op jit(solution)/shard_map/pallas_call | solution.py:64
  59.8 6.2 %shard_map.70 = (f32[320,640]{1,0:T(8,128)S(1)}, f32[320,640]{1,0:T(8,128)S(1)}) custom-call(s32[16]{0:T(128)S(1)} %stack.48.ids_ref, f32[328,640]{1,0:T(8,128)} %get-tuple-element.29.refs_0_, f32[328,640]{1,0:T(8,128)S(1)} %collective-permute-done.2.refs_1_.refs_2_, f32[328,640]{1,0:T(8,128)S(1)} %collective-permute-done.3.refs_2_.refs_3_, ...), custom_call_target="tpu_custom_call" | custom-call | tf_op jit(solution)/shard_map/pallas_call | solution.py:64
  67.1 2.5 %shard_map.72 = (f32[320,640]{1,0:T(8,128)S(1)}, f32[320,960]{1,0:T(8,128)S(1)}) custom-call(s32[16]{0:T(128)S(1)} %stack.48.ids_ref, f32[328,640]{1,0:T(8,128)S(1)} %collective-permute-done.1.refs_0_.refs_1_.refs_4_, f32[320,640]{1,0:T(8,128)S(1)} %get-tuple-element.34.refs_1_, f32[320,640]{1,0:T(8,128)S(1)} %get-tuple-element.35.refs_2_, ...), custom_call_target="tpu_custom_call" | custom-call | tf_op jit(solution)/shard_map/pallas_call | solution.py:64
  69.8 2.2 %shard_map.73 = (f32[320,640]{1,0:T(8,128)S(1)}, f32[320,640]{1,0:T(8,128)S(1)}, f32[8,128]{1,0:T(8,128)S(1)}) custom-call(s32[16]{0:T(128)S(1)} %stack.48.ids_ref, f32[640,640]{1,0:T(8,128)S(1)} %shard_map.71.refs_0_, f32[328,640]{1,0:T(8,128)S(1)} %collective-permute-done.1.refs_0_.refs_1_.refs_4_, f32[328,640]{1,0:T(8,128)S(1)} %collective-permute-done.2.refs_1_.refs_2_, ...), custom_call_target="tpu_custom_call" | custom-call | tf_op jit(solution)/shard_map/pallas_call | solution.py:64
  72.8 2.4 %shard_map.74 = (f32[320,640]{1,0:T(8,128)S(1)}, f32[320,640]{1,0:T(8,128)S(1)}, f32[320,640]{1,0:T(8,128)S(1)}, f32[320,640]{1,0:T(8,128)S(1)}) custom-call(s32[16]{0:T(128)S(1)} %stack.48.ids_ref, f32[320,640]{1,0:T(8,128)S(1)} %get-tuple-element.38.refs_0_.refs_4_, f32[320,960]{1,0:T(8,128)S(1)} %get-tuple-element.39.refs_1_, ...), custom_call_target="tpu_custom_call" | custom-call | tf_op jit(solution)/shard_map/pallas_call | solution.py:64
  75.2 1.3 collective-permute-start.9
  79.2 4.5 %shard_map.75 = (f32[320,640]{1,0:T(8,128)S(1)}, f32[320,640]{1,0:T(8,128)S(1)}, f32[8,320]{1,0:T(8,128)S(1)}) custom-call(s32[16]{0:T(128)S(1)} %stack.48.ids_ref, f32[320,640]{1,0:T(8,128)S(1)} %get-tuple-element.41.refs_0_.refs_2_, f32[320,640]{1,0:T(8,128)S(1)} %get-tuple-element.42.refs_1_, f32[320,640]{1,0:T(8,128)S(1)} %collective-permute-done.8.refs_2_, ...), custom_call_target="tpu_custom_call" | custom-call | tf_op jit(solution)/shard_map/pallas_call | solution.py:64
  83.6 13.8 %collective-permute-done.9.refs_5_.refs_4_ = f32[320,640]{1,0:T(8,128)S(1)} collective-permute-done((f32[320,640]{1,0:T(8,128)S(1)}, f32[320,640]{1,0:T(8,128)S(1)}, u32[]{:S(2)}, u32[]{:S(2)}) %collective-permute-start.9) | collective-permute-done | bytes 819232 | tf_op jit(solution)/shard_map/ppermute | solution.py:313
  97.4 19.3 %collective-permute-done.10.refs_6_.refs_5_ = f32[320,640]{1,0:T(8,128)S(1)} collective-permute-done((f32[320,640]{1,0:T(8,128)S(1)}, f32[320,640]{1,0:T(8,128)S(1)}, u32[]{:S(2)}, u32[]{:S(2)}) %collective-permute-start.10) | collective-permute-done | bytes 819232 | tf_op jit(solution)/shard_map/ppermute | solution.py:313
  116.7 4.2 %shard_map.77 = f32[328,640]{1,0:T(8,128)S(1)} custom-call(s32[16]{0:T(128)S(1)} %stack.48.ids_ref, f32[320,640]{1,0:T(8,128)S(1)} %get-tuple-element.48.refs_0_, f32[1,640]{1,0:T(1,128)S(1)} %broadcast_in_dim.2.refs_6_.refs_1_, bf16[4,320,960]{2,1,0:T(8,128)(2,1)S(1)} %get-tuple-element.32.refs_4_.refs_8_.refs_2_, ...), custom_call_target="tpu_custom_call" | custom-call | tf_op jit(solution)/shard_map/pallas_call | solution.py:64
  121.0 4.4 %shard_map.76 = f32[328,640]{1,0:T(8,128)S(1)} custom-call(s32[16]{0:T(128)S(1)} %stack.48.ids_ref, f32[320,640]{1,0:T(8,128)S(1)} %get-tuple-element.44.refs_0_, f32[1,640]{1,0:T(1,128)S(1)} %broadcast_in_dim.2.refs_6_.refs_1_, f32[320,640]{1,0:T(8,128)S(1)} %get-tuple-element.41.refs_0_.refs_2_, f32[8,128]{1,0:T(8,128)S(1)} %get-tuple-element.40.refs_3_, ...), custom_call_target="tpu_custom_call" | custom-call | tf_op jit(solution)/shard_map/pallas_call | solution.py:64
  125.6 3.6 %collective-permute-done.13 = f32[8,320]{1,0:T(8,128)S(1)} collective-permute-done((f32[8,320]{1,0:T(8,128)S(1)}, f32[8,320]{1,0:T(8,128)S(1)}, u32[]{:S(2)}, u32[]{:S(2)}) %collective-permute-start.13) | collective-permute-done | bytes 10272 | tf_op jit(solution)/shard_map/ppermute | solution.py:313
  130.3 2.5 %collective-permute-done.14 = f32[8,320]{1,0:T(8,128)S(1)} collective-permute-done((f32[8,320]{1,0:T(8,128)S(1)}, f32[8,320]{1,0:T(8,128)S(1)}, u32[]{:S(2)}, u32[]{:S(2)}) %collective-permute-start.14) | collective-permute-done | bytes 10272 | tf_op jit(solution)/shard_map/ppermute | solution.py:313
  (41 shorter events, 13.2 us)
Async XLA Ops:
  0.6 1.1 copy-start.4
  1.8 0.7 copy-start.5
  3.8 3.2 %collective-permute-start = (f32[328,320]{1,0:T(8,128)S(1)}, f32[328,320]{1,0:T(8,128)S(1)}, u32[]{:S(2)}, u32[]{:S(2)}) collective-permute-start(f32[328,320]{1,0:T(8,128)S(1)} %get-tuple-element.28), channel_id=1, source_target_pairs={{0,1},{1,0},{2,3},{3,2},{4,5},{5,4},{6,7},{7,6},{8,9},{9,8},{10,11... | collective-permute-start | bytes 1259528 | tf_op jit(solution)/shard_map/ppermute | solution.py:316
  4.3 24.2 %collective-permute-start.2 = (f32[328,640]{1,0:T(8,128)}, f32[328,640]{1,0:T(8,128)S(1)}, u32[]{:S(2)}, u32[]{:S(2)}) collective-permute-start(f32[328,640]{1,0:T(8,128)} %get-tuple-element.29.refs_0_), channel_id=1, source_target_pairs={{0,2},{1,3},{2,4},{3,5},{4,6},{5,7},{6,0},{7,1},{8,10},{9,11},{10,... | collective-permute-start | bytes 2519048 | tf_op jit(solution)/shard_map/ppermute | solution.py:313
  8.1 24.2 %collective-permute-start.4 = (f32[320,640]{1,0:T(8,128)}, f32[320,640]{1,0:T(8,128)S(1)}, u32[]{:S(2)}, u32[]{:S(2)}) collective-permute-start(f32[320,640]{1,0:T(8,128)} %pad_maximum_fusion.refs_0_), channel_id=1, source_target_pairs={{0,8},{1,9},{2,10},{3,11},{4,12},{5,13},{6,14},{7,15},{8,0},{9,1},... | collective-permute-start | bytes 2457608 | tf_op jit(solution)/shard_map/ppermute | solution.py:313
  9.8 23.4 %collective-permute-start.5 = (f32[320,640]{1,0:T(8,128)}, f32[320,640]{1,0:T(8,128)S(1)}, u32[]{:S(2)}, u32[]{:S(2)}) collective-permute-start(f32[320,640]{1,0:T(8,128)} %pad_maximum_fusion.refs_0_), channel_id=1, source_target_pairs={{0,16},{1,17},{2,18},{3,19},{4,20},{5,21},{6,22},{7,23},{8,24},{9,... | collective-permute-start | bytes 2457608 | tf_op jit(solution)/shard_map/ppermute | solution.py:313
  28.5 23.4 %collective-permute-start.3 = (f32[328,640]{1,0:T(8,128)S(1)}, f32[328,640]{1,0:T(8,128)S(1)}, u32[]{:S(2)}, u32[]{:S(2)}) collective-permute-start(f32[328,640]{1,0:T(8,128)S(1)} %collective-permute-done.2.refs_1_.refs_2_), channel_id=1, source_target_pairs={{0,2},{1,3},{2,4},{3,5},{4,6},{5,7},{6,0},{7,1},{8,10},{9,11},{10,... | collective-permute-start | bytes 2519048 | tf_op jit(solution)/shard_map/ppermute | solution.py:313
  28.5 38.7 %collective-permute-start.1 = (f32[328,640]{1,0:T(8,128)}, f32[328,640]{1,0:T(8,128)S(1)}, u32[]{:S(2)}, u32[]{:S(2)}) collective-permute-start(f32[328,640]{1,0:T(8,128)} %get-tuple-element.29.refs_0_), channel_id=1, source_target_pairs={{0,6},{1,7},{2,0},{3,1},{4,2},{5,3},{6,4},{7,5},{8,14},{9,15},{10,... | collective-permute-start | bytes 2519048 | tf_op jit(solution)/shard_map/ppermute | solution.py:313
  32.3 0.9 copy-start
  33.2 0.9 copy-start.2
  34.1 22.7 %collective-permute-start.6 = (f32[320,640]{1,0:T(8,128)}, f32[320,640]{1,0:T(8,128)}, u32[]{:S(2)}, u32[]{:S(2)}) collective-permute-start(f32[320,640]{1,0:T(8,128)} %pad_maximum_fusion.refs_0_), channel_id=1, source_target_pairs={{0,24},{1,25},{2,26},{3,27},{4,28},{5,29},{6,30},{7,31},{8,16},{9,... | collective-permute-start | bytes 2457608 | tf_op jit(solution)/shard_map/ppermute | solution.py:313
  41.8 15.1 %copy-start.1 = (f32[320,640]{1,0:T(8,128)S(1)}, f32[320,640]{1,0:T(8,128)}, u32[]{:S(2)}) copy-start(f32[320,640]{1,0:T(8,128)} %copy-done) | copy-start | bytes 2457604
  41.8 15.1 %copy-start.3 = (f32[320,640]{1,0:T(8,128)S(1)}, f32[320,640]{1,0:T(8,128)}, u32[]{:S(2)}) copy-start(f32[320,640]{1,0:T(8,128)} %copy-done.2) | copy-start | bytes 2457604
  69.7 3.1 %collective-permute-start.7 = (f32[320,960]{1,0:T(8,128)S(1)}, f32[320,960]{1,0:T(8,128)S(1)}, u32[]{:S(2)}, u32[]{:S(2)}) collective-permute-start(f32[320,960]{1,0:T(8,128)S(1)} %get-tuple-element.39.refs_1_), channel_id=1, source_target_pairs={{0,1},{1,0},{2,3},{3,2},{4,5},{5,4},{6,7},{7,6},{8,9},{9,8},{10,11... | collective-permute-start | bytes 3686408 | tf_op jit(solution)/shard_map/ppermute | solution.py:316
  72.0 7.1 %collective-permute-start.8 = (f32[320,640]{1,0:T(8,128)S(1)}, f32[320,640]{1,0:T(8,128)S(1)}, u32[]{:S(2)}, u32[]{:S(2)}) collective-permute-start(f32[320,640]{1,0:T(8,128)S(1)} %get-tuple-element.37), channel_id=1, source_target_pairs={{0,1},{1,0},{2,3},{3,2},{4,5},{5,4},{6,7},{7,6},{8,9},{9,8},{10,11... | collective-permute-start | bytes 2457608 | tf_op jit(solution)/shard_map/ppermute | solution.py:316
  72.8 6.3 %copy-start.6 = (f32[640]{0:T(1024)S(1)}, f32[640]{0:T(1024)}, u32[]{:S(2)}) copy-start(f32[640]{0:T(1024)} %param.7) | copy-start | bytes 7684
  75.2 22.2 %collective-permute-start.9 = (f32[320,640]{1,0:T(8,128)S(1)}, f32[320,640]{1,0:T(8,128)S(1)}, u32[]{:S(2)}, u32[]{:S(2)}) collective-permute-start(f32[320,640]{1,0:T(8,128)S(1)} %get-tuple-element.45), channel_id=1, source_target_pairs={{2,10},{3,11},{4,20},{5,21},{6,30},{7,31},{8,0},{9,1},{12,14},{13,... | collective-permute-start | bytes 2457608 | tf_op jit(solution)/shard_map/ppermute | solution.py:313
  76.5 40.2 %collective-permute-start.10 = (f32[320,640]{1,0:T(8,128)S(1)}, f32[320,640]{1,0:T(8,128)S(1)}, u32[]{:S(2)}, u32[]{:S(2)}) collective-permute-start(f32[320,640]{1,0:T(8,128)S(1)} %get-tuple-element.46), channel_id=1, source_target_pairs={{2,6},{3,7},{4,2},{5,3},{6,4},{7,5},{8,12},{9,13},{12,20},{13,21},... | collective-permute-start | bytes 2457608 | tf_op jit(solution)/shard_map/ppermute | solution.py:313
  77.8 38.9 %collective-permute-start.11 = (f32[320,640]{1,0:T(8,128)S(1)}, f32[320,640]{1,0:T(8,128)S(1)}, u32[]{:S(2)}, u32[]{:S(2)}) collective-permute-start(f32[320,640]{1,0:T(8,128)S(1)} %get-tuple-element.47), channel_id=1, source_target_pairs={{2,4},{3,5},{4,6},{5,7},{6,2},{7,3},{8,14},{9,15},{12,8},{13,9},{1... | collective-permute-start | bytes 2457608 | tf_op jit(solution)/shard_map/ppermute | solution.py:313
  120.9 4.5 %collective-permute-start.12 = (f32[328,640]{1,0:T(8,128)S(1)}, f32[328,640]{1,0:T(8,128)S(1)}, u32[]{:S(2)}, u32[]{:S(2)}) collective-permute-start(f32[328,640]{1,0:T(8,128)S(1)} %shard_map.77), channel_id=1, source_target_pairs={{0,1},{1,0},{2,3},{3,2},{4,5},{5,4},{6,7},{7,6},{8,9},{9,8},{10,11... | collective-permute-start | bytes 2519048 | tf_op jit(solution)/shard_map/ppermute | solution.py:316
  125.4 3.8 %collective-permute-start.13 = (f32[8,320]{1,0:T(8,128)S(1)}, f32[8,320]{1,0:T(8,128)S(1)}, u32[]{:S(2)}, u32[]{:S(2)}) collective-permute-start(f32[8,320]{1,0:T(8,128)S(1)} %slice_add_fusion.1), channel_id=1, source_target_pairs={{0,8},{1,9},{2,10},{3,11},{4,12},{5,13},{6,14},{7,15},{8,0},{9,1},... | collective-permute-start | bytes 30728 | tf_op jit(solution)/shard_map/ppermute | solution.py:313
  129.2 3.7 %collective-permute-start.14 = (f32[8,320]{1,0:T(8,128)S(1)}, f32[8,320]{1,0:T(8,128)S(1)}, u32[]{:S(2)}, u32[]{:S(2)}) collective-permute-start(f32[8,320]{1,0:T(8,128)S(1)} %add.57), channel_id=1, source_target_pairs={{0,16},{1,17},{2,18},{3,19},{4,20},{5,21},{6,22},{7,23},{8,24},{9,... | collective-permute-start | bytes 30728 | tf_op jit(solution)/shard_map/ppermute | solution.py:313

commit v5 on v4

--- a/solution.py
+++ b/solution.py
@@ -213,15 +213,19 @@
         copy.start()
         copy.wait()
     for t in range(count):
-        for copy in copies(t):
-            copy.start()
+
+        @pl.when(ids[place + t] >= 0)
+        def _():
+            for copy in copies(t):
+                copy.start()
+
     out[:half, :] = start[...]
     for t in range(count):
-        for copy in copies(t):
-            copy.wait()
 
         @pl.when(ids[place + t] >= 0)
         def _():
+            for copy in copies(t):
+                copy.wait()
             out[:half, :] += dot(held[t], second(tiles[t], 0))
 
     out[half:, :] = jnp.zeros((ROWS, height), jnp.float32)
@@ -463,8 +467,7 @@
         )
         received = swap_core(given_cube)
         sums = sums + kept_cube[half:, :half] + received[half:, :half]
-        for m in powers:
-            sums = sums + send(sums, across(m))
+        sums = sums + sum(send(sums, across(m)) for m in range(1, panels))
         return (kept_cube[:half] + received[:half]).T, sums[:2]
 
     return body

time: 134 us -> 132 us (0.985)
  waiting for transfers between devices: 67.7 us -> 62.4 us
  starting transfers between devices: 17.6 us -> 20.8 us
    ppermute x11 -> x12, waiting for transfers between devices: 67.4 us -> 62.1 us  [send(): return lax.ppermute(value, ('row', 'col'), pairs)]
    ppermute x11 -> x12, starting transfers between devices: 16.4 us -> 19.6 us  [send(): return lax.ppermute(value, ('row', 'col'), pairs)]
  transfers between devices with their start and end apart: 15 -> 16, of which waited for: 8 -> 8; matrix products, arithmetic and copies ran while one was open for 6% -> 6% of each run, Pallas kernels for 21% -> 21%
where the time goes in v5:
time: 132 us; the launch traced here: 131 us
  waiting for transfers between devices  62.4 us (47%)
  Pallas kernels  35.7 us (27%)
  starting transfers between devices  20.8 us (16%)
  local copies, waits for them, and re-layouts  8.82 us (7%)
  other arithmetic  2.67 us (2%)
    ppermute x12, waiting for transfers between devices, send(): return lax.ppermute(value, ('row', 'col'), pairs)  62.1 us
    pallas_call x10, Pallas kernels, call(): pl.pallas_call(body, out_shape=outs, in_specs=[pl.BlockSpec(memory_space=...  35.7 us
    ppermute x12, starting transfers between devices, send(): return lax.ppermute(value, ('row', 'col'), pairs)  19.6 us
    unnamed x14, local copies, waits for them, and re-layouts  3.66 us
  transfers between devices with their start and end apart: 16, of which 8 were waited for; matrix products, arithmetic and copies ran while one was open for 6% of the time, Pallas kernels for 21%

profile of v5, /device:TPU:0, one launch (start us, length us, event | category | flops | bytes accessed | tf_op | source)
XLA Modules:
  0.0 131.2 jit_solution(3982518803421886747)
XLA Ops:
  2.5 1.3 %shard_map.68 = (f32[328,640]{1,0:T(8,128)}, f32[320,320]{1,0:T(8,128)S(1)}, f32[328,320]{1,0:T(8,128)S(1)}, f32[8,128]{1,0:T(8,128)S(1)}) custom-call(s32[1]{0:T(128)} %bitcast.ids_ref, f32[320,640]{1,0:T(8,128)S(1)} %bitcast.19, s32[5,10]{1,0:T(8,128)S(1)} %bitcast.20), custom_call_target="tpu_custom_call" | custom-call | tf_op jit(solution)/shard_map/pallas_call | solution.py:64
  4.3 2.6 %collective-permute-start.2 = (f32[328,640]{1,0:T(8,128)}, f32[328,640]{1,0:T(8,128)S(1)}, u32[]{:S(2)}, u32[]{:S(2)}) collective-permute-start(f32[328,640]{1,0:T(8,128)} %get-tuple-element.29.refs_0_), channel_id=1, source_target_pairs={{0,2},{1,3},{2,4},{3,5},{4,6},{5,7},{6,0},{7,1},{8,10},{9,11},{10,... | collective-permute-start | bytes 2519048 | tf_op jit(solution)/shard_map/ppermute | solution.py:317
  8.1 1.7 %collective-permute-start.4 = (f32[320,640]{1,0:T(8,128)}, f32[320,640]{1,0:T(8,128)S(1)}, u32[]{:S(2)}, u32[]{:S(2)}) collective-permute-start(f32[320,640]{1,0:T(8,128)} %pad_maximum_fusion.refs_0_), channel_id=1, source_target_pairs={{0,8},{1,9},{2,10},{3,11},{4,12},{5,13},{6,14},{7,15},{8,0},{9,1},... | collective-permute-start | bytes 2457608 | tf_op jit(solution)/shard_map/ppermute | solution.py:317
  9.8 1.5 %collective-permute-start.5 = (f32[320,640]{1,0:T(8,128)}, f32[320,640]{1,0:T(8,128)S(1)}, u32[]{:S(2)}, u32[]{:S(2)}) collective-permute-start(f32[320,640]{1,0:T(8,128)} %pad_maximum_fusion.refs_0_), channel_id=1, source_target_pairs={{0,16},{1,17},{2,18},{3,19},{4,20},{5,21},{6,22},{7,23},{8,24},{9,... | collective-permute-start | bytes 2457608 | tf_op jit(solution)/shard_map/ppermute | solution.py:317
  11.3 17.1 %collective-permute-done.2.refs_1_.refs_2_ = f32[328,640]{1,0:T(8,128)S(1)} collective-permute-done((f32[328,640]{1,0:T(8,128)}, f32[328,640]{1,0:T(8,128)S(1)}, u32[]{:S(2)}, u32[]{:S(2)}) %collective-permute-start.2) | collective-permute-done | bytes 839712 | tf_op jit(solution)/shard_map/ppermute | solution.py:317
  28.5 3.8 %collective-permute-start.1 = (f32[328,640]{1,0:T(8,128)}, f32[328,640]{1,0:T(8,128)S(1)}, u32[]{:S(2)}, u32[]{:S(2)}) collective-permute-start(f32[328,640]{1,0:T(8,128)} %get-tuple-element.29.refs_0_), channel_id=1, source_target_pairs={{0,6},{1,7},{2,0},{3,1},{4,2},{5,3},{6,4},{7,5},{8,14},{9,15},{10,... | collective-permute-start | bytes 2519048 | tf_op jit(solution)/shard_map/ppermute | solution.py:317
  34.1 2.4 %collective-permute-start.6 = (f32[320,640]{1,0:T(8,128)}, f32[320,640]{1,0:T(8,128)}, u32[]{:S(2)}, u32[]{:S(2)}) collective-permute-start(f32[320,640]{1,0:T(8,128)} %pad_maximum_fusion.refs_0_), channel_id=1, source_target_pairs={{0,24},{1,25},{2,26},{3,27},{4,28},{5,29},{6,30},{7,31},{8,16},{9,... | collective-permute-start | bytes 2457608 | tf_op jit(solution)/shard_map/ppermute | solution.py:317
  39.2 2.5 %stack.48.ids_ref = s32[16]{0:T(128)S(1)} concatenate(s32[1]{0:T(128)} %bitcast.ids_ref, s32[1]{0:T(128)} %bitcast.1, s32[1]{0:T(128)} %bitcast.2, s32[1]{0:T(128)} %bitcast.3, s32[1]{0:T(128)} %bitcast.4, s32[1]{0:T(128)} %bitcast.2, s32[1]{0:T(128)} %bitcast.5, s32[1]{0:T(128)} %bitcast.6, s32[1]{0:T(128)} %bitcast.7, s32[1]{0:T(128)} %bitcast.8, s32[1]{0:T(128)} %bitcast.9, ...), dimensions={0} | concatenate | bytes 128 | tf_op jit(solution)/shard_map/stack | solution.py:343
  41.7 10.1 %collective-permute-done.3.refs_2_.refs_3_ = f32[328,640]{1,0:T(8,128)S(1)} collective-permute-done((f32[328,640]{1,0:T(8,128)S(1)}, f32[328,640]{1,0:T(8,128)S(1)}, u32[]{:S(2)}, u32[]{:S(2)}) %collective-permute-start.3) | collective-permute-done | bytes 839712 | tf_op jit(solution)/shard_map/ppermute | solution.py:317
  51.9 5.0 %shard_map.71.refs_0_ = f32[640,640]{1,0:T(8,128)S(1)} custom-call(s32[16]{0:T(128)S(1)} %stack.48.ids_ref, f32[328,640]{1,0:T(8,128)} %get-tuple-element.29.refs_0_, f32[328,640]{1,0:T(8,128)S(1)} %collective-permute-done.2.refs_1_.refs_2_, f32[328,640]{1,0:T(8,128)S(1)} %collective-permute-done.3.refs_2_.refs_3_), custom_call_target="tpu_custom_call" | custom-call | tf_op jit(solution)/shard_map/pallas_call | solution.py:64
  56.9 2.9 %shard_map.69 = (bf16[4,320,960]{2,1,0:T(8,128)(2,1)S(1)}, bf16[4,320,960]{2,1,0:T(8,128)(2,1)S(1)}) custom-call(s32[16]{0:T(128)S(1)} %stack.48.ids_ref, f32[320,640]{1,0:T(8,128)} %pad_maximum_fusion.refs_0_, f32[320,640]{1,0:T(8,128)S(1)} %copy-done.1, f32[320,640]{1,0:T(8,128)S(1)} %copy-done.3, f32[320,640]{1,0:T(8,128)} %collective-permute-done.6.refs_3_), custom_call_target="tpu_custom_call" | custom-call | tf_op jit(solution)/shard_map/pallas_call | solution.py:64
  59.8 6.2 %shard_map.70 = (f32[320,640]{1,0:T(8,128)S(1)}, f32[320,640]{1,0:T(8,128)S(1)}) custom-call(s32[16]{0:T(128)S(1)} %stack.48.ids_ref, f32[328,640]{1,0:T(8,128)} %get-tuple-element.29.refs_0_, f32[328,640]{1,0:T(8,128)S(1)} %collective-permute-done.2.refs_1_.refs_2_, f32[328,640]{1,0:T(8,128)S(1)} %collective-permute-done.3.refs_2_.refs_3_, ...), custom_call_target="tpu_custom_call" | custom-call | tf_op jit(solution)/shard_map/pallas_call | solution.py:64
  67.1 2.5 %shard_map.72 = (f32[320,640]{1,0:T(8,128)S(1)}, f32[320,960]{1,0:T(8,128)S(1)}) custom-call(s32[16]{0:T(128)S(1)} %stack.48.ids_ref, f32[328,640]{1,0:T(8,128)S(1)} %collective-permute-done.1.refs_0_.refs_1_.refs_4_, f32[320,640]{1,0:T(8,128)S(1)} %get-tuple-element.34.refs_1_, f32[320,640]{1,0:T(8,128)S(1)} %get-tuple-element.35.refs_2_, ...), custom_call_target="tpu_custom_call" | custom-call | tf_op jit(solution)/shard_map/pallas_call | solution.py:64
  69.8 2.2 %shard_map.73 = (f32[320,640]{1,0:T(8,128)S(1)}, f32[320,640]{1,0:T(8,128)S(1)}, f32[8,128]{1,0:T(8,128)S(1)}) custom-call(s32[16]{0:T(128)S(1)} %stack.48.ids_ref, f32[640,640]{1,0:T(8,128)S(1)} %shard_map.71.refs_0_, f32[328,640]{1,0:T(8,128)S(1)} %collective-permute-done.1.refs_0_.refs_1_.refs_4_, f32[328,640]{1,0:T(8,128)S(1)} %collective-permute-done.2.refs_1_.refs_2_, ...), custom_call_target="tpu_custom_call" | custom-call | tf_op jit(solution)/shard_map/pallas_call | solution.py:64
  72.8 2.4 %shard_map.74 = (f32[320,640]{1,0:T(8,128)S(1)}, f32[320,640]{1,0:T(8,128)S(1)}, f32[320,640]{1,0:T(8,128)S(1)}, f32[320,640]{1,0:T(8,128)S(1)}) custom-call(s32[16]{0:T(128)S(1)} %stack.48.ids_ref, f32[320,640]{1,0:T(8,128)S(1)} %get-tuple-element.38.refs_0_.refs_4_, f32[320,960]{1,0:T(8,128)S(1)} %get-tuple-element.39.refs_1_, ...), custom_call_target="tpu_custom_call" | custom-call | tf_op jit(solution)/shard_map/pallas_call | solution.py:64
  75.2 1.3 collective-permute-start.9
  76.5 1.3 collective-permute-start.10
  77.8 1.3 collective-permute-start.11
  79.2 4.5 %shard_map.75 = (f32[320,640]{1,0:T(8,128)S(1)}, f32[320,640]{1,0:T(8,128)S(1)}, f32[8,320]{1,0:T(8,128)S(1)}) custom-call(s32[16]{0:T(128)S(1)} %stack.48.ids_ref, f32[320,640]{1,0:T(8,128)S(1)} %get-tuple-element.41.refs_0_.refs_2_, f32[320,640]{1,0:T(8,128)S(1)} %get-tuple-element.42.refs_1_, f32[320,640]{1,0:T(8,128)S(1)} %collective-permute-done.8.refs_2_, ...), custom_call_target="tpu_custom_call" | custom-call | tf_op jit(solution)/shard_map/pallas_call | solution.py:64
  83.6 13.8 %collective-permute-done.9.refs_5_.refs_4_ = f32[320,640]{1,0:T(8,128)S(1)} collective-permute-done((f32[320,640]{1,0:T(8,128)S(1)}, f32[320,640]{1,0:T(8,128)S(1)}, u32[]{:S(2)}, u32[]{:S(2)}) %collective-permute-start.9) | collective-permute-done | bytes 819232 | tf_op jit(solution)/shard_map/ppermute | solution.py:317
  97.4 19.3 %collective-permute-done.10.refs_6_.refs_5_ = f32[320,640]{1,0:T(8,128)S(1)} collective-permute-done((f32[320,640]{1,0:T(8,128)S(1)}, f32[320,640]{1,0:T(8,128)S(1)}, u32[]{:S(2)}, u32[]{:S(2)}) %collective-permute-start.10) | collective-permute-done | bytes 819232 | tf_op jit(solution)/shard_map/ppermute | solution.py:317
  116.7 4.2 %shard_map.77 = f32[328,640]{1,0:T(8,128)S(1)} custom-call(s32[16]{0:T(128)S(1)} %stack.48.ids_ref, f32[320,640]{1,0:T(8,128)S(1)} %get-tuple-element.48.refs_0_, f32[1,640]{1,0:T(1,128)S(1)} %broadcast_in_dim.2.refs_6_.refs_1_, bf16[4,320,960]{2,1,0:T(8,128)(2,1)S(1)} %get-tuple-element.32.refs_4_.refs_8_.refs_2_, ...), custom_call_target="tpu_custom_call" | custom-call | tf_op jit(solution)/shard_map/pallas_call | solution.py:64
  121.0 4.4 %shard_map.76 = f32[328,640]{1,0:T(8,128)S(1)} custom-call(s32[16]{0:T(128)S(1)} %stack.48.ids_ref, f32[320,640]{1,0:T(8,128)S(1)} %get-tuple-element.44.refs_0_, f32[1,640]{1,0:T(1,128)S(1)} %broadcast_in_dim.2.refs_6_.refs_1_, f32[320,640]{1,0:T(8,128)S(1)} %get-tuple-element.41.refs_0_.refs_2_, f32[8,128]{1,0:T(8,128)S(1)} %get-tuple-element.40.refs_3_, ...), custom_call_target="tpu_custom_call" | custom-call | tf_op jit(solution)/shard_map/pallas_call | solution.py:64
  126.5 2.5 %collective-permute-start.13 = (f32[8,320]{1,0:T(8,128)S(1)}, f32[8,320]{1,0:T(8,128)S(1)}, u32[]{:S(2)}, u32[]{:S(2)}) collective-permute-start(f32[8,320]{1,0:T(8,128)S(1)} %slice_add_fusion.1), channel_id=1, source_target_pairs={{0,8},{1,9},{2,10},{3,11},{4,12},{5,13},{6,14},{7,15},{8,0},{9,1},... | collective-permute-start | bytes 30728 | tf_op jit(solution)/shard_map/ppermute | solution.py:317
  (42 shorter events, 13.3 us)
Async XLA Ops:
  0.6 1.1 copy-start.4
  1.8 0.7 copy-start.5
  3.8 3.2 %collective-permute-start = (f32[328,320]{1,0:T(8,128)S(1)}, f32[328,320]{1,0:T(8,128)S(1)}, u32[]{:S(2)}, u32[]{:S(2)}) collective-permute-start(f32[328,320]{1,0:T(8,128)S(1)} %get-tuple-element.28), channel_id=1, source_target_pairs={{0,1},{1,0},{2,3},{3,2},{4,5},{5,4},{6,7},{7,6},{8,9},{9,8},{10,11... | collective-permute-start | bytes 1259528 | tf_op jit(solution)/shard_map/ppermute | solution.py:320
  4.3 24.2 %collective-permute-start.2 = (f32[328,640]{1,0:T(8,128)}, f32[328,640]{1,0:T(8,128)S(1)}, u32[]{:S(2)}, u32[]{:S(2)}) collective-permute-start(f32[328,640]{1,0:T(8,128)} %get-tuple-element.29.refs_0_), channel_id=1, source_target_pairs={{0,2},{1,3},{2,4},{3,5},{4,6},{5,7},{6,0},{7,1},{8,10},{9,11},{10,... | collective-permute-start | bytes 2519048 | tf_op jit(solution)/shard_map/ppermute | solution.py:317
  8.1 24.2 %collective-permute-start.4 = (f32[320,640]{1,0:T(8,128)}, f32[320,640]{1,0:T(8,128)S(1)}, u32[]{:S(2)}, u32[]{:S(2)}) collective-permute-start(f32[320,640]{1,0:T(8,128)} %pad_maximum_fusion.refs_0_), channel_id=1, source_target_pairs={{0,8},{1,9},{2,10},{3,11},{4,12},{5,13},{6,14},{7,15},{8,0},{9,1},... | collective-permute-start | bytes 2457608 | tf_op jit(solution)/shard_map/ppermute | solution.py:317
  9.8 23.4 %collective-permute-start.5 = (f32[320,640]{1,0:T(8,128)}, f32[320,640]{1,0:T(8,128)S(1)}, u32[]{:S(2)}, u32[]{:S(2)}) collective-permute-start(f32[320,640]{1,0:T(8,128)} %pad_maximum_fusion.refs_0_), channel_id=1, source_target_pairs={{0,16},{1,17},{2,18},{3,19},{4,20},{5,21},{6,22},{7,23},{8,24},{9,... | collective-permute-start | bytes 2457608 | tf_op jit(solution)/shard_map/ppermute | solution.py:317
  28.5 23.4 %collective-permute-start.3 = (f32[328,640]{1,0:T(8,128)S(1)}, f32[328,640]{1,0:T(8,128)S(1)}, u32[]{:S(2)}, u32[]{:S(2)}) collective-permute-start(f32[328,640]{1,0:T(8,128)S(1)} %collective-permute-done.2.refs_1_.refs_2_), channel_id=1, source_target_pairs={{0,2},{1,3},{2,4},{3,5},{4,6},{5,7},{6,0},{7,1},{8,10},{9,11},{10,... | collective-permute-start | bytes 2519048 | tf_op jit(solution)/shard_map/ppermute | solution.py:317
  28.5 38.7 %collective-permute-start.1 = (f32[328,640]{1,0:T(8,128)}, f32[328,640]{1,0:T(8,128)S(1)}, u32[]{:S(2)}, u32[]{:S(2)}) collective-permute-start(f32[328,640]{1,0:T(8,128)} %get-tuple-element.29.refs_0_), channel_id=1, source_target_pairs={{0,6},{1,7},{2,0},{3,1},{4,2},{5,3},{6,4},{7,5},{8,14},{9,15},{10,... | collective-permute-start | bytes 2519048 | tf_op jit(solution)/shard_map/ppermute | solution.py:317
  32.3 0.9 copy-start
  33.2 0.9 copy-start.2
  34.1 22.7 %collective-permute-start.6 = (f32[320,640]{1,0:T(8,128)}, f32[320,640]{1,0:T(8,128)}, u32[]{:S(2)}, u32[]{:S(2)}) collective-permute-start(f32[320,640]{1,0:T(8,128)} %pad_maximum_fusion.refs_0_), channel_id=1, source_target_pairs={{0,24},{1,25},{2,26},{3,27},{4,28},{5,29},{6,30},{7,31},{8,16},{9,... | collective-permute-start | bytes 2457608 | tf_op jit(solution)/shard_map/ppermute | solution.py:317
  41.7 15.2 %copy-start.1 = (f32[320,640]{1,0:T(8,128)S(1)}, f32[320,640]{1,0:T(8,128)}, u32[]{:S(2)}) copy-start(f32[320,640]{1,0:T(8,128)} %copy-done) | copy-start | bytes 2457604
  41.7 15.2 %copy-start.3 = (f32[320,640]{1,0:T(8,128)S(1)}, f32[320,640]{1,0:T(8,128)}, u32[]{:S(2)}) copy-start(f32[320,640]{1,0:T(8,128)} %copy-done.2) | copy-start | bytes 2457604
  69.7 3.1 %collective-permute-start.7 = (f32[320,960]{1,0:T(8,128)S(1)}, f32[320,960]{1,0:T(8,128)S(1)}, u32[]{:S(2)}, u32[]{:S(2)}) collective-permute-start(f32[320,960]{1,0:T(8,128)S(1)} %get-tuple-element.39.refs_1_), channel_id=1, source_target_pairs={{0,1},{1,0},{2,3},{3,2},{4,5},{5,4},{6,7},{7,6},{8,9},{9,8},{10,11... | collective-permute-start | bytes 3686408 | tf_op jit(solution)/shard_map/ppermute | solution.py:320
  72.0 7.1 %collective-permute-start.8 = (f32[320,640]{1,0:T(8,128)S(1)}, f32[320,640]{1,0:T(8,128)S(1)}, u32[]{:S(2)}, u32[]{:S(2)}) collective-permute-start(f32[320,640]{1,0:T(8,128)S(1)} %get-tuple-element.37), channel_id=1, source_target_pairs={{0,1},{1,0},{2,3},{3,2},{4,5},{5,4},{6,7},{7,6},{8,9},{9,8},{10,11... | collective-permute-start | bytes 2457608 | tf_op jit(solution)/shard_map/ppermute | solution.py:320
  72.8 6.3 %copy-start.6 = (f32[640]{0:T(1024)S(1)}, f32[640]{0:T(1024)}, u32[]{:S(2)}) copy-start(f32[640]{0:T(1024)} %param.7) | copy-start | bytes 7684
  75.2 22.2 %collective-permute-start.9 = (f32[320,640]{1,0:T(8,128)S(1)}, f32[320,640]{1,0:T(8,128)S(1)}, u32[]{:S(2)}, u32[]{:S(2)}) collective-permute-start(f32[320,640]{1,0:T(8,128)S(1)} %get-tuple-element.45), channel_id=1, source_target_pairs={{2,10},{3,11},{4,20},{5,21},{6,30},{7,31},{8,0},{9,1},{12,14},{13,... | collective-permute-start | bytes 2457608 | tf_op jit(solution)/shard_map/ppermute | solution.py:317
  76.5 40.2 %collective-permute-start.10 = (f32[320,640]{1,0:T(8,128)S(1)}, f32[320,640]{1,0:T(8,128)S(1)}, u32[]{:S(2)}, u32[]{:S(2)}) collective-permute-start(f32[320,640]{1,0:T(8,128)S(1)} %get-tuple-element.46), channel_id=1, source_target_pairs={{2,6},{3,7},{4,2},{5,3},{6,4},{7,5},{8,12},{9,13},{12,20},{13,21},... | collective-permute-start | bytes 2457608 | tf_op jit(solution)/shard_map/ppermute | solution.py:317
  77.8 38.9 %collective-permute-start.11 = (f32[320,640]{1,0:T(8,128)S(1)}, f32[320,640]{1,0:T(8,128)S(1)}, u32[]{:S(2)}, u32[]{:S(2)}) collective-permute-start(f32[320,640]{1,0:T(8,128)S(1)} %get-tuple-element.47), channel_id=1, source_target_pairs={{2,4},{3,5},{4,6},{5,7},{6,2},{7,3},{8,14},{9,15},{12,8},{13,9},{1... | collective-permute-start | bytes 2457608 | tf_op jit(solution)/shard_map/ppermute | solution.py:317
  120.9 4.5 %collective-permute-start.12 = (f32[328,640]{1,0:T(8,128)S(1)}, f32[328,640]{1,0:T(8,128)S(1)}, u32[]{:S(2)}, u32[]{:S(2)}) collective-permute-start(f32[328,640]{1,0:T(8,128)S(1)} %shard_map.77), channel_id=1, source_target_pairs={{0,1},{1,0},{2,3},{3,2},{4,5},{5,4},{6,7},{7,6},{8,9},{9,8},{10,11... | collective-permute-start | bytes 2519048 | tf_op jit(solution)/shard_map/ppermute | solution.py:320
  125.4 4.7 %collective-permute-start.15 = (f32[8,320]{1,0:T(8,128)S(1)}, f32[8,320]{1,0:T(8,128)S(1)}, u32[]{:S(2)}, u32[]{:S(2)}) collective-permute-start(f32[8,320]{1,0:T(8,128)S(1)} %slice_add_fusion.1), channel_id=1, source_target_pairs={{0,24},{1,25},{2,26},{3,27},{4,28},{5,29},{6,30},{7,31},{8,16},{9,... | collective-permute-start | bytes 30728 | tf_op jit(solution)/shard_map/ppermute | solution.py:317
  125.5 4.6 %collective-permute-start.14 = (f32[8,320]{1,0:T(8,128)S(1)}, f32[8,320]{1,0:T(8,128)S(1)}, u32[]{:S(2)}, u32[]{:S(2)}) collective-permute-start(f32[8,320]{1,0:T(8,128)S(1)} %slice_add_fusion.1), channel_id=1, source_target_pairs={{0,16},{1,17},{2,18},{3,19},{4,20},{5,21},{6,22},{7,23},{8,24},{9,... | collective-permute-start | bytes 30728 | tf_op jit(solution)/shard_map/ppermute | solution.py:317
  126.5 4.1 %collective-permute-start.13 = (f32[8,320]{1,0:T(8,128)S(1)}, f32[8,320]{1,0:T(8,128)S(1)}, u32[]{:S(2)}, u32[]{:S(2)}) collective-permute-start(f32[8,320]{1,0:T(8,128)S(1)} %slice_add_fusion.1), channel_id=1, source_target_pairs={{0,8},{1,9},{2,10},{3,11},{4,12},{5,13},{6,14},{7,15},{8,0},{9,1},... | collective-permute-start | bytes 30728 | tf_op jit(solution)/shard_map/ppermute | solution.py:317

commit v6 on v5

--- a/solution.py
+++ b/solution.py
@@ -297,8 +297,8 @@
     assert columns == 2 * panels and panels & (panels - 1) == 0
     chips = [(r, z) for r in range(panels) for z in range(panels)]
 
-    edges = [((r, z), (r, q)) for r, z in chips for q in range(panels) if z != r and q != r and q != z]
-    edges += [((r, z), (z, z)) for r, z in chips if z != r]
+    edges = [((r, z), (z, z)) for r, z in chips if z != r]
+    edges += [((r, z), (r, q)) for r, z in chips for q in range(panels) if z != r and q != r and q != z]
     steps, sent, got = in_steps(edges)
     down_step = [[-1] * panels for _ in range(panels)]
     tile_got = [[[-1] * steps for _ in range(panels)] for _ in range(panels)]

time: 132 us -> 131 us (level)
  no operation moved by 1% of the time
where the time goes in v6:
time: 131 us
  waiting for transfers between devices  61.9 us (47%)
  Pallas kernels  35.7 us (27%)
  starting transfers between devices  20.8 us (16%)
  local copies, waits for them, and re-layouts  8.82 us (7%)
  other arithmetic  2.67 us (2%)
    ppermute x12, waiting for transfers between devices, send(): return lax.ppermute(value, ('row', 'col'), pairs)  61.6 us
    pallas_call x10, Pallas kernels, call(): pl.pallas_call(body, out_shape=outs, in_specs=[pl.BlockSpec(memory_space=...  35.7 us
    ppermute x12, starting transfers between devices, send(): return lax.ppermute(value, ('row', 'col'), pairs)  19.6 us
    unnamed x14, local copies, waits for them, and re-layouts  3.66 us
  transfers between devices with their start and end apart: 16, of which 8 were waited for; matrix products, arithmetic and copies ran while one was open for 6% of the time, Pallas kernels for 21%

profile of v6, /device:TPU:0, one launch (start us, length us, event | category | flops | bytes accessed | tf_op | source)
XLA Modules:
  0.0 130.8 jit_solution(3351362918289986586)
XLA Ops:
  2.5 1.3 %shard_map.68 = (f32[328,640]{1,0:T(8,128)}, f32[320,320]{1,0:T(8,128)S(1)}, f32[328,320]{1,0:T(8,128)S(1)}, f32[8,128]{1,0:T(8,128)S(1)}) custom-call(s32[1]{0:T(128)} %bitcast.ids_ref, f32[320,640]{1,0:T(8,128)S(1)} %bitcast.19, s32[5,10]{1,0:T(8,128)S(1)} %bitcast.20), custom_call_target="tpu_custom_call" | custom-call | tf_op jit(solution)/shard_map/pallas_call | solution.py:64
  4.3 2.6 %collective-permute-start.2 = (f32[328,640]{1,0:T(8,128)}, f32[328,640]{1,0:T(8,128)S(1)}, u32[]{:S(2)}, u32[]{:S(2)}) collective-permute-start(f32[328,640]{1,0:T(8,128)} %get-tuple-element.29.refs_0_), channel_id=1, source_target_pairs={{0,2},{1,3},{2,4},{3,5},{4,6},{5,7},{6,0},{7,1},{8,10},{9,11},{10,... | collective-permute-start | bytes 2519048 | tf_op jit(solution)/shard_map/ppermute | solution.py:317
  8.1 1.7 %collective-permute-start.4 = (f32[320,640]{1,0:T(8,128)}, f32[320,640]{1,0:T(8,128)S(1)}, u32[]{:S(2)}, u32[]{:S(2)}) collective-permute-start(f32[320,640]{1,0:T(8,128)} %pad_maximum_fusion.refs_0_), channel_id=1, source_target_pairs={{0,8},{1,9},{2,10},{3,11},{4,12},{5,13},{6,14},{7,15},{8,0},{9,1},... | collective-permute-start | bytes 2457608 | tf_op jit(solution)/shard_map/ppermute | solution.py:317
  9.8 1.5 %collective-permute-start.5 = (f32[320,640]{1,0:T(8,128)}, f32[320,640]{1,0:T(8,128)S(1)}, u32[]{:S(2)}, u32[]{:S(2)}) collective-permute-start(f32[320,640]{1,0:T(8,128)} %pad_maximum_fusion.refs_0_), channel_id=1, source_target_pairs={{0,16},{1,17},{2,18},{3,19},{4,20},{5,21},{6,22},{7,23},{8,24},{9,... | collective-permute-start | bytes 2457608 | tf_op jit(solution)/shard_map/ppermute | solution.py:317
  11.3 17.1 %collective-permute-done.2.refs_1_.refs_2_ = f32[328,640]{1,0:T(8,128)S(1)} collective-permute-done((f32[328,640]{1,0:T(8,128)}, f32[328,640]{1,0:T(8,128)S(1)}, u32[]{:S(2)}, u32[]{:S(2)}) %collective-permute-start.2) | collective-permute-done | bytes 839712 | tf_op jit(solution)/shard_map/ppermute | solution.py:317
  28.5 3.8 %collective-permute-start.1 = (f32[328,640]{1,0:T(8,128)}, f32[328,640]{1,0:T(8,128)S(1)}, u32[]{:S(2)}, u32[]{:S(2)}) collective-permute-start(f32[328,640]{1,0:T(8,128)} %get-tuple-element.29.refs_0_), channel_id=1, source_target_pairs={{0,6},{1,7},{2,0},{3,1},{4,2},{5,3},{6,4},{7,5},{8,14},{9,15},{10,... | collective-permute-start | bytes 2519048 | tf_op jit(solution)/shard_map/ppermute | solution.py:317
  34.1 2.4 %collective-permute-start.6 = (f32[320,640]{1,0:T(8,128)}, f32[320,640]{1,0:T(8,128)}, u32[]{:S(2)}, u32[]{:S(2)}) collective-permute-start(f32[320,640]{1,0:T(8,128)} %pad_maximum_fusion.refs_0_), channel_id=1, source_target_pairs={{0,24},{1,25},{2,26},{3,27},{4,28},{5,29},{6,30},{7,31},{8,16},{9,... | collective-permute-start | bytes 2457608 | tf_op jit(solution)/shard_map/ppermute | solution.py:317
  39.2 2.5 %stack.48.ids_ref = s32[16]{0:T(128)S(1)} concatenate(s32[1]{0:T(128)} %bitcast.ids_ref, s32[1]{0:T(128)} %bitcast.1, s32[1]{0:T(128)} %bitcast.2, s32[1]{0:T(128)} %bitcast.3, s32[1]{0:T(128)} %bitcast.4, s32[1]{0:T(128)} %bitcast.2, s32[1]{0:T(128)} %bitcast.5, s32[1]{0:T(128)} %bitcast.6, s32[1]{0:T(128)} %bitcast.7, s32[1]{0:T(128)} %bitcast.8, s32[1]{0:T(128)} %bitcast.9, ...), dimensions={0} | concatenate | bytes 128 | tf_op jit(solution)/shard_map/stack | solution.py:343
  41.7 10.1 %collective-permute-done.3.refs_2_.refs_3_ = f32[328,640]{1,0:T(8,128)S(1)} collective-permute-done((f32[328,640]{1,0:T(8,128)S(1)}, f32[328,640]{1,0:T(8,128)S(1)}, u32[]{:S(2)}, u32[]{:S(2)}) %collective-permute-start.3) | collective-permute-done | bytes 839712 | tf_op jit(solution)/shard_map/ppermute | solution.py:317
  51.9 5.0 %shard_map.71.refs_0_ = f32[640,640]{1,0:T(8,128)S(1)} custom-call(s32[16]{0:T(128)S(1)} %stack.48.ids_ref, f32[328,640]{1,0:T(8,128)} %get-tuple-element.29.refs_0_, f32[328,640]{1,0:T(8,128)S(1)} %collective-permute-done.2.refs_1_.refs_2_, f32[328,640]{1,0:T(8,128)S(1)} %collective-permute-done.3.refs_2_.refs_3_), custom_call_target="tpu_custom_call" | custom-call | tf_op jit(solution)/shard_map/pallas_call | solution.py:64
  56.9 2.9 %shard_map.69 = (bf16[4,320,960]{2,1,0:T(8,128)(2,1)S(1)}, bf16[4,320,960]{2,1,0:T(8,128)(2,1)S(1)}) custom-call(s32[16]{0:T(128)S(1)} %stack.48.ids_ref, f32[320,640]{1,0:T(8,128)} %pad_maximum_fusion.refs_0_, f32[320,640]{1,0:T(8,128)S(1)} %copy-done.1, f32[320,640]{1,0:T(8,128)S(1)} %copy-done.3, f32[320,640]{1,0:T(8,128)} %collective-permute-done.6.refs_3_), custom_call_target="tpu_custom_call" | custom-call | tf_op jit(solution)/shard_map/pallas_call | solution.py:64
  59.8 6.2 %shard_map.70 = (f32[320,640]{1,0:T(8,128)S(1)}, f32[320,640]{1,0:T(8,128)S(1)}) custom-call(s32[16]{0:T(128)S(1)} %stack.48.ids_ref, f32[328,640]{1,0:T(8,128)} %get-tuple-element.29.refs_0_, f32[328,640]{1,0:T(8,128)S(1)} %collective-permute-done.2.refs_1_.refs_2_, f32[328,640]{1,0:T(8,128)S(1)} %collective-permute-done.3.refs_2_.refs_3_, ...), custom_call_target="tpu_custom_call" | custom-call | tf_op jit(solution)/shard_map/pallas_call | solution.py:64
  67.1 2.5 %shard_map.72 = (f32[320,640]{1,0:T(8,128)S(1)}, f32[320,960]{1,0:T(8,128)S(1)}) custom-call(s32[16]{0:T(128)S(1)} %stack.48.ids_ref, f32[328,640]{1,0:T(8,128)S(1)} %collective-permute-done.1.refs_0_.refs_1_.refs_4_, f32[320,640]{1,0:T(8,128)S(1)} %get-tuple-element.34.refs_1_, f32[320,640]{1,0:T(8,128)S(1)} %get-tuple-element.35.refs_2_, ...), custom_call_target="tpu_custom_call" | custom-call | tf_op jit(solution)/shard_map/pallas_call | solution.py:64
  69.8 2.2 %shard_map.73 = (f32[320,640]{1,0:T(8,128)S(1)}, f32[320,640]{1,0:T(8,128)S(1)}, f32[8,128]{1,0:T(8,128)S(1)}) custom-call(s32[16]{0:T(128)S(1)} %stack.48.ids_ref, f32[640,640]{1,0:T(8,128)S(1)} %shard_map.71.refs_0_, f32[328,640]{1,0:T(8,128)S(1)} %collective-permute-done.1.refs_0_.refs_1_.refs_4_, f32[328,640]{1,0:T(8,128)S(1)} %collective-permute-done.2.refs_1_.refs_2_, ...), custom_call_target="tpu_custom_call" | custom-call | tf_op jit(solution)/shard_map/pallas_call | solution.py:64
  72.8 2.4 %shard_map.74 = (f32[320,640]{1,0:T(8,128)S(1)}, f32[320,640]{1,0:T(8,128)S(1)}, f32[320,640]{1,0:T(8,128)S(1)}, f32[320,640]{1,0:T(8,128)S(1)}) custom-call(s32[16]{0:T(128)S(1)} %stack.48.ids_ref, f32[320,640]{1,0:T(8,128)S(1)} %get-tuple-element.38.refs_0_.refs_4_, f32[320,960]{1,0:T(8,128)S(1)} %get-tuple-element.39.refs_1_, ...), custom_call_target="tpu_custom_call" | custom-call | tf_op jit(solution)/shard_map/pallas_call | solution.py:64
  75.2 1.3 collective-permute-start.9
  76.5 1.3 collective-permute-start.10
  79.2 4.5 %shard_map.75 = (f32[320,640]{1,0:T(8,128)S(1)}, f32[320,640]{1,0:T(8,128)S(1)}, f32[8,320]{1,0:T(8,128)S(1)}) custom-call(s32[16]{0:T(128)S(1)} %stack.48.ids_ref, f32[320,640]{1,0:T(8,128)S(1)} %get-tuple-element.41.refs_0_.refs_2_, f32[320,640]{1,0:T(8,128)S(1)} %get-tuple-element.42.refs_1_, f32[320,640]{1,0:T(8,128)S(1)} %collective-permute-done.8.refs_2_, ...), custom_call_target="tpu_custom_call" | custom-call | tf_op jit(solution)/shard_map/pallas_call | solution.py:64
  83.6 31.3 %collective-permute-done.9.refs_5_.refs_4_ = f32[320,640]{1,0:T(8,128)S(1)} collective-permute-done((f32[320,640]{1,0:T(8,128)S(1)}, f32[320,640]{1,0:T(8,128)S(1)}, u32[]{:S(2)}, u32[]{:S(2)}) %collective-permute-start.9) | collective-permute-done | bytes 819232 | tf_op jit(solution)/shard_map/ppermute | solution.py:317
  115.0 4.2 %shard_map.77 = f32[328,640]{1,0:T(8,128)S(1)} custom-call(s32[16]{0:T(128)S(1)} %stack.48.ids_ref, f32[320,640]{1,0:T(8,128)S(1)} %get-tuple-element.48.refs_0_, f32[1,640]{1,0:T(1,128)S(1)} %broadcast_in_dim.2.refs_6_.refs_1_, bf16[4,320,960]{2,1,0:T(8,128)(2,1)S(1)} %get-tuple-element.32.refs_4_.refs_8_.refs_2_, ...), custom_call_target="tpu_custom_call" | custom-call | tf_op jit(solution)/shard_map/pallas_call | solution.py:64
  119.3 4.4 %shard_map.76 = f32[328,640]{1,0:T(8,128)S(1)} custom-call(s32[16]{0:T(128)S(1)} %stack.48.ids_ref, f32[320,640]{1,0:T(8,128)S(1)} %get-tuple-element.44.refs_0_, f32[1,640]{1,0:T(1,128)S(1)} %broadcast_in_dim.2.refs_6_.refs_1_, f32[320,640]{1,0:T(8,128)S(1)} %get-tuple-element.41.refs_0_.refs_2_, f32[8,128]{1,0:T(8,128)S(1)} %get-tuple-element.40.refs_3_, ...), custom_call_target="tpu_custom_call" | custom-call | tf_op jit(solution)/shard_map/pallas_call | solution.py:64
  123.7 1.4 %collective-permute-start.15 = (f32[8,320]{1,0:T(8,128)S(1)}, f32[8,320]{1,0:T(8,128)S(1)}, u32[]{:S(2)}, u32[]{:S(2)}) collective-permute-start(f32[8,320]{1,0:T(8,128)S(1)} %slice_add_fusion.1), channel_id=1, source_target_pairs={{0,24},{1,25},{2,26},{3,27},{4,28},{5,29},{6,30},{7,31},{8,16},{9,... | collective-permute-start | bytes 30728 | tf_op jit(solution)/shard_map/ppermute | solution.py:317
  125.1 1.4 %collective-permute-start.14 = (f32[8,320]{1,0:T(8,128)S(1)}, f32[8,320]{1,0:T(8,128)S(1)}, u32[]{:S(2)}, u32[]{:S(2)}) collective-permute-start(f32[8,320]{1,0:T(8,128)S(1)} %slice_add_fusion.1), channel_id=1, source_target_pairs={{0,16},{1,17},{2,18},{3,19},{4,20},{5,21},{6,22},{7,23},{8,24},{9,... | collective-permute-start | bytes 30728 | tf_op jit(solution)/shard_map/ppermute | solution.py:317
  128.8 1.4 %collective-permute-done.13 = f32[8,320]{1,0:T(8,128)S(1)} collective-permute-done((f32[8,320]{1,0:T(8,128)S(1)}, f32[8,320]{1,0:T(8,128)S(1)}, u32[]{:S(2)}, u32[]{:S(2)}) %collective-permute-start.13) | collective-permute-done | bytes 10272 | tf_op jit(solution)/shard_map/ppermute | solution.py:317
  (42 shorter events, 14.1 us)
Async XLA Ops:
  0.6 1.1 copy-start.4
  1.8 0.7 copy-start.5
  3.8 3.2 %collective-permute-start = (f32[328,320]{1,0:T(8,128)S(1)}, f32[328,320]{1,0:T(8,128)S(1)}, u32[]{:S(2)}, u32[]{:S(2)}) collective-permute-start(f32[328,320]{1,0:T(8,128)S(1)} %get-tuple-element.28), channel_id=1, source_target_pairs={{0,1},{1,0},{2,3},{3,2},{4,5},{5,4},{6,7},{7,6},{8,9},{9,8},{10,11... | collective-permute-start | bytes 1259528 | tf_op jit(solution)/shard_map/ppermute | solution.py:320
  4.3 24.2 %collective-permute-start.2 = (f32[328,640]{1,0:T(8,128)}, f32[328,640]{1,0:T(8,128)S(1)}, u32[]{:S(2)}, u32[]{:S(2)}) collective-permute-start(f32[328,640]{1,0:T(8,128)} %get-tuple-element.29.refs_0_), channel_id=1, source_target_pairs={{0,2},{1,3},{2,4},{3,5},{4,6},{5,7},{6,0},{7,1},{8,10},{9,11},{10,... | collective-permute-start | bytes 2519048 | tf_op jit(solution)/shard_map/ppermute | solution.py:317
  8.1 24.2 %collective-permute-start.4 = (f32[320,640]{1,0:T(8,128)}, f32[320,640]{1,0:T(8,128)S(1)}, u32[]{:S(2)}, u32[]{:S(2)}) collective-permute-start(f32[320,640]{1,0:T(8,128)} %pad_maximum_fusion.refs_0_), channel_id=1, source_target_pairs={{0,8},{1,9},{2,10},{3,11},{4,12},{5,13},{6,14},{7,15},{8,0},{9,1},... | collective-permute-start | bytes 2457608 | tf_op jit(solution)/shard_map/ppermute | solution.py:317
  9.8 23.4 %collective-permute-start.5 = (f32[320,640]{1,0:T(8,128)}, f32[320,640]{1,0:T(8,128)S(1)}, u32[]{:S(2)}, u32[]{:S(2)}) collective-permute-start(f32[320,640]{1,0:T(8,128)} %pad_maximum_fusion.refs_0_), channel_id=1, source_target_pairs={{0,16},{1,17},{2,18},{3,19},{4,20},{5,21},{6,22},{7,23},{8,24},{9,... | collective-permute-start | bytes 2457608 | tf_op jit(solution)/shard_map/ppermute | solution.py:317
  28.5 23.4 %collective-permute-start.3 = (f32[328,640]{1,0:T(8,128)S(1)}, f32[328,640]{1,0:T(8,128)S(1)}, u32[]{:S(2)}, u32[]{:S(2)}) collective-permute-start(f32[328,640]{1,0:T(8,128)S(1)} %collective-permute-done.2.refs_1_.refs_2_), channel_id=1, source_target_pairs={{0,2},{1,3},{2,4},{3,5},{4,6},{5,7},{6,0},{7,1},{8,10},{9,11},{10,... | collective-permute-start | bytes 2519048 | tf_op jit(solution)/shard_map/ppermute | solution.py:317
  28.5 38.7 %collective-permute-start.1 = (f32[328,640]{1,0:T(8,128)}, f32[328,640]{1,0:T(8,128)S(1)}, u32[]{:S(2)}, u32[]{:S(2)}) collective-permute-start(f32[328,640]{1,0:T(8,128)} %get-tuple-element.29.refs_0_), channel_id=1, source_target_pairs={{0,6},{1,7},{2,0},{3,1},{4,2},{5,3},{6,4},{7,5},{8,14},{9,15},{10,... | collective-permute-start | bytes 2519048 | tf_op jit(solution)/shard_map/ppermute | solution.py:317
  32.3 0.9 copy-start
  33.2 0.9 copy-start.2
  34.1 22.7 %collective-permute-start.6 = (f32[320,640]{1,0:T(8,128)}, f32[320,640]{1,0:T(8,128)}, u32[]{:S(2)}, u32[]{:S(2)}) collective-permute-start(f32[320,640]{1,0:T(8,128)} %pad_maximum_fusion.refs_0_), channel_id=1, source_target_pairs={{0,24},{1,25},{2,26},{3,27},{4,28},{5,29},{6,30},{7,31},{8,16},{9,... | collective-permute-start | bytes 2457608 | tf_op jit(solution)/shard_map/ppermute | solution.py:317
  41.7 15.2 %copy-start.1 = (f32[320,640]{1,0:T(8,128)S(1)}, f32[320,640]{1,0:T(8,128)}, u32[]{:S(2)}) copy-start(f32[320,640]{1,0:T(8,128)} %copy-done) | copy-start | bytes 2457604
  41.7 15.2 %copy-start.3 = (f32[320,640]{1,0:T(8,128)S(1)}, f32[320,640]{1,0:T(8,128)}, u32[]{:S(2)}) copy-start(f32[320,640]{1,0:T(8,128)} %copy-done.2) | copy-start | bytes 2457604
  69.7 3.1 %collective-permute-start.7 = (f32[320,960]{1,0:T(8,128)S(1)}, f32[320,960]{1,0:T(8,128)S(1)}, u32[]{:S(2)}, u32[]{:S(2)}) collective-permute-start(f32[320,960]{1,0:T(8,128)S(1)} %get-tuple-element.39.refs_1_), channel_id=1, source_target_pairs={{0,1},{1,0},{2,3},{3,2},{4,5},{5,4},{6,7},{7,6},{8,9},{9,8},{10,11... | collective-permute-start | bytes 3686408 | tf_op jit(solution)/shard_map/ppermute | solution.py:320
  72.0 7.1 %collective-permute-start.8 = (f32[320,640]{1,0:T(8,128)S(1)}, f32[320,640]{1,0:T(8,128)S(1)}, u32[]{:S(2)}, u32[]{:S(2)}) collective-permute-start(f32[320,640]{1,0:T(8,128)S(1)} %get-tuple-element.37), channel_id=1, source_target_pairs={{0,1},{1,0},{2,3},{3,2},{4,5},{5,4},{6,7},{7,6},{8,9},{9,8},{10,11... | collective-permute-start | bytes 2457608 | tf_op jit(solution)/shard_map/ppermute | solution.py:320
  72.8 6.3 %copy-start.6 = (f32[640]{0:T(1024)S(1)}, f32[640]{0:T(1024)}, u32[]{:S(2)}) copy-start(f32[640]{0:T(1024)} %param.7) | copy-start | bytes 7684
  75.2 39.7 %collective-permute-start.9 = (f32[320,640]{1,0:T(8,128)S(1)}, f32[320,640]{1,0:T(8,128)S(1)}, u32[]{:S(2)}, u32[]{:S(2)}) collective-permute-start(f32[320,640]{1,0:T(8,128)S(1)} %get-tuple-element.45), channel_id=1, source_target_pairs={{2,4},{3,5},{4,6},{5,7},{6,2},{7,3},{8,14},{9,15},{12,20},{13,21},... | collective-permute-start | bytes 2457608 | tf_op jit(solution)/shard_map/ppermute | solution.py:317
  76.5 38.4 %collective-permute-start.10 = (f32[320,640]{1,0:T(8,128)S(1)}, f32[320,640]{1,0:T(8,128)S(1)}, u32[]{:S(2)}, u32[]{:S(2)}) collective-permute-start(f32[320,640]{1,0:T(8,128)S(1)} %get-tuple-element.46), channel_id=1, source_target_pairs={{2,10},{3,11},{4,2},{5,3},{6,30},{7,31},{8,0},{9,1},{12,8},{13,9},... | collective-permute-start | bytes 2457608 | tf_op jit(solution)/shard_map/ppermute | solution.py:317
  77.8 37.1 %collective-permute-start.11 = (f32[320,640]{1,0:T(8,128)S(1)}, f32[320,640]{1,0:T(8,128)S(1)}, u32[]{:S(2)}, u32[]{:S(2)}) collective-permute-start(f32[320,640]{1,0:T(8,128)S(1)} %get-tuple-element.47), channel_id=1, source_target_pairs={{2,6},{3,7},{4,20},{5,21},{6,4},{7,5},{8,12},{9,13},{12,14},{13,15... | collective-permute-start | bytes 2457608 | tf_op jit(solution)/shard_map/ppermute | solution.py:317
  119.2 4.5 %collective-permute-start.12 = (f32[328,640]{1,0:T(8,128)S(1)}, f32[328,640]{1,0:T(8,128)S(1)}, u32[]{:S(2)}, u32[]{:S(2)}) collective-permute-start(f32[328,640]{1,0:T(8,128)S(1)} %shard_map.77), channel_id=1, source_target_pairs={{0,1},{1,0},{2,3},{3,2},{4,5},{5,4},{6,7},{7,6},{8,9},{9,8},{10,11... | collective-permute-start | bytes 2519048 | tf_op jit(solution)/shard_map/ppermute | solution.py:320
  123.7 4.7 %collective-permute-start.15 = (f32[8,320]{1,0:T(8,128)S(1)}, f32[8,320]{1,0:T(8,128)S(1)}, u32[]{:S(2)}, u32[]{:S(2)}) collective-permute-start(f32[8,320]{1,0:T(8,128)S(1)} %slice_add_fusion.1), channel_id=1, source_target_pairs={{0,24},{1,25},{2,26},{3,27},{4,28},{5,29},{6,30},{7,31},{8,16},{9,... | collective-permute-start | bytes 30728 | tf_op jit(solution)/shard_map/ppermute | solution.py:317
  125.1 3.7 %collective-permute-start.14 = (f32[8,320]{1,0:T(8,128)S(1)}, f32[8,320]{1,0:T(8,128)S(1)}, u32[]{:S(2)}, u32[]{:S(2)}) collective-permute-start(f32[8,320]{1,0:T(8,128)S(1)} %slice_add_fusion.1), channel_id=1, source_target_pairs={{0,16},{1,17},{2,18},{3,19},{4,20},{5,21},{6,22},{7,23},{8,24},{9,... | collective-permute-start | bytes 30728 | tf_op jit(solution)/shard_map/ppermute | solution.py:317
  126.5 3.7 %collective-permute-start.13 = (f32[8,320]{1,0:T(8,128)S(1)}, f32[8,320]{1,0:T(8,128)S(1)}, u32[]{:S(2)}, u32[]{:S(2)}) collective-permute-start(f32[8,320]{1,0:T(8,128)S(1)} %slice_add_fusion.1), channel_id=1, source_target_pairs={{0,8},{1,9},{2,10},{3,11},{4,12},{5,13},{6,14},{7,15},{8,0},{9,1},... | collective-permute-start | bytes 30728 | tf_op jit(solution)/shard_map/ppermute | solution.py:317

commit v7 on v6

--- a/solution.py
+++ b/solution.py
@@ -36,7 +36,7 @@
     return lax.dot_general(a, b, (contract, ((), ())), preferred_element_type=jnp.float32)
 
 
-def call(kernel, outs, ids, *arrays, placed=0, scratch=()):
+def call(kernel, outs, ids, *arrays, placed=0, scratch=(), waits=False):
     pieces, held, homes = [], [], []
     for array in arrays[: len(arrays) - placed]:
         array = array if isinstance(array, list) else [array]
@@ -57,9 +57,16 @@
             copies.append(pltpu.make_async_copy(source, target, sems.at[i]))
         for copy in copies:
             copy.start()
-        for copy in copies:
-            copy.wait()
-        kernel(ids_ref, *targets, *rest, *own)
+
+        def arrive():
+            for copy in copies:
+                copy.wait()
+
+        if waits:
+            kernel(arrive, ids_ref, *targets, *rest, *own)
+        else:
+            arrive()
+            kernel(ids_ref, *targets, *rest, *own)
 
     return pl.pallas_call(
         body,
@@ -87,12 +94,13 @@
     dims = [wide, wide]
     dims[entry] = count * BLK
     entries = lax.broadcasted_iota(jnp.int32, dims, entry)
-    return (entries // BLK == lax.broadcasted_iota(jnp.int32, dims, 1 - entry)).astype(jnp.bfloat16)
+    return (lax.shift_right_logical(entries, BLK.bit_length() - 1) == lax.broadcasted_iota(jnp.int32, dims, 1 - entry)).astype(jnp.bfloat16)
 
 
 def spread(blocks, half, height):
-    rows = dot(ones(half // BLK, blocks.shape[0], 0), blocks.astype(jnp.bfloat16))
-    return dot(rows.astype(jnp.bfloat16), ones(height // BLK, blocks.shape[1], 1))
+    wide = -(-height // BLK // 16) * 16
+    rows = dot(ones(half // BLK, blocks.shape[0], 0), blocks[:, :wide].astype(jnp.bfloat16))
+    return dot(rows.astype(jnp.bfloat16), ones(height // BLK, wide, 1))
 
 
 def pack_kernel(core, tile, pattern, packed, mine, other, blocks):
@@ -125,17 +133,19 @@
     return [pltpu.VMEM((count, half, 3 * half), jnp.bfloat16), pltpu.SemaphoreType.DMA((count,))]
 
 
-def fetch(sources, held, sems):
+def fetch(sources, held, sems, arrive=None):
     copies = [pltpu.make_async_copy(source, held.at[t], sems.at[t]) for t, source in enumerate(sources)]
     for copy in copies:
         copy.start()
+    if arrive is not None:
+        arrive()
     for copy in copies:
         copy.wait()
 
 
-def sums_of_products(places, lefts, starts, rights, held, sems):
+def sums_of_products(arrive, places, lefts, starts, rights, held, sems):
     half, count = held.shape[1], len(lefts)
-    fetch([right.at[place] for right in rights for place in places], held, sems)
+    fetch([right.at[place] for right in rights for place in places], held, sems, arrive)
     totals = [None if start is None else start[...] for start in starts]
     for j, left in enumerate(lefts):
         value = second(left[:half, :], 0)
@@ -145,18 +155,18 @@
     return totals
 
 
-def early_products_kernel(early, line_at, ids, *refs):
+def early_products_kernel(early, line_at, arrive, ids, *refs):
     count = len(early)
     lefts, rights, outs, (held, sems) = refs[:count], refs[count : count + 2], refs[count + 2 : count + 4], refs[count + 4 :]
     places = [ids[line_at + j] for j in early]
-    for out, total in zip(outs, sums_of_products(places, lefts, [None, None], rights, held, sems)):
+    for out, total in zip(outs, sums_of_products(arrive, places, lefts, [None, None], rights, held, sems)):
         out[...] = total
 
 
-def last_product_kernel(place, ids, left, start_kept, start_given, right_kept, right_given, kept, given, held, sems):
+def last_product_kernel(place, arrive, ids, left, start_kept, start_given, right_kept, right_given, kept, given, held, sems):
     height = kept.shape[1]
     starts = [start_kept, start_given]
-    kept_sum, given_sum = sums_of_products([ids[place]], [left], starts, [right_kept, right_given], held, sems)
+    kept_sum, given_sum = sums_of_products(arrive, [ids[place]], [left], starts, [right_kept, right_given], held, sems)
     kept[...] = kept_sum
     given[:, :height] = given_sum
     given[:, height:] = in_half(kept_sum, 1 - ids[CORE])
@@ -193,7 +203,7 @@
     return jnp.where(lax.broadcasted_iota(jnp.int32, value.shape, 0) == row, value, 0.0)
 
 
-def last_kernel(count, place, is_kept, ids, start, weights, *refs):
+def last_kernel(count, place, is_kept, arrive, ids, start, weights, *refs):
     if is_kept:
         square, blocks, *refs = refs
     right, *refs = refs
@@ -209,9 +219,8 @@
 
     if not is_kept:
         blocks, sem = refs
-        copy = pltpu.make_async_copy(theirs.at[half:, :LANES], blocks, sem)
-        copy.start()
-        copy.wait()
+        blocks_copy = pltpu.make_async_copy(theirs.at[half:, :LANES], blocks, sem)
+        blocks_copy.start()
     for t in range(count):
 
         @pl.when(ids[place + t] >= 0)
@@ -219,6 +228,7 @@
             for copy in copies(t):
                 copy.start()
 
+    arrive()
     out[:half, :] = start[...]
     for t in range(count):
 
@@ -230,6 +240,8 @@
 
     out[half:, :] = jnp.zeros((ROWS, height), jnp.float32)
     out[half:, :half] = in_row(check_sums(weights, out[:half, :]), 1)
+    if not is_kept:
+        blocks_copy.wait()
     cube_term = spread(blocks[...], half, height) * out[:half, :]
     out[:half, :] = 3.0 * square[...] - 2.0 * cube_term if is_kept else -2.0 * cube_term
 
@@ -375,6 +387,7 @@
             given,
             placed=2,
             scratch=held_parts(2 * len(early), half),
+            waits=True,
         )
         diagonal_start = call(diagonal_early_kernel, shape(height, height), ids, *[left[j] for j in early])
         kept_sum, given_sum = call(
@@ -388,6 +401,7 @@
             given,
             placed=2,
             scratch=held_parts(2, half),
+            waits=True,
         )
         diagonal_given, diagonal_kept, diagonal_blocks = call(
             diagonal_kernel,
@@ -450,6 +464,7 @@
             theirs,
             *arrived,
             placed=steps + 2,
+            waits=True,
             scratch=scratch + [pltpu.VMEM((ROWS, LANES), jnp.float32), pltpu.SemaphoreType.DMA],
         )
         kept_cube = call(
@@ -463,6 +478,7 @@
             kept,
             *arrived,
             placed=steps + 1,
+            waits=True,
             scratch=scratch,
         )
         received = swap_core(given_cube)

time: 131 us -> 131 us (level)
  transfers between devices with their start and end apart: 16 -> 16, of which waited for: 8 -> 8; matrix products, arithmetic and copies ran while one was open for 6% -> 6% of each run, Pallas kernels for 21% -> 20%
where the time goes in v7:
time: 131 us
  waiting for transfers between devices  62.8 us (48%)
  Pallas kernels  35 us (27%)
  starting transfers between devices  20.8 us (16%)
  local copies, waits for them, and re-layouts  8.82 us (7%)
  other arithmetic  2.67 us (2%)
    ppermute x12, waiting for transfers between devices, send(): return lax.ppermute(value, ('row', 'col'), pairs)  62.6 us
    pallas_call x10, Pallas kernels, call(): pl.pallas_call(body, out_shape=outs, in_specs=[pl.BlockSpec(memory_space=...  35 us
    ppermute x12, starting transfers between devices, send(): return lax.ppermute(value, ('row', 'col'), pairs)  19.6 us
    unnamed x14, local copies, waits for them, and re-layouts  3.66 us
  transfers between devices with their start and end apart: 16, of which 8 were waited for; matrix products, arithmetic and copies ran while one was open for 6% of the time, Pallas kernels for 20%

profile of v7, /device:TPU:0, one launch (start us, length us, event | category | flops | bytes accessed | tf_op | source)
XLA Modules:
  0.0 131.0 jit_solution(8580938783093982815)
XLA Ops:
  2.5 1.3 %shard_map.68 = (f32[328,640]{1,0:T(8,128)}, f32[320,320]{1,0:T(8,128)S(1)}, f32[328,320]{1,0:T(8,128)S(1)}, f32[8,128]{1,0:T(8,128)S(1)}) custom-call(s32[1]{0:T(128)} %bitcast.ids_ref, f32[320,640]{1,0:T(8,128)S(1)} %bitcast.19, s32[5,10]{1,0:T(8,128)S(1)} %bitcast.20), custom_call_target="tpu_custom_call" | custom-call | tf_op jit(solution)/shard_map/pallas_call | solution.py:71
  4.3 2.6 %collective-permute-start.2 = (f32[328,640]{1,0:T(8,128)}, f32[328,640]{1,0:T(8,128)S(1)}, u32[]{:S(2)}, u32[]{:S(2)}) collective-permute-start(f32[328,640]{1,0:T(8,128)} %get-tuple-element.29.refs_0_), channel_id=1, source_target_pairs={{0,2},{1,3},{2,4},{3,5},{4,6},{5,7},{6,0},{7,1},{8,10},{9,11},{10,... | collective-permute-start | bytes 2519048 | tf_op jit(solution)/shard_map/ppermute | solution.py:329
  8.1 1.7 %collective-permute-start.4 = (f32[320,640]{1,0:T(8,128)}, f32[320,640]{1,0:T(8,128)S(1)}, u32[]{:S(2)}, u32[]{:S(2)}) collective-permute-start(f32[320,640]{1,0:T(8,128)} %pad_maximum_fusion.refs_0_), channel_id=1, source_target_pairs={{0,8},{1,9},{2,10},{3,11},{4,12},{5,13},{6,14},{7,15},{8,0},{9,1},... | collective-permute-start | bytes 2457608 | tf_op jit(solution)/shard_map/ppermute | solution.py:329
  9.8 1.5 %collective-permute-start.5 = (f32[320,640]{1,0:T(8,128)}, f32[320,640]{1,0:T(8,128)S(1)}, u32[]{:S(2)}, u32[]{:S(2)}) collective-permute-start(f32[320,640]{1,0:T(8,128)} %pad_maximum_fusion.refs_0_), channel_id=1, source_target_pairs={{0,16},{1,17},{2,18},{3,19},{4,20},{5,21},{6,22},{7,23},{8,24},{9,... | collective-permute-start | bytes 2457608 | tf_op jit(solution)/shard_map/ppermute | solution.py:329
  11.3 17.1 %collective-permute-done.2.refs_1_.refs_2_ = f32[328,640]{1,0:T(8,128)S(1)} collective-permute-done((f32[328,640]{1,0:T(8,128)}, f32[328,640]{1,0:T(8,128)S(1)}, u32[]{:S(2)}, u32[]{:S(2)}) %collective-permute-start.2) | collective-permute-done | bytes 839712 | tf_op jit(solution)/shard_map/ppermute | solution.py:329
  28.5 3.8 %collective-permute-start.1 = (f32[328,640]{1,0:T(8,128)}, f32[328,640]{1,0:T(8,128)S(1)}, u32[]{:S(2)}, u32[]{:S(2)}) collective-permute-start(f32[328,640]{1,0:T(8,128)} %get-tuple-element.29.refs_0_), channel_id=1, source_target_pairs={{0,6},{1,7},{2,0},{3,1},{4,2},{5,3},{6,4},{7,5},{8,14},{9,15},{10,... | collective-permute-start | bytes 2519048 | tf_op jit(solution)/shard_map/ppermute | solution.py:329
  34.1 2.4 %collective-permute-start.6 = (f32[320,640]{1,0:T(8,128)}, f32[320,640]{1,0:T(8,128)}, u32[]{:S(2)}, u32[]{:S(2)}) collective-permute-start(f32[320,640]{1,0:T(8,128)} %pad_maximum_fusion.refs_0_), channel_id=1, source_target_pairs={{0,24},{1,25},{2,26},{3,27},{4,28},{5,29},{6,30},{7,31},{8,16},{9,... | collective-permute-start | bytes 2457608 | tf_op jit(solution)/shard_map/ppermute | solution.py:329
  39.2 2.5 %stack.48.ids_ref = s32[16]{0:T(128)S(1)} concatenate(s32[1]{0:T(128)} %bitcast.ids_ref, s32[1]{0:T(128)} %bitcast.1, s32[1]{0:T(128)} %bitcast.2, s32[1]{0:T(128)} %bitcast.3, s32[1]{0:T(128)} %bitcast.4, s32[1]{0:T(128)} %bitcast.2, s32[1]{0:T(128)} %bitcast.5, s32[1]{0:T(128)} %bitcast.6, s32[1]{0:T(128)} %bitcast.7, s32[1]{0:T(128)} %bitcast.8, s32[1]{0:T(128)} %bitcast.9, ...), dimensions={0} | concatenate | bytes 128 | tf_op jit(solution)/shard_map/stack | solution.py:355
  41.7 10.1 %collective-permute-done.3.refs_2_.refs_3_ = f32[328,640]{1,0:T(8,128)S(1)} collective-permute-done((f32[328,640]{1,0:T(8,128)S(1)}, f32[328,640]{1,0:T(8,128)S(1)}, u32[]{:S(2)}, u32[]{:S(2)}) %collective-permute-start.3) | collective-permute-done | bytes 839712 | tf_op jit(solution)/shard_map/ppermute | solution.py:329
  51.9 5.0 %shard_map.71.refs_0_ = f32[640,640]{1,0:T(8,128)S(1)} custom-call(s32[16]{0:T(128)S(1)} %stack.48.ids_ref, f32[328,640]{1,0:T(8,128)} %get-tuple-element.29.refs_0_, f32[328,640]{1,0:T(8,128)S(1)} %collective-permute-done.2.refs_1_.refs_2_, f32[328,640]{1,0:T(8,128)S(1)} %collective-permute-done.3.refs_2_.refs_3_), custom_call_target="tpu_custom_call" | custom-call | tf_op jit(solution)/shard_map/pallas_call | solution.py:71
  56.9 2.9 %shard_map.69 = (bf16[4,320,960]{2,1,0:T(8,128)(2,1)S(1)}, bf16[4,320,960]{2,1,0:T(8,128)(2,1)S(1)}) custom-call(s32[16]{0:T(128)S(1)} %stack.48.ids_ref, f32[320,640]{1,0:T(8,128)} %pad_maximum_fusion.refs_0_, f32[320,640]{1,0:T(8,128)S(1)} %copy-done.1, f32[320,640]{1,0:T(8,128)S(1)} %copy-done.3, f32[320,640]{1,0:T(8,128)} %collective-permute-done.6.refs_3_), custom_call_target="tpu_custom_call" | custom-call | tf_op jit(solution)/shard_map/pallas_call | solution.py:71
  59.8 5.3 %shard_map.70 = (f32[320,640]{1,0:T(8,128)S(1)}, f32[320,640]{1,0:T(8,128)S(1)}) custom-call(s32[16]{0:T(128)S(1)} %stack.48.ids_ref, f32[328,640]{1,0:T(8,128)} %get-tuple-element.29.refs_0_, f32[328,640]{1,0:T(8,128)S(1)} %collective-permute-done.2.refs_1_.refs_2_, f32[328,640]{1,0:T(8,128)S(1)} %collective-permute-done.3.refs_2_.refs_3_, ...), custom_call_target="tpu_custom_call" | custom-call | tf_op jit(solution)/shard_map/pallas_call | solution.py:71
  65.2 2.0 %collective-permute-done.1.refs_0_.refs_1_.refs_4_ = f32[328,640]{1,0:T(8,128)S(1)} collective-permute-done((f32[328,640]{1,0:T(8,128)}, f32[328,640]{1,0:T(8,128)S(1)}, u32[]{:S(2)}, u32[]{:S(2)}) %collective-permute-start.1) | collective-permute-done | bytes 839712 | tf_op jit(solution)/shard_map/ppermute | solution.py:329
  67.1 2.5 %shard_map.72 = (f32[320,640]{1,0:T(8,128)S(1)}, f32[320,960]{1,0:T(8,128)S(1)}) custom-call(s32[16]{0:T(128)S(1)} %stack.48.ids_ref, f32[328,640]{1,0:T(8,128)S(1)} %collective-permute-done.1.refs_0_.refs_1_.refs_4_, f32[320,640]{1,0:T(8,128)S(1)} %get-tuple-element.34.refs_1_, f32[320,640]{1,0:T(8,128)S(1)} %get-tuple-element.35.refs_2_, ...), custom_call_target="tpu_custom_call" | custom-call | tf_op jit(solution)/shard_map/pallas_call | solution.py:71
  69.8 2.2 %shard_map.73 = (f32[320,640]{1,0:T(8,128)S(1)}, f32[320,640]{1,0:T(8,128)S(1)}, f32[8,128]{1,0:T(8,128)S(1)}) custom-call(s32[16]{0:T(128)S(1)} %stack.48.ids_ref, f32[640,640]{1,0:T(8,128)S(1)} %shard_map.71.refs_0_, f32[328,640]{1,0:T(8,128)S(1)} %collective-permute-done.1.refs_0_.refs_1_.refs_4_, f32[328,640]{1,0:T(8,128)S(1)} %collective-permute-done.2.refs_1_.refs_2_, ...), custom_call_target="tpu_custom_call" | custom-call | tf_op jit(solution)/shard_map/pallas_call | solution.py:71
  72.8 2.4 %shard_map.74 = (f32[320,640]{1,0:T(8,128)S(1)}, f32[320,640]{1,0:T(8,128)S(1)}, f32[320,640]{1,0:T(8,128)S(1)}, f32[320,640]{1,0:T(8,128)S(1)}) custom-call(s32[16]{0:T(128)S(1)} %stack.48.ids_ref, f32[320,640]{1,0:T(8,128)S(1)} %get-tuple-element.38.refs_0_.refs_4_, f32[320,960]{1,0:T(8,128)S(1)} %get-tuple-element.39.refs_1_, ...), custom_call_target="tpu_custom_call" | custom-call | tf_op jit(solution)/shard_map/pallas_call | solution.py:71
  75.2 1.3 collective-permute-start.9
  79.2 4.5 %shard_map.75 = (f32[320,640]{1,0:T(8,128)S(1)}, f32[320,640]{1,0:T(8,128)S(1)}, f32[8,320]{1,0:T(8,128)S(1)}) custom-call(s32[16]{0:T(128)S(1)} %stack.48.ids_ref, f32[320,640]{1,0:T(8,128)S(1)} %get-tuple-element.41.refs_0_.refs_2_, f32[320,640]{1,0:T(8,128)S(1)} %get-tuple-element.42.refs_1_, f32[320,640]{1,0:T(8,128)S(1)} %collective-permute-done.8.refs_2_, ...), custom_call_target="tpu_custom_call" | custom-call | tf_op jit(solution)/shard_map/pallas_call | solution.py:71
  83.7 31.3 %collective-permute-done.9.refs_5_.refs_4_ = f32[320,640]{1,0:T(8,128)S(1)} collective-permute-done((f32[320,640]{1,0:T(8,128)S(1)}, f32[320,640]{1,0:T(8,128)S(1)}, u32[]{:S(2)}, u32[]{:S(2)}) %collective-permute-start.9) | collective-permute-done | bytes 819232 | tf_op jit(solution)/shard_map/ppermute | solution.py:329
  115.0 4.4 %shard_map.77 = f32[328,640]{1,0:T(8,128)S(1)} custom-call(s32[16]{0:T(128)S(1)} %stack.48.ids_ref, f32[320,640]{1,0:T(8,128)S(1)} %get-tuple-element.48.refs_0_, f32[1,640]{1,0:T(1,128)S(1)} %broadcast_in_dim.2.refs_6_.refs_1_, bf16[4,320,960]{2,1,0:T(8,128)(2,1)S(1)} %get-tuple-element.32.refs_4_.refs_8_.refs_2_, ...), custom_call_target="tpu_custom_call" | custom-call | tf_op jit(solution)/shard_map/pallas_call | solution.py:71
  119.5 4.4 %shard_map.76 = f32[328,640]{1,0:T(8,128)S(1)} custom-call(s32[16]{0:T(128)S(1)} %stack.48.ids_ref, f32[320,640]{1,0:T(8,128)S(1)} %get-tuple-element.44.refs_0_, f32[1,640]{1,0:T(1,128)S(1)} %broadcast_in_dim.2.refs_6_.refs_1_, f32[320,640]{1,0:T(8,128)S(1)} %get-tuple-element.41.refs_0_.refs_2_, f32[8,128]{1,0:T(8,128)S(1)} %get-tuple-element.40.refs_3_, ...), custom_call_target="tpu_custom_call" | custom-call | tf_op jit(solution)/shard_map/pallas_call | solution.py:71
  123.9 1.4 %collective-permute-start.15 = (f32[8,320]{1,0:T(8,128)S(1)}, f32[8,320]{1,0:T(8,128)S(1)}, u32[]{:S(2)}, u32[]{:S(2)}) collective-permute-start(f32[8,320]{1,0:T(8,128)S(1)} %slice_add_fusion.1), channel_id=1, source_target_pairs={{0,24},{1,25},{2,26},{3,27},{4,28},{5,29},{6,30},{7,31},{8,16},{9,... | collective-permute-start | bytes 30728 | tf_op jit(solution)/shard_map/ppermute | solution.py:329
  125.3 1.4 %collective-permute-start.14 = (f32[8,320]{1,0:T(8,128)S(1)}, f32[8,320]{1,0:T(8,128)S(1)}, u32[]{:S(2)}, u32[]{:S(2)}) collective-permute-start(f32[8,320]{1,0:T(8,128)S(1)} %slice_add_fusion.1), channel_id=1, source_target_pairs={{0,16},{1,17},{2,18},{3,19},{4,20},{5,21},{6,22},{7,23},{8,24},{9,... | collective-permute-start | bytes 30728 | tf_op jit(solution)/shard_map/ppermute | solution.py:329
  129.0 1.4 %collective-permute-done.13 = f32[8,320]{1,0:T(8,128)S(1)} collective-permute-done((f32[8,320]{1,0:T(8,128)S(1)}, f32[8,320]{1,0:T(8,128)S(1)}, u32[]{:S(2)}, u32[]{:S(2)}) %collective-permute-start.13) | collective-permute-done | bytes 10272 | tf_op jit(solution)/shard_map/ppermute | solution.py:329
  (42 shorter events, 14.3 us)
Async XLA Ops:
  0.6 1.1 copy-start.4
  1.8 0.7 copy-start.5
  3.8 3.2 %collective-permute-start = (f32[328,320]{1,0:T(8,128)S(1)}, f32[328,320]{1,0:T(8,128)S(1)}, u32[]{:S(2)}, u32[]{:S(2)}) collective-permute-start(f32[328,320]{1,0:T(8,128)S(1)} %get-tuple-element.28), channel_id=1, source_target_pairs={{0,1},{1,0},{2,3},{3,2},{4,5},{5,4},{6,7},{7,6},{8,9},{9,8},{10,11... | collective-permute-start | bytes 1259528 | tf_op jit(solution)/shard_map/ppermute | solution.py:332
  4.3 24.2 %collective-permute-start.2 = (f32[328,640]{1,0:T(8,128)}, f32[328,640]{1,0:T(8,128)S(1)}, u32[]{:S(2)}, u32[]{:S(2)}) collective-permute-start(f32[328,640]{1,0:T(8,128)} %get-tuple-element.29.refs_0_), channel_id=1, source_target_pairs={{0,2},{1,3},{2,4},{3,5},{4,6},{5,7},{6,0},{7,1},{8,10},{9,11},{10,... | collective-permute-start | bytes 2519048 | tf_op jit(solution)/shard_map/ppermute | solution.py:329
  8.1 24.2 %collective-permute-start.4 = (f32[320,640]{1,0:T(8,128)}, f32[320,640]{1,0:T(8,128)S(1)}, u32[]{:S(2)}, u32[]{:S(2)}) collective-permute-start(f32[320,640]{1,0:T(8,128)} %pad_maximum_fusion.refs_0_), channel_id=1, source_target_pairs={{0,8},{1,9},{2,10},{3,11},{4,12},{5,13},{6,14},{7,15},{8,0},{9,1},... | collective-permute-start | bytes 2457608 | tf_op jit(solution)/shard_map/ppermute | solution.py:329
  9.8 23.4 %collective-permute-start.5 = (f32[320,640]{1,0:T(8,128)}, f32[320,640]{1,0:T(8,128)S(1)}, u32[]{:S(2)}, u32[]{:S(2)}) collective-permute-start(f32[320,640]{1,0:T(8,128)} %pad_maximum_fusion.refs_0_), channel_id=1, source_target_pairs={{0,16},{1,17},{2,18},{3,19},{4,20},{5,21},{6,22},{7,23},{8,24},{9,... | collective-permute-start | bytes 2457608 | tf_op jit(solution)/shard_map/ppermute | solution.py:329
  28.5 23.4 %collective-permute-start.3 = (f32[328,640]{1,0:T(8,128)S(1)}, f32[328,640]{1,0:T(8,128)S(1)}, u32[]{:S(2)}, u32[]{:S(2)}) collective-permute-start(f32[328,640]{1,0:T(8,128)S(1)} %collective-permute-done.2.refs_1_.refs_2_), channel_id=1, source_target_pairs={{0,2},{1,3},{2,4},{3,5},{4,6},{5,7},{6,0},{7,1},{8,10},{9,11},{10,... | collective-permute-start | bytes 2519048 | tf_op jit(solution)/shard_map/ppermute | solution.py:329
  28.5 38.7 %collective-permute-start.1 = (f32[328,640]{1,0:T(8,128)}, f32[328,640]{1,0:T(8,128)S(1)}, u32[]{:S(2)}, u32[]{:S(2)}) collective-permute-start(f32[328,640]{1,0:T(8,128)} %get-tuple-element.29.refs_0_), channel_id=1, source_target_pairs={{0,6},{1,7},{2,0},{3,1},{4,2},{5,3},{6,4},{7,5},{8,14},{9,15},{10,... | collective-permute-start | bytes 2519048 | tf_op jit(solution)/shard_map/ppermute | solution.py:329
  32.3 0.9 copy-start
  33.2 0.9 copy-start.2
  34.1 22.7 %collective-permute-start.6 = (f32[320,640]{1,0:T(8,128)}, f32[320,640]{1,0:T(8,128)}, u32[]{:S(2)}, u32[]{:S(2)}) collective-permute-start(f32[320,640]{1,0:T(8,128)} %pad_maximum_fusion.refs_0_), channel_id=1, source_target_pairs={{0,24},{1,25},{2,26},{3,27},{4,28},{5,29},{6,30},{7,31},{8,16},{9,... | collective-permute-start | bytes 2457608 | tf_op jit(solution)/shard_map/ppermute | solution.py:329
  41.7 15.2 %copy-start.1 = (f32[320,640]{1,0:T(8,128)S(1)}, f32[320,640]{1,0:T(8,128)}, u32[]{:S(2)}) copy-start(f32[320,640]{1,0:T(8,128)} %copy-done) | copy-start | bytes 2457604
  41.7 15.2 %copy-start.3 = (f32[320,640]{1,0:T(8,128)S(1)}, f32[320,640]{1,0:T(8,128)}, u32[]{:S(2)}) copy-start(f32[320,640]{1,0:T(8,128)} %copy-done.2) | copy-start | bytes 2457604
  69.7 3.1 %collective-permute-start.7 = (f32[320,960]{1,0:T(8,128)S(1)}, f32[320,960]{1,0:T(8,128)S(1)}, u32[]{:S(2)}, u32[]{:S(2)}) collective-permute-start(f32[320,960]{1,0:T(8,128)S(1)} %get-tuple-element.39.refs_1_), channel_id=1, source_target_pairs={{0,1},{1,0},{2,3},{3,2},{4,5},{5,4},{6,7},{7,6},{8,9},{9,8},{10,11... | collective-permute-start | bytes 3686408 | tf_op jit(solution)/shard_map/ppermute | solution.py:332
  72.0 7.2 %collective-permute-start.8 = (f32[320,640]{1,0:T(8,128)S(1)}, f32[320,640]{1,0:T(8,128)S(1)}, u32[]{:S(2)}, u32[]{:S(2)}) collective-permute-start(f32[320,640]{1,0:T(8,128)S(1)} %get-tuple-element.37), channel_id=1, source_target_pairs={{0,1},{1,0},{2,3},{3,2},{4,5},{5,4},{6,7},{7,6},{8,9},{9,8},{10,11... | collective-permute-start | bytes 2457608 | tf_op jit(solution)/shard_map/ppermute | solution.py:332
  72.8 6.4 %copy-start.6 = (f32[640]{0:T(1024)S(1)}, f32[640]{0:T(1024)}, u32[]{:S(2)}) copy-start(f32[640]{0:T(1024)} %param.7) | copy-start | bytes 7684
  75.2 39.7 %collective-permute-start.9 = (f32[320,640]{1,0:T(8,128)S(1)}, f32[320,640]{1,0:T(8,128)S(1)}, u32[]{:S(2)}, u32[]{:S(2)}) collective-permute-start(f32[320,640]{1,0:T(8,128)S(1)} %get-tuple-element.45), channel_id=1, source_target_pairs={{2,4},{3,5},{4,6},{5,7},{6,2},{7,3},{8,14},{9,15},{12,20},{13,21},... | collective-permute-start | bytes 2457608 | tf_op jit(solution)/shard_map/ppermute | solution.py:329
  76.5 38.4 %collective-permute-start.10 = (f32[320,640]{1,0:T(8,128)S(1)}, f32[320,640]{1,0:T(8,128)S(1)}, u32[]{:S(2)}, u32[]{:S(2)}) collective-permute-start(f32[320,640]{1,0:T(8,128)S(1)} %get-tuple-element.46), channel_id=1, source_target_pairs={{2,10},{3,11},{4,2},{5,3},{6,30},{7,31},{8,0},{9,1},{12,8},{13,9},... | collective-permute-start | bytes 2457608 | tf_op jit(solution)/shard_map/ppermute | solution.py:329
  77.8 37.1 %collective-permute-start.11 = (f32[320,640]{1,0:T(8,128)S(1)}, f32[320,640]{1,0:T(8,128)S(1)}, u32[]{:S(2)}, u32[]{:S(2)}) collective-permute-start(f32[320,640]{1,0:T(8,128)S(1)} %get-tuple-element.47), channel_id=1, source_target_pairs={{2,6},{3,7},{4,20},{5,21},{6,4},{7,5},{8,12},{9,13},{12,14},{13,15... | collective-permute-start | bytes 2457608 | tf_op jit(solution)/shard_map/ppermute | solution.py:329
  119.4 4.5 %collective-permute-start.12 = (f32[328,640]{1,0:T(8,128)S(1)}, f32[328,640]{1,0:T(8,128)S(1)}, u32[]{:S(2)}, u32[]{:S(2)}) collective-permute-start(f32[328,640]{1,0:T(8,128)S(1)} %shard_map.77), channel_id=1, source_target_pairs={{0,1},{1,0},{2,3},{3,2},{4,5},{5,4},{6,7},{7,6},{8,9},{9,8},{10,11... | collective-permute-start | bytes 2519048 | tf_op jit(solution)/shard_map/ppermute | solution.py:332
  123.9 4.7 %collective-permute-start.15 = (f32[8,320]{1,0:T(8,128)S(1)}, f32[8,320]{1,0:T(8,128)S(1)}, u32[]{:S(2)}, u32[]{:S(2)}) collective-permute-start(f32[8,320]{1,0:T(8,128)S(1)} %slice_add_fusion.1), channel_id=1, source_target_pairs={{0,24},{1,25},{2,26},{3,27},{4,28},{5,29},{6,30},{7,31},{8,16},{9,... | collective-permute-start | bytes 30728 | tf_op jit(solution)/shard_map/ppermute | solution.py:329
  125.3 3.7 %collective-permute-start.14 = (f32[8,320]{1,0:T(8,128)S(1)}, f32[8,320]{1,0:T(8,128)S(1)}, u32[]{:S(2)}, u32[]{:S(2)}) collective-permute-start(f32[8,320]{1,0:T(8,128)S(1)} %slice_add_fusion.1), channel_id=1, source_target_pairs={{0,16},{1,17},{2,18},{3,19},{4,20},{5,21},{6,22},{7,23},{8,24},{9,... | collective-permute-start | bytes 30728 | tf_op jit(solution)/shard_map/ppermute | solution.py:329
  126.7 3.7 %collective-permute-start.13 = (f32[8,320]{1,0:T(8,128)S(1)}, f32[8,320]{1,0:T(8,128)S(1)}, u32[]{:S(2)}, u32[]{:S(2)}) collective-permute-start(f32[8,320]{1,0:T(8,128)S(1)} %slice_add_fusion.1), channel_id=1, source_target_pairs={{0,8},{1,9},{2,10},{3,11},{4,12},{5,13},{6,14},{7,15},{8,0},{9,1},... | collective-permute-start | bytes 30728 | tf_op jit(solution)/shard_map/ppermute | solution.py:329

commit v8 on v7

--- a/solution.py
+++ b/solution.py
@@ -201,6 +201,23 @@
 
 def in_row(value, row):
     return jnp.where(lax.broadcasted_iota(jnp.int32, value.shape, 0) == row, value, 0.0)
+
+
+def middle_kernel(place, ids, tile, *refs):
+    starts, rights, outs, (held, sems) = refs[:2], refs[2:4], refs[4:6], refs[6:]
+    k = ids[place]
+    fetch([right.at[jnp.maximum(k, 0)] for right in rights], held, sems)
+
+    @pl.when(k >= 0)
+    def _():
+        value = second(tile[...], 0)
+        for s, (out, start) in enumerate(zip(outs, starts)):
+            out[...] = start[...] + dot(held[s], value)
+
+    @pl.when(k < 0)
+    def _():
+        for out, start in zip(outs, starts):
+            out[...] = start[...]
 
 
 def last_kernel(count, place, is_kept, arrive, ids, start, weights, *refs):
@@ -449,11 +466,23 @@
             scratch=held_parts(4, half),
         )
 
-        held = [pltpu.VMEM((steps, half, height), jnp.float32), pltpu.SemaphoreType.DMA((steps,))]
-
-        kernel = functools.partial(last_kernel, steps, steps_at)
+        cube = call(
+            functools.partial(middle_kernel, steps_at),
+            [shape(half, height)] * 2,
+            ids,
+            arrived[0],
+            *cube,
+            kept,
+            given,
+            placed=2,
+            scratch=held_parts(2, half),
+        )
+        steps_at, steps_left, arrived = steps_at + 1, steps - 1, arrived[1:]
+        held = [pltpu.VMEM((steps_left, half, height), jnp.float32), pltpu.SemaphoreType.DMA((steps_left,))]
+
+        kernel = functools.partial(last_kernel, steps_left, steps_at)
         out = shape(half + ROWS, height)
-        scratch = held_parts(steps, half) + held
+        scratch = held_parts(steps_left, half) + held
         given_cube = call(
             functools.partial(kernel, False),
             out,
@@ -463,7 +492,7 @@
             given,
             theirs,
             *arrived,
-            placed=steps + 2,
+            placed=steps_left + 2,
             waits=True,
             scratch=scratch + [pltpu.VMEM((ROWS, LANES), jnp.float32), pltpu.SemaphoreType.DMA],
         )
@@ -477,7 +506,7 @@
             blocks,
             kept,
             *arrived,
-            placed=steps + 1,
+            placed=steps_left + 1,
             waits=True,
             scratch=scratch,
         )

time: 131 us -> 131 us (level)
  waiting for transfers between devices: 62.8 us -> 61.3 us
    ppermute x12, waiting for transfers between devices: 62.6 us -> 61.1 us  [send(): return lax.ppermute(value, ('row', 'col'), pairs)]
    pallas_call x10 -> x11, Pallas kernels: 35 us -> 35.5 us  [call(): pl.pallas_call(body, out_shape=outs, in_specs=[pl.BlockSpec(memory_space=...]
  transfers between devices with their start and end apart: 16 -> 16, of which waited for: 8 -> 7; matrix products, arithmetic and copies ran while one was open for 6% -> 6% of each run, Pallas kernels for 20% -> 22%
where the time goes in v8:
time: 131 us; the launch traced here: 130 us
  waiting for transfers between devices  61.3 us (47%)
  Pallas kernels  35.5 us (27%)
  starting transfers between devices  20.8 us (16%)
  local copies, waits for them, and re-layouts  8.95 us (7%)
  other arithmetic  2.69 us (2%)
    ppermute x12, waiting for transfers between devices, send(): return lax.ppermute(value, ('row', 'col'), pairs)  61.1 us
    pallas_call x11, Pallas kernels, call(): pl.pallas_call(body, out_shape=outs, in_specs=[pl.BlockSpec(memory_space=...  35.5 us
    ppermute x12, starting transfers between devices, send(): return lax.ppermute(value, ('row', 'col'), pairs)  19.6 us
    unnamed x14, local copies, waits for them, and re-layouts  3.66 us
    another operation x1, local copies, waits for them, and re-layouts, body(): ids = jnp.stack([jnp.asarray(s, jnp.int32) for s in scalars])  2.64 us
  transfers between devices with their start and end apart: 16, of which 7 were waited for; matrix products, arithmetic and copies ran while one was open for 6% of the time, Pallas kernels for 22%

profile of v8, /device:TPU:0, one launch (start us, length us, event | category | flops | bytes accessed | tf_op | source)
XLA Modules:
  0.0 130.1 jit_solution(17156466555673816354)
XLA Ops:
  2.5 1.3 %shard_map.68 = (f32[328,640]{1,0:T(8,128)}, f32[320,320]{1,0:T(8,128)S(1)}, f32[328,320]{1,0:T(8,128)S(1)}, f32[8,128]{1,0:T(8,128)S(1)}) custom-call(s32[1]{0:T(128)} %bitcast.ids_ref, f32[320,640]{1,0:T(8,128)S(1)} %bitcast.19, s32[5,10]{1,0:T(8,128)S(1)} %bitcast.20), custom_call_target="tpu_custom_call" | custom-call | tf_op jit(solution)/shard_map/pallas_call | solution.py:71
  4.3 2.6 %collective-permute-start.2 = (f32[328,640]{1,0:T(8,128)}, f32[328,640]{1,0:T(8,128)S(1)}, u32[]{:S(2)}, u32[]{:S(2)}) collective-permute-start(f32[328,640]{1,0:T(8,128)} %get-tuple-element.31.refs_0_), channel_id=1, source_target_pairs={{0,2},{1,3},{2,4},{3,5},{4,6},{5,7},{6,0},{7,1},{8,10},{9,11},{10,... | collective-permute-start | bytes 2519048 | tf_op jit(solution)/shard_map/ppermute | solution.py:346
  8.1 1.7 %collective-permute-start.4 = (f32[320,640]{1,0:T(8,128)}, f32[320,640]{1,0:T(8,128)S(1)}, u32[]{:S(2)}, u32[]{:S(2)}) collective-permute-start(f32[320,640]{1,0:T(8,128)} %pad_maximum_fusion.refs_0_), channel_id=1, source_target_pairs={{0,8},{1,9},{2,10},{3,11},{4,12},{5,13},{6,14},{7,15},{8,0},{9,1},... | collective-permute-start | bytes 2457608 | tf_op jit(solution)/shard_map/ppermute | solution.py:346
  9.8 1.5 %collective-permute-start.5 = (f32[320,640]{1,0:T(8,128)}, f32[320,640]{1,0:T(8,128)S(1)}, u32[]{:S(2)}, u32[]{:S(2)}) collective-permute-start(f32[320,640]{1,0:T(8,128)} %pad_maximum_fusion.refs_0_), channel_id=1, source_target_pairs={{0,16},{1,17},{2,18},{3,19},{4,20},{5,21},{6,22},{7,23},{8,24},{9,... | collective-permute-start | bytes 2457608 | tf_op jit(solution)/shard_map/ppermute | solution.py:346
  11.3 17.1 %collective-permute-done.2.refs_1_.refs_2_ = f32[328,640]{1,0:T(8,128)S(1)} collective-permute-done((f32[328,640]{1,0:T(8,128)}, f32[328,640]{1,0:T(8,128)S(1)}, u32[]{:S(2)}, u32[]{:S(2)}) %collective-permute-start.2) | collective-permute-done | bytes 839712 | tf_op jit(solution)/shard_map/ppermute | solution.py:346
  28.5 3.8 %collective-permute-start.1 = (f32[328,640]{1,0:T(8,128)}, f32[328,640]{1,0:T(8,128)S(1)}, u32[]{:S(2)}, u32[]{:S(2)}) collective-permute-start(f32[328,640]{1,0:T(8,128)} %get-tuple-element.31.refs_0_), channel_id=1, source_target_pairs={{0,6},{1,7},{2,0},{3,1},{4,2},{5,3},{6,4},{7,5},{8,14},{9,15},{10,... | collective-permute-start | bytes 2519048 | tf_op jit(solution)/shard_map/ppermute | solution.py:346
  34.1 2.4 %collective-permute-start.6 = (f32[320,640]{1,0:T(8,128)}, f32[320,640]{1,0:T(8,128)}, u32[]{:S(2)}, u32[]{:S(2)}) collective-permute-start(f32[320,640]{1,0:T(8,128)} %pad_maximum_fusion.refs_0_), channel_id=1, source_target_pairs={{0,24},{1,25},{2,26},{3,27},{4,28},{5,29},{6,30},{7,31},{8,16},{9,... | collective-permute-start | bytes 2457608 | tf_op jit(solution)/shard_map/ppermute | solution.py:346
  39.2 2.6 %stack.48.ids_ref = s32[16]{0:T(128)S(1)} concatenate(s32[1]{0:T(128)} %bitcast.ids_ref, s32[1]{0:T(128)} %bitcast.1, s32[1]{0:T(128)} %bitcast.2, s32[1]{0:T(128)} %bitcast.3, s32[1]{0:T(128)} %bitcast.4, s32[1]{0:T(128)} %bitcast.2, s32[1]{0:T(128)} %bitcast.5, s32[1]{0:T(128)} %bitcast.6, s32[1]{0:T(128)} %bitcast.7, s32[1]{0:T(128)} %bitcast.8, s32[1]{0:T(128)} %bitcast.9, ...), dimensions={0} | concatenate | bytes 128 | tf_op jit(solution)/shard_map/stack | solution.py:372
  41.9 10.0 %collective-permute-done.3.refs_2_.refs_3_ = f32[328,640]{1,0:T(8,128)S(1)} collective-permute-done((f32[328,640]{1,0:T(8,128)S(1)}, f32[328,640]{1,0:T(8,128)S(1)}, u32[]{:S(2)}, u32[]{:S(2)}) %collective-permute-start.3) | collective-permute-done | bytes 839712 | tf_op jit(solution)/shard_map/ppermute | solution.py:346
  51.9 5.0 %shard_map.71.refs_0_ = f32[640,640]{1,0:T(8,128)S(1)} custom-call(s32[16]{0:T(128)S(1)} %stack.48.ids_ref, f32[328,640]{1,0:T(8,128)} %get-tuple-element.31.refs_0_, f32[328,640]{1,0:T(8,128)S(1)} %collective-permute-done.2.refs_1_.refs_2_, f32[328,640]{1,0:T(8,128)S(1)} %collective-permute-done.3.refs_2_.refs_3_), custom_call_target="tpu_custom_call" | custom-call | tf_op jit(solution)/shard_map/pallas_call | solution.py:71
  56.9 2.9 %shard_map.69 = (bf16[4,320,960]{2,1,0:T(8,128)(2,1)S(1)}, bf16[4,320,960]{2,1,0:T(8,128)(2,1)S(1)}) custom-call(s32[16]{0:T(128)S(1)} %stack.48.ids_ref, f32[320,640]{1,0:T(8,128)} %pad_maximum_fusion.refs_0_, f32[320,640]{1,0:T(8,128)S(1)} %copy-done.1, f32[320,640]{1,0:T(8,128)S(1)} %copy-done.3, f32[320,640]{1,0:T(8,128)} %collective-permute-done.6.refs_3_), custom_call_target="tpu_custom_call" | custom-call | tf_op jit(solution)/shard_map/pallas_call | solution.py:71
  59.8 5.3 %shard_map.70 = (f32[320,640]{1,0:T(8,128)S(1)}, f32[320,640]{1,0:T(8,128)S(1)}) custom-call(s32[16]{0:T(128)S(1)} %stack.48.ids_ref, f32[328,640]{1,0:T(8,128)} %get-tuple-element.31.refs_0_, f32[328,640]{1,0:T(8,128)S(1)} %collective-permute-done.2.refs_1_.refs_2_, f32[328,640]{1,0:T(8,128)S(1)} %collective-permute-done.3.refs_2_.refs_3_, ...), custom_call_target="tpu_custom_call" | custom-call | tf_op jit(solution)/shard_map/pallas_call | solution.py:71
  65.1 2.0 %collective-permute-done.1.refs_0_.refs_1_.refs_4_ = f32[328,640]{1,0:T(8,128)S(1)} collective-permute-done((f32[328,640]{1,0:T(8,128)}, f32[328,640]{1,0:T(8,128)S(1)}, u32[]{:S(2)}, u32[]{:S(2)}) %collective-permute-start.1) | collective-permute-done | bytes 839712 | tf_op jit(solution)/shard_map/ppermute | solution.py:346
  67.1 2.5 %shard_map.72 = (f32[320,640]{1,0:T(8,128)S(1)}, f32[320,960]{1,0:T(8,128)S(1)}) custom-call(s32[16]{0:T(128)S(1)} %stack.48.ids_ref, f32[328,640]{1,0:T(8,128)S(1)} %collective-permute-done.1.refs_0_.refs_1_.refs_4_, f32[320,640]{1,0:T(8,128)S(1)} %get-tuple-element.36.refs_1_, f32[320,640]{1,0:T(8,128)S(1)} %get-tuple-element.37.refs_2_, ...), custom_call_target="tpu_custom_call" | custom-call | tf_op jit(solution)/shard_map/pallas_call | solution.py:71
  69.8 2.2 %shard_map.73 = (f32[320,640]{1,0:T(8,128)S(1)}, f32[320,640]{1,0:T(8,128)S(1)}, f32[8,128]{1,0:T(8,128)S(1)}) custom-call(s32[16]{0:T(128)S(1)} %stack.48.ids_ref, f32[640,640]{1,0:T(8,128)S(1)} %shard_map.71.refs_0_, f32[328,640]{1,0:T(8,128)S(1)} %collective-permute-done.1.refs_0_.refs_1_.refs_4_, f32[328,640]{1,0:T(8,128)S(1)} %collective-permute-done.2.refs_1_.refs_2_, ...), custom_call_target="tpu_custom_call" | custom-call | tf_op jit(solution)/shard_map/pallas_call | solution.py:71
  72.8 2.4 %shard_map.74 = (f32[320,640]{1,0:T(8,128)S(1)}, f32[320,640]{1,0:T(8,128)S(1)}, f32[320,640]{1,0:T(8,128)S(1)}, f32[320,640]{1,0:T(8,128)S(1)}) custom-call(s32[16]{0:T(128)S(1)} %stack.48.ids_ref, f32[320,640]{1,0:T(8,128)S(1)} %get-tuple-element.40.refs_0_.refs_4_, f32[320,960]{1,0:T(8,128)S(1)} %get-tuple-element.41.refs_1_, ...), custom_call_target="tpu_custom_call" | custom-call | tf_op jit(solution)/shard_map/pallas_call | solution.py:71
  75.2 1.3 collective-permute-start.8
  76.5 1.3 collective-permute-start.10
  79.2 4.5 %shard_map.75 = (f32[320,640]{1,0:T(8,128)S(1)}, f32[320,640]{1,0:T(8,128)S(1)}, f32[8,320]{1,0:T(8,128)S(1)}) custom-call(s32[16]{0:T(128)S(1)} %stack.48.ids_ref, f32[320,640]{1,0:T(8,128)S(1)} %get-tuple-element.44.refs_0_.refs_2_, f32[320,640]{1,0:T(8,128)S(1)} %get-tuple-element.45.refs_1_, f32[320,640]{1,0:T(8,128)S(1)} %collective-permute-done.9.refs_2_, ...), custom_call_target="tpu_custom_call" | custom-call | tf_op jit(solution)/shard_map/pallas_call | solution.py:71
  83.7 31.3 %collective-permute-done.8.refs_0_ = f32[320,640]{1,0:T(8,128)S(1)} collective-permute-done((f32[320,640]{1,0:T(8,128)S(1)}, f32[320,640]{1,0:T(8,128)S(1)}, u32[]{:S(2)}, u32[]{:S(2)}) %collective-permute-start.8) | collective-permute-done | bytes 819232 | tf_op jit(solution)/shard_map/ppermute | solution.py:346
  115.0 2.5 %shard_map.76 = (f32[320,640]{1,0:T(8,128)S(1)}, f32[320,640]{1,0:T(8,128)S(1)}) custom-call(s32[16]{0:T(128)S(1)} %stack.48.ids_ref, f32[320,640]{1,0:T(8,128)S(1)} %collective-permute-done.8.refs_0_, f32[320,640]{1,0:T(8,128)S(1)} %get-tuple-element.47.refs_1_, f32[320,640]{1,0:T(8,128)S(1)} %get-tuple-element.48.refs_2_, ...), custom_call_target="tpu_custom_call" | custom-call | tf_op jit(solution)/shard_map/pallas_call | solution.py:71
  117.5 3.4 %shard_map.78 = f32[328,640]{1,0:T(8,128)S(1)} custom-call(s32[16]{0:T(128)S(1)} %stack.48.ids_ref, f32[320,640]{1,0:T(8,128)S(1)} %get-tuple-element.52.refs_0_, f32[1,640]{1,0:T(1,128)S(1)} %broadcast_in_dim.2.refs_6_.refs_1_, bf16[4,320,960]{2,1,0:T(8,128)(2,1)S(1)} %get-tuple-element.34.refs_4_.refs_8_.refs_2_, ...), custom_call_target="tpu_custom_call" | custom-call | tf_op jit(solution)/shard_map/pallas_call | solution.py:71
  121.0 3.3 %shard_map.77 = f32[328,640]{1,0:T(8,128)S(1)} custom-call(s32[16]{0:T(128)S(1)} %stack.48.ids_ref, f32[320,640]{1,0:T(8,128)S(1)} %get-tuple-element.49.refs_0_, f32[1,640]{1,0:T(1,128)S(1)} %broadcast_in_dim.2.refs_6_.refs_1_, f32[320,640]{1,0:T(8,128)S(1)} %get-tuple-element.44.refs_0_.refs_2_, f32[8,128]{1,0:T(8,128)S(1)} %get-tuple-element.42.refs_3_, ...), custom_call_target="tpu_custom_call" | custom-call | tf_op jit(solution)/shard_map/pallas_call | solution.py:71
  124.6 3.3 %collective-permute-start.13 = (f32[8,320]{1,0:T(8,128)S(1)}, f32[8,320]{1,0:T(8,128)S(1)}, u32[]{:S(2)}, u32[]{:S(2)}) collective-permute-start(f32[8,320]{1,0:T(8,128)S(1)} %slice_add_fusion.1), channel_id=1, source_target_pairs={{0,8},{1,9},{2,10},{3,11},{4,12},{5,13},{6,14},{7,15},{8,0},{9,1},... | collective-permute-start | bytes 30728 | tf_op jit(solution)/shard_map/ppermute | solution.py:346
  (43 shorter events, 12.7 us)
Async XLA Ops:
  0.6 1.1 copy-start.4
  1.8 0.7 copy-start.5
  3.8 3.2 %collective-permute-start = (f32[328,320]{1,0:T(8,128)S(1)}, f32[328,320]{1,0:T(8,128)S(1)}, u32[]{:S(2)}, u32[]{:S(2)}) collective-permute-start(f32[328,320]{1,0:T(8,128)S(1)} %get-tuple-element.30), channel_id=1, source_target_pairs={{0,1},{1,0},{2,3},{3,2},{4,5},{5,4},{6,7},{7,6},{8,9},{9,8},{10,11... | collective-permute-start | bytes 1259528 | tf_op jit(solution)/shard_map/ppermute | solution.py:349
  4.3 24.2 %collective-permute-start.2 = (f32[328,640]{1,0:T(8,128)}, f32[328,640]{1,0:T(8,128)S(1)}, u32[]{:S(2)}, u32[]{:S(2)}) collective-permute-start(f32[328,640]{1,0:T(8,128)} %get-tuple-element.31.refs_0_), channel_id=1, source_target_pairs={{0,2},{1,3},{2,4},{3,5},{4,6},{5,7},{6,0},{7,1},{8,10},{9,11},{10,... | collective-permute-start | bytes 2519048 | tf_op jit(solution)/shard_map/ppermute | solution.py:346
  8.1 24.2 %collective-permute-start.4 = (f32[320,640]{1,0:T(8,128)}, f32[320,640]{1,0:T(8,128)S(1)}, u32[]{:S(2)}, u32[]{:S(2)}) collective-permute-start(f32[320,640]{1,0:T(8,128)} %pad_maximum_fusion.refs_0_), channel_id=1, source_target_pairs={{0,8},{1,9},{2,10},{3,11},{4,12},{5,13},{6,14},{7,15},{8,0},{9,1},... | collective-permute-start | bytes 2457608 | tf_op jit(solution)/shard_map/ppermute | solution.py:346
  9.8 23.4 %collective-permute-start.5 = (f32[320,640]{1,0:T(8,128)}, f32[320,640]{1,0:T(8,128)S(1)}, u32[]{:S(2)}, u32[]{:S(2)}) collective-permute-start(f32[320,640]{1,0:T(8,128)} %pad_maximum_fusion.refs_0_), channel_id=1, source_target_pairs={{0,16},{1,17},{2,18},{3,19},{4,20},{5,21},{6,22},{7,23},{8,24},{9,... | collective-permute-start | bytes 2457608 | tf_op jit(solution)/shard_map/ppermute | solution.py:346
  28.5 23.4 %collective-permute-start.3 = (f32[328,640]{1,0:T(8,128)S(1)}, f32[328,640]{1,0:T(8,128)S(1)}, u32[]{:S(2)}, u32[]{:S(2)}) collective-permute-start(f32[328,640]{1,0:T(8,128)S(1)} %collective-permute-done.2.refs_1_.refs_2_), channel_id=1, source_target_pairs={{0,2},{1,3},{2,4},{3,5},{4,6},{5,7},{6,0},{7,1},{8,10},{9,11},{10,... | collective-permute-start | bytes 2519048 | tf_op jit(solution)/shard_map/ppermute | solution.py:346
  28.5 38.7 %collective-permute-start.1 = (f32[328,640]{1,0:T(8,128)}, f32[328,640]{1,0:T(8,128)S(1)}, u32[]{:S(2)}, u32[]{:S(2)}) collective-permute-start(f32[328,640]{1,0:T(8,128)} %get-tuple-element.31.refs_0_), channel_id=1, source_target_pairs={{0,6},{1,7},{2,0},{3,1},{4,2},{5,3},{6,4},{7,5},{8,14},{9,15},{10,... | collective-permute-start | bytes 2519048 | tf_op jit(solution)/shard_map/ppermute | solution.py:346
  32.3 0.9 copy-start
  33.2 0.9 copy-start.2
  34.1 22.7 %collective-permute-start.6 = (f32[320,640]{1,0:T(8,128)}, f32[320,640]{1,0:T(8,128)}, u32[]{:S(2)}, u32[]{:S(2)}) collective-permute-start(f32[320,640]{1,0:T(8,128)} %pad_maximum_fusion.refs_0_), channel_id=1, source_target_pairs={{0,24},{1,25},{2,26},{3,27},{4,28},{5,29},{6,30},{7,31},{8,16},{9,... | collective-permute-start | bytes 2457608 | tf_op jit(solution)/shard_map/ppermute | solution.py:346
  41.8 15.0 %copy-start.1 = (f32[320,640]{1,0:T(8,128)S(1)}, f32[320,640]{1,0:T(8,128)}, u32[]{:S(2)}) copy-start(f32[320,640]{1,0:T(8,128)} %copy-done) | copy-start | bytes 2457604
  41.9 15.0 %copy-start.3 = (f32[320,640]{1,0:T(8,128)S(1)}, f32[320,640]{1,0:T(8,128)}, u32[]{:S(2)}) copy-start(f32[320,640]{1,0:T(8,128)} %copy-done.2) | copy-start | bytes 2457604
  69.7 3.1 %collective-permute-start.7 = (f32[320,960]{1,0:T(8,128)S(1)}, f32[320,960]{1,0:T(8,128)S(1)}, u32[]{:S(2)}, u32[]{:S(2)}) collective-permute-start(f32[320,960]{1,0:T(8,128)S(1)} %get-tuple-element.41.refs_1_), channel_id=1, source_target_pairs={{0,1},{1,0},{2,3},{3,2},{4,5},{5,4},{6,7},{7,6},{8,9},{9,8},{10,11... | collective-permute-start | bytes 3686408 | tf_op jit(solution)/shard_map/ppermute | solution.py:349
  72.0 7.2 %collective-permute-start.9 = (f32[320,640]{1,0:T(8,128)S(1)}, f32[320,640]{1,0:T(8,128)S(1)}, u32[]{:S(2)}, u32[]{:S(2)}) collective-permute-start(f32[320,640]{1,0:T(8,128)S(1)} %get-tuple-element.39), channel_id=1, source_target_pairs={{0,1},{1,0},{2,3},{3,2},{4,5},{5,4},{6,7},{7,6},{8,9},{9,8},{10,11... | collective-permute-start | bytes 2457608 | tf_op jit(solution)/shard_map/ppermute | solution.py:349
  72.8 6.3 %copy-start.6 = (f32[640]{0:T(1024)S(1)}, f32[640]{0:T(1024)}, u32[]{:S(2)}) copy-start(f32[640]{0:T(1024)} %param.7) | copy-start | bytes 7684
  75.2 39.7 %collective-permute-start.8 = (f32[320,640]{1,0:T(8,128)S(1)}, f32[320,640]{1,0:T(8,128)S(1)}, u32[]{:S(2)}, u32[]{:S(2)}) collective-permute-start(f32[320,640]{1,0:T(8,128)S(1)} %get-tuple-element.43), channel_id=1, source_target_pairs={{2,4},{3,5},{4,6},{5,7},{6,2},{7,3},{8,14},{9,15},{12,20},{13,21},... | collective-permute-start | bytes 2457608 | tf_op jit(solution)/shard_map/ppermute | solution.py:346
  76.5 40.9 %collective-permute-start.10 = (f32[320,640]{1,0:T(8,128)S(1)}, f32[320,640]{1,0:T(8,128)S(1)}, u32[]{:S(2)}, u32[]{:S(2)}) collective-permute-start(f32[320,640]{1,0:T(8,128)S(1)} %get-tuple-element.50), channel_id=1, source_target_pairs={{2,10},{3,11},{4,2},{5,3},{6,30},{7,31},{8,0},{9,1},{12,8},{13,9},... | collective-permute-start | bytes 2457608 | tf_op jit(solution)/shard_map/ppermute | solution.py:346
  77.8 39.7 %collective-permute-start.11 = (f32[320,640]{1,0:T(8,128)S(1)}, f32[320,640]{1,0:T(8,128)S(1)}, u32[]{:S(2)}, u32[]{:S(2)}) collective-permute-start(f32[320,640]{1,0:T(8,128)S(1)} %get-tuple-element.51), channel_id=1, source_target_pairs={{2,6},{3,7},{4,20},{5,21},{6,4},{7,5},{8,12},{9,13},{12,14},{13,15... | collective-permute-start | bytes 2457608 | tf_op jit(solution)/shard_map/ppermute | solution.py:346
  120.9 3.4 %collective-permute-start.12 = (f32[328,640]{1,0:T(8,128)S(1)}, f32[328,640]{1,0:T(8,128)S(1)}, u32[]{:S(2)}, u32[]{:S(2)}) collective-permute-start(f32[328,640]{1,0:T(8,128)S(1)} %shard_map.78), channel_id=1, source_target_pairs={{0,1},{1,0},{2,3},{3,2},{4,5},{5,4},{6,7},{7,6},{8,9},{9,8},{10,11... | collective-permute-start | bytes 2519048 | tf_op jit(solution)/shard_map/ppermute | solution.py:349
  124.3 4.7 %collective-permute-start.15 = (f32[8,320]{1,0:T(8,128)S(1)}, f32[8,320]{1,0:T(8,128)S(1)}, u32[]{:S(2)}, u32[]{:S(2)}) collective-permute-start(f32[8,320]{1,0:T(8,128)S(1)} %slice_add_fusion.1), channel_id=1, source_target_pairs={{0,24},{1,25},{2,26},{3,27},{4,28},{5,29},{6,30},{7,31},{8,16},{9,... | collective-permute-start | bytes 30728 | tf_op jit(solution)/shard_map/ppermute | solution.py:346
  124.4 4.6 %collective-permute-start.14 = (f32[8,320]{1,0:T(8,128)S(1)}, f32[8,320]{1,0:T(8,128)S(1)}, u32[]{:S(2)}, u32[]{:S(2)}) collective-permute-start(f32[8,320]{1,0:T(8,128)S(1)} %slice_add_fusion.1), channel_id=1, source_target_pairs={{0,16},{1,17},{2,18},{3,19},{4,20},{5,21},{6,22},{7,23},{8,24},{9,... | collective-permute-start | bytes 30728 | tf_op jit(solution)/shard_map/ppermute | solution.py:346
  124.6 5.0 %collective-permute-start.13 = (f32[8,320]{1,0:T(8,128)S(1)}, f32[8,320]{1,0:T(8,128)S(1)}, u32[]{:S(2)}, u32[]{:S(2)}) collective-permute-start(f32[8,320]{1,0:T(8,128)S(1)} %slice_add_fusion.1), channel_id=1, source_target_pairs={{0,8},{1,9},{2,10},{3,11},{4,12},{5,13},{6,14},{7,15},{8,0},{9,1},... | collective-permute-start | bytes 30728 | tf_op jit(solution)/shard_map/ppermute | solution.py:346

commit v9 on v8

--- a/solution.py
+++ b/solution.py
@@ -368,7 +368,8 @@
 
         scalars = [core, jnp.asarray(down_step)[r, z], r, z, (z - r) % panels]
         scalars += [r ^ m for m in range(panels)] + [(z - j) % panels for j in range(panels)]
-        scalars += list(jnp.asarray(tile_got)[r, z])
+        order = [1, 0, *range(2, steps)]
+        scalars += [jnp.asarray(tile_got)[r, z, step] for step in order]
         ids = jnp.stack([jnp.asarray(s, jnp.int32) for s in scalars])
         line_at, steps_at = LISTS + panels, LISTS + 2 * panels
 
@@ -466,6 +467,7 @@
             scratch=held_parts(4, half),
         )
 
+        arrived = [arrived[step] for step in order]
         cube = call(
             functools.partial(middle_kernel, steps_at),
             [shape(half, height)] * 2,

time: 131 us -> 133 us (1.015); the launches traced: 130 us -> 130 us
  transfers between devices with their start and end apart: 16 -> 16, of which waited for: 7 -> 8; matrix products, arithmetic and copies ran while one was open for 6% -> 6% of each run, Pallas kernels for 22% -> 22%
where the time goes in v9:
time: 133 us; the launch traced here: 130 us
  waiting for transfers between devices  61.1 us (46%)
  Pallas kernels  35.4 us (27%)
  starting transfers between devices  20.8 us (16%)
  local copies, waits for them, and re-layouts  9.06 us (7%)
  other arithmetic  2.69 us (2%)
    ppermute x12, waiting for transfers between devices, send(): return lax.ppermute(value, ('row', 'col'), pairs)  60.9 us
    pallas_call x11, Pallas kernels, call(): pl.pallas_call(body, out_shape=outs, in_specs=[pl.BlockSpec(memory_space=...  35.4 us
    ppermute x12, starting transfers between devices, send(): return lax.ppermute(value, ('row', 'col'), pairs)  19.6 us
    unnamed x14, local copies, waits for them, and re-layouts  3.66 us
  transfers between devices with their start and end apart: 16, of which 8 were waited for; matrix products, arithmetic and copies ran while one was open for 6% of the time, Pallas kernels for 22%

profile of v9, /device:TPU:0, one launch (start us, length us, event | category | flops | bytes accessed | tf_op | source)
XLA Modules:
  0.0 130.0 jit_solution(18331431019815294271)
XLA Ops:
  2.5 1.3 %shard_map.86 = (f32[328,640]{1,0:T(8,128)}, f32[320,320]{1,0:T(8,128)S(1)}, f32[328,320]{1,0:T(8,128)S(1)}, f32[8,128]{1,0:T(8,128)S(1)}) custom-call(s32[1]{0:T(128)} %bitcast.ids_ref, f32[320,640]{1,0:T(8,128)S(1)} %bitcast.19, s32[5,10]{1,0:T(8,128)S(1)} %bitcast.20), custom_call_target="tpu_custom_call" | custom-call | tf_op jit(solution)/shard_map/pallas_call | solution.py:71
  4.3 2.6 %collective-permute-start.2 = (f32[328,640]{1,0:T(8,128)}, f32[328,640]{1,0:T(8,128)S(1)}, u32[]{:S(2)}, u32[]{:S(2)}) collective-permute-start(f32[328,640]{1,0:T(8,128)} %get-tuple-element.31.refs_0_), channel_id=1, source_target_pairs={{0,2},{1,3},{2,4},{3,5},{4,6},{5,7},{6,0},{7,1},{8,10},{9,11},{10,... | collective-permute-start | bytes 2519048 | tf_op jit(solution)/shard_map/ppermute | solution.py:346
  8.1 1.7 %collective-permute-start.4 = (f32[320,640]{1,0:T(8,128)}, f32[320,640]{1,0:T(8,128)S(1)}, u32[]{:S(2)}, u32[]{:S(2)}) collective-permute-start(f32[320,640]{1,0:T(8,128)} %pad_maximum_fusion.refs_0_), channel_id=1, source_target_pairs={{0,8},{1,9},{2,10},{3,11},{4,12},{5,13},{6,14},{7,15},{8,0},{9,1},... | collective-permute-start | bytes 2457608 | tf_op jit(solution)/shard_map/ppermute | solution.py:346
  9.8 1.5 %collective-permute-start.5 = (f32[320,640]{1,0:T(8,128)}, f32[320,640]{1,0:T(8,128)S(1)}, u32[]{:S(2)}, u32[]{:S(2)}) collective-permute-start(f32[320,640]{1,0:T(8,128)} %pad_maximum_fusion.refs_0_), channel_id=1, source_target_pairs={{0,16},{1,17},{2,18},{3,19},{4,20},{5,21},{6,22},{7,23},{8,24},{9,... | collective-permute-start | bytes 2457608 | tf_op jit(solution)/shard_map/ppermute | solution.py:346
  11.3 17.1 %collective-permute-done.2.refs_1_.refs_2_ = f32[328,640]{1,0:T(8,128)S(1)} collective-permute-done((f32[328,640]{1,0:T(8,128)}, f32[328,640]{1,0:T(8,128)S(1)}, u32[]{:S(2)}, u32[]{:S(2)}) %collective-permute-start.2) | collective-permute-done | bytes 839712 | tf_op jit(solution)/shard_map/ppermute | solution.py:346
  28.5 3.8 %collective-permute-start.1 = (f32[328,640]{1,0:T(8,128)}, f32[328,640]{1,0:T(8,128)S(1)}, u32[]{:S(2)}, u32[]{:S(2)}) collective-permute-start(f32[328,640]{1,0:T(8,128)} %get-tuple-element.31.refs_0_), channel_id=1, source_target_pairs={{0,6},{1,7},{2,0},{3,1},{4,2},{5,3},{6,4},{7,5},{8,14},{9,15},{10,... | collective-permute-start | bytes 2519048 | tf_op jit(solution)/shard_map/ppermute | solution.py:346
  34.1 2.4 %collective-permute-start.6 = (f32[320,640]{1,0:T(8,128)}, f32[320,640]{1,0:T(8,128)}, u32[]{:S(2)}, u32[]{:S(2)}) collective-permute-start(f32[320,640]{1,0:T(8,128)} %pad_maximum_fusion.refs_0_), channel_id=1, source_target_pairs={{0,24},{1,25},{2,26},{3,27},{4,28},{5,29},{6,30},{7,31},{8,16},{9,... | collective-permute-start | bytes 2457608 | tf_op jit(solution)/shard_map/ppermute | solution.py:346
  37.9 1.4 %constant_dynamic-slice_fusion = (s32[1,1,1]{2,1,0:T(1,128)}, s32[1,1,1]{2,1,0:T(1,128)}, s32[1,1,1]{2,1,0:T(1,128)}) fusion(s32[4,4,3]{2,1,0:T(4,128)} %constant.71.clone, s32[]{:T(128)S(6)} %select_n.44, s32[]{:T(128)S(6)} %select_n.46), kind=kLoop, calls=%fused_computation.8 | loop fusion | bytes 32 | tf_op jit(solution)/shard_map/dynamic_slice | solution.py:372
  39.3 2.6 %stack.48.ids_ref = s32[16]{0:T(128)S(1)} concatenate(s32[1]{0:T(128)} %bitcast.ids_ref, s32[1]{0:T(128)} %bitcast.1, s32[1]{0:T(128)} %bitcast.2, s32[1]{0:T(128)} %bitcast.3, s32[1]{0:T(128)} %bitcast.4, s32[1]{0:T(128)} %bitcast.2, s32[1]{0:T(128)} %bitcast.5, s32[1]{0:T(128)} %bitcast.6, s32[1]{0:T(128)} %bitcast.7, s32[1]{0:T(128)} %bitcast.8, s32[1]{0:T(128)} %bitcast.9, ...), dimensions={0} | concatenate | bytes 128 | tf_op jit(solution)/shard_map/stack | solution.py:373
  42.0 9.9 %collective-permute-done.3.refs_2_.refs_3_ = f32[328,640]{1,0:T(8,128)S(1)} collective-permute-done((f32[328,640]{1,0:T(8,128)S(1)}, f32[328,640]{1,0:T(8,128)S(1)}, u32[]{:S(2)}, u32[]{:S(2)}) %collective-permute-start.3) | collective-permute-done | bytes 839712 | tf_op jit(solution)/shard_map/ppermute | solution.py:346
  51.9 5.0 %shard_map.89.refs_0_ = f32[640,640]{1,0:T(8,128)S(1)} custom-call(s32[16]{0:T(128)S(1)} %stack.48.ids_ref, f32[328,640]{1,0:T(8,128)} %get-tuple-element.31.refs_0_, f32[328,640]{1,0:T(8,128)S(1)} %collective-permute-done.2.refs_1_.refs_2_, f32[328,640]{1,0:T(8,128)S(1)} %collective-permute-done.3.refs_2_.refs_3_), custom_call_target="tpu_custom_call" | custom-call | tf_op jit(solution)/shard_map/pallas_call | solution.py:71
  56.9 2.9 %shard_map.87 = (bf16[4,320,960]{2,1,0:T(8,128)(2,1)S(1)}, bf16[4,320,960]{2,1,0:T(8,128)(2,1)S(1)}) custom-call(s32[16]{0:T(128)S(1)} %stack.48.ids_ref, f32[320,640]{1,0:T(8,128)} %pad_maximum_fusion.refs_0_, f32[320,640]{1,0:T(8,128)S(1)} %copy-done.1, f32[320,640]{1,0:T(8,128)S(1)} %copy-done.3, f32[320,640]{1,0:T(8,128)} %collective-permute-done.6.refs_3_), custom_call_target="tpu_custom_call" | custom-call | tf_op jit(solution)/shard_map/pallas_call | solution.py:71
  59.8 5.3 %shard_map.88 = (f32[320,640]{1,0:T(8,128)S(1)}, f32[320,640]{1,0:T(8,128)S(1)}) custom-call(s32[16]{0:T(128)S(1)} %stack.48.ids_ref, f32[328,640]{1,0:T(8,128)} %get-tuple-element.31.refs_0_, f32[328,640]{1,0:T(8,128)S(1)} %collective-permute-done.2.refs_1_.refs_2_, f32[328,640]{1,0:T(8,128)S(1)} %collective-permute-done.3.refs_2_.refs_3_, ...), custom_call_target="tpu_custom_call" | custom-call | tf_op jit(solution)/shard_map/pallas_call | solution.py:71
  65.1 2.0 %collective-permute-done.1.refs_0_.refs_1_.refs_4_ = f32[328,640]{1,0:T(8,128)S(1)} collective-permute-done((f32[328,640]{1,0:T(8,128)}, f32[328,640]{1,0:T(8,128)S(1)}, u32[]{:S(2)}, u32[]{:S(2)}) %collective-permute-start.1) | collective-permute-done | bytes 839712 | tf_op jit(solution)/shard_map/ppermute | solution.py:346
  67.1 2.5 %shard_map.90 = (f32[320,640]{1,0:T(8,128)S(1)}, f32[320,960]{1,0:T(8,128)S(1)}) custom-call(s32[16]{0:T(128)S(1)} %stack.48.ids_ref, f32[328,640]{1,0:T(8,128)S(1)} %collective-permute-done.1.refs_0_.refs_1_.refs_4_, f32[320,640]{1,0:T(8,128)S(1)} %get-tuple-element.36.refs_1_, f32[320,640]{1,0:T(8,128)S(1)} %get-tuple-element.37.refs_2_, ...), custom_call_target="tpu_custom_call" | custom-call | tf_op jit(solution)/shard_map/pallas_call | solution.py:71
  69.8 2.2 %shard_map.91 = (f32[320,640]{1,0:T(8,128)S(1)}, f32[320,640]{1,0:T(8,128)S(1)}, f32[8,128]{1,0:T(8,128)S(1)}) custom-call(s32[16]{0:T(128)S(1)} %stack.48.ids_ref, f32[640,640]{1,0:T(8,128)S(1)} %shard_map.89.refs_0_, f32[328,640]{1,0:T(8,128)S(1)} %collective-permute-done.1.refs_0_.refs_1_.refs_4_, f32[328,640]{1,0:T(8,128)S(1)} %collective-permute-done.2.refs_1_.refs_2_, ...), custom_call_target="tpu_custom_call" | custom-call | tf_op jit(solution)/shard_map/pallas_call | solution.py:71
  72.8 2.4 %shard_map.92 = (f32[320,640]{1,0:T(8,128)S(1)}, f32[320,640]{1,0:T(8,128)S(1)}, f32[320,640]{1,0:T(8,128)S(1)}, f32[320,640]{1,0:T(8,128)S(1)}) custom-call(s32[16]{0:T(128)S(1)} %stack.48.ids_ref, f32[320,640]{1,0:T(8,128)S(1)} %get-tuple-element.40.refs_0_.refs_4_, f32[320,960]{1,0:T(8,128)S(1)} %get-tuple-element.41.refs_1_, ...), custom_call_target="tpu_custom_call" | custom-call | tf_op jit(solution)/shard_map/pallas_call | solution.py:71
  79.2 4.5 %shard_map.93 = (f32[320,640]{1,0:T(8,128)S(1)}, f32[320,640]{1,0:T(8,128)S(1)}, f32[8,320]{1,0:T(8,128)S(1)}) custom-call(s32[16]{0:T(128)S(1)} %stack.48.ids_ref, f32[320,640]{1,0:T(8,128)S(1)} %get-tuple-element.44.refs_0_.refs_2_, f32[320,640]{1,0:T(8,128)S(1)} %get-tuple-element.45.refs_1_, f32[320,640]{1,0:T(8,128)S(1)} %collective-permute-done.9.refs_2_, ...), custom_call_target="tpu_custom_call" | custom-call | tf_op jit(solution)/shard_map/pallas_call | solution.py:71
  83.7 13.8 %collective-permute-done.8.refs_0_ = f32[320,640]{1,0:T(8,128)S(1)} collective-permute-done((f32[320,640]{1,0:T(8,128)S(1)}, f32[320,640]{1,0:T(8,128)S(1)}, u32[]{:S(2)}, u32[]{:S(2)}) %collective-permute-start.8) | collective-permute-done | bytes 819232 | tf_op jit(solution)/shard_map/ppermute | solution.py:346
  97.4 2.5 %shard_map.94 = (f32[320,640]{1,0:T(8,128)S(1)}, f32[320,640]{1,0:T(8,128)S(1)}) custom-call(s32[16]{0:T(128)S(1)} %stack.48.ids_ref, f32[320,640]{1,0:T(8,128)S(1)} %collective-permute-done.8.refs_0_, f32[320,640]{1,0:T(8,128)S(1)} %get-tuple-element.47.refs_1_, f32[320,640]{1,0:T(8,128)S(1)} %get-tuple-element.48.refs_2_, ...), custom_call_target="tpu_custom_call" | custom-call | tf_op jit(solution)/shard_map/pallas_call | solution.py:71
  99.9 17.4 %collective-permute-done.10.refs_5_.refs_4_ = f32[320,640]{1,0:T(8,128)S(1)} collective-permute-done((f32[320,640]{1,0:T(8,128)S(1)}, f32[320,640]{1,0:T(8,128)S(1)}, u32[]{:S(2)}, u32[]{:S(2)}) %collective-permute-start.10) | collective-permute-done | bytes 819232 | tf_op jit(solution)/shard_map/ppermute | solution.py:346
  117.4 3.4 %shard_map.96 = f32[328,640]{1,0:T(8,128)S(1)} custom-call(s32[16]{0:T(128)S(1)} %stack.48.ids_ref, f32[320,640]{1,0:T(8,128)S(1)} %get-tuple-element.52.refs_0_, f32[1,640]{1,0:T(1,128)S(1)} %broadcast_in_dim.2.refs_6_.refs_1_, bf16[4,320,960]{2,1,0:T(8,128)(2,1)S(1)} %get-tuple-element.34.refs_4_.refs_8_.refs_2_, ...), custom_call_target="tpu_custom_call" | custom-call | tf_op jit(solution)/shard_map/pallas_call | solution.py:71
  120.8 3.3 %shard_map.95 = f32[328,640]{1,0:T(8,128)S(1)} custom-call(s32[16]{0:T(128)S(1)} %stack.48.ids_ref, f32[320,640]{1,0:T(8,128)S(1)} %get-tuple-element.49.refs_0_, f32[1,640]{1,0:T(1,128)S(1)} %broadcast_in_dim.2.refs_6_.refs_1_, f32[320,640]{1,0:T(8,128)S(1)} %get-tuple-element.44.refs_0_.refs_2_, f32[8,128]{1,0:T(8,128)S(1)} %get-tuple-element.42.refs_3_, ...), custom_call_target="tpu_custom_call" | custom-call | tf_op jit(solution)/shard_map/pallas_call | solution.py:71
  125.7 2.1 %collective-permute-start.13 = (f32[8,320]{1,0:T(8,128)S(1)}, f32[8,320]{1,0:T(8,128)S(1)}, u32[]{:S(2)}, u32[]{:S(2)}) collective-permute-start(f32[8,320]{1,0:T(8,128)S(1)} %slice_add_fusion.1), channel_id=1, source_target_pairs={{0,8},{1,9},{2,10},{3,11},{4,12},{5,13},{6,14},{7,15},{8,0},{9,1},... | collective-permute-start | bytes 30728 | tf_op jit(solution)/shard_map/ppermute | solution.py:346
  (42 shorter events, 15.2 us)
Async XLA Ops:
  0.6 1.1 copy-start.4
  1.8 0.7 copy-start.5
  3.8 3.2 %collective-permute-start = (f32[328,320]{1,0:T(8,128)S(1)}, f32[328,320]{1,0:T(8,128)S(1)}, u32[]{:S(2)}, u32[]{:S(2)}) collective-permute-start(f32[328,320]{1,0:T(8,128)S(1)} %get-tuple-element.30), channel_id=1, source_target_pairs={{0,1},{1,0},{2,3},{3,2},{4,5},{5,4},{6,7},{7,6},{8,9},{9,8},{10,11... | collective-permute-start | bytes 1259528 | tf_op jit(solution)/shard_map/ppermute | solution.py:349
  4.3 24.2 %collective-permute-start.2 = (f32[328,640]{1,0:T(8,128)}, f32[328,640]{1,0:T(8,128)S(1)}, u32[]{:S(2)}, u32[]{:S(2)}) collective-permute-start(f32[328,640]{1,0:T(8,128)} %get-tuple-element.31.refs_0_), channel_id=1, source_target_pairs={{0,2},{1,3},{2,4},{3,5},{4,6},{5,7},{6,0},{7,1},{8,10},{9,11},{10,... | collective-permute-start | bytes 2519048 | tf_op jit(solution)/shard_map/ppermute | solution.py:346
  8.1 24.2 %collective-permute-start.4 = (f32[320,640]{1,0:T(8,128)}, f32[320,640]{1,0:T(8,128)S(1)}, u32[]{:S(2)}, u32[]{:S(2)}) collective-permute-start(f32[320,640]{1,0:T(8,128)} %pad_maximum_fusion.refs_0_), channel_id=1, source_target_pairs={{0,8},{1,9},{2,10},{3,11},{4,12},{5,13},{6,14},{7,15},{8,0},{9,1},... | collective-permute-start | bytes 2457608 | tf_op jit(solution)/shard_map/ppermute | solution.py:346
  9.8 23.4 %collective-permute-start.5 = (f32[320,640]{1,0:T(8,128)}, f32[320,640]{1,0:T(8,128)S(1)}, u32[]{:S(2)}, u32[]{:S(2)}) collective-permute-start(f32[320,640]{1,0:T(8,128)} %pad_maximum_fusion.refs_0_), channel_id=1, source_target_pairs={{0,16},{1,17},{2,18},{3,19},{4,20},{5,21},{6,22},{7,23},{8,24},{9,... | collective-permute-start | bytes 2457608 | tf_op jit(solution)/shard_map/ppermute | solution.py:346
  28.5 23.4 %collective-permute-start.3 = (f32[328,640]{1,0:T(8,128)S(1)}, f32[328,640]{1,0:T(8,128)S(1)}, u32[]{:S(2)}, u32[]{:S(2)}) collective-permute-start(f32[328,640]{1,0:T(8,128)S(1)} %collective-permute-done.2.refs_1_.refs_2_), channel_id=1, source_target_pairs={{0,2},{1,3},{2,4},{3,5},{4,6},{5,7},{6,0},{7,1},{8,10},{9,11},{10,... | collective-permute-start | bytes 2519048 | tf_op jit(solution)/shard_map/ppermute | solution.py:346
  28.5 38.7 %collective-permute-start.1 = (f32[328,640]{1,0:T(8,128)}, f32[328,640]{1,0:T(8,128)S(1)}, u32[]{:S(2)}, u32[]{:S(2)}) collective-permute-start(f32[328,640]{1,0:T(8,128)} %get-tuple-element.31.refs_0_), channel_id=1, source_target_pairs={{0,6},{1,7},{2,0},{3,1},{4,2},{5,3},{6,4},{7,5},{8,14},{9,15},{10,... | collective-permute-start | bytes 2519048 | tf_op jit(solution)/shard_map/ppermute | solution.py:346
  32.3 0.9 copy-start
  33.2 0.9 copy-start.2
  34.1 22.7 %collective-permute-start.6 = (f32[320,640]{1,0:T(8,128)}, f32[320,640]{1,0:T(8,128)}, u32[]{:S(2)}, u32[]{:S(2)}) collective-permute-start(f32[320,640]{1,0:T(8,128)} %pad_maximum_fusion.refs_0_), channel_id=1, source_target_pairs={{0,24},{1,25},{2,26},{3,27},{4,28},{5,29},{6,30},{7,31},{8,16},{9,... | collective-permute-start | bytes 2457608 | tf_op jit(solution)/shard_map/ppermute | solution.py:346
  42.0 14.9 %copy-start.1 = (f32[320,640]{1,0:T(8,128)S(1)}, f32[320,640]{1,0:T(8,128)}, u32[]{:S(2)}) copy-start(f32[320,640]{1,0:T(8,128)} %copy-done) | copy-start | bytes 2457604
  42.0 14.9 %copy-start.3 = (f32[320,640]{1,0:T(8,128)S(1)}, f32[320,640]{1,0:T(8,128)}, u32[]{:S(2)}) copy-start(f32[320,640]{1,0:T(8,128)} %copy-done.2) | copy-start | bytes 2457604
  69.7 3.1 %collective-permute-start.7 = (f32[320,960]{1,0:T(8,128)S(1)}, f32[320,960]{1,0:T(8,128)S(1)}, u32[]{:S(2)}, u32[]{:S(2)}) collective-permute-start(f32[320,960]{1,0:T(8,128)S(1)} %get-tuple-element.41.refs_1_), channel_id=1, source_target_pairs={{0,1},{1,0},{2,3},{3,2},{4,5},{5,4},{6,7},{7,6},{8,9},{9,8},{10,11... | collective-permute-start | bytes 3686408 | tf_op jit(solution)/shard_map/ppermute | solution.py:349
  72.0 7.2 %collective-permute-start.9 = (f32[320,640]{1,0:T(8,128)S(1)}, f32[320,640]{1,0:T(8,128)S(1)}, u32[]{:S(2)}, u32[]{:S(2)}) collective-permute-start(f32[320,640]{1,0:T(8,128)S(1)} %get-tuple-element.39), channel_id=1, source_target_pairs={{0,1},{1,0},{2,3},{3,2},{4,5},{5,4},{6,7},{7,6},{8,9},{9,8},{10,11... | collective-permute-start | bytes 2457608 | tf_op jit(solution)/shard_map/ppermute | solution.py:349
  72.8 6.3 %copy-start.6 = (f32[640]{0:T(1024)S(1)}, f32[640]{0:T(1024)}, u32[]{:S(2)}) copy-start(f32[640]{0:T(1024)} %param.9) | copy-start | bytes 7684
  75.2 22.2 %collective-permute-start.8 = (f32[320,640]{1,0:T(8,128)S(1)}, f32[320,640]{1,0:T(8,128)S(1)}, u32[]{:S(2)}, u32[]{:S(2)}) collective-permute-start(f32[320,640]{1,0:T(8,128)S(1)} %get-tuple-element.43), channel_id=1, source_target_pairs={{2,10},{3,11},{4,2},{5,3},{6,30},{7,31},{8,0},{9,1},{12,8},{13,9},... | collective-permute-start | bytes 2457608 | tf_op jit(solution)/shard_map/ppermute | solution.py:346
  76.5 40.8 %collective-permute-start.10 = (f32[320,640]{1,0:T(8,128)S(1)}, f32[320,640]{1,0:T(8,128)S(1)}, u32[]{:S(2)}, u32[]{:S(2)}) collective-permute-start(f32[320,640]{1,0:T(8,128)S(1)} %get-tuple-element.50), channel_id=1, source_target_pairs={{2,4},{3,5},{4,6},{5,7},{6,2},{7,3},{8,14},{9,15},{12,20},{13,21},... | collective-permute-start | bytes 2457608 | tf_op jit(solution)/shard_map/ppermute | solution.py:346
  77.8 39.5 %collective-permute-start.11 = (f32[320,640]{1,0:T(8,128)S(1)}, f32[320,640]{1,0:T(8,128)S(1)}, u32[]{:S(2)}, u32[]{:S(2)}) collective-permute-start(f32[320,640]{1,0:T(8,128)S(1)} %get-tuple-element.51), channel_id=1, source_target_pairs={{2,6},{3,7},{4,20},{5,21},{6,4},{7,5},{8,12},{9,13},{12,14},{13,15... | collective-permute-start | bytes 2457608 | tf_op jit(solution)/shard_map/ppermute | solution.py:346
  120.7 3.4 %collective-permute-start.12 = (f32[328,640]{1,0:T(8,128)S(1)}, f32[328,640]{1,0:T(8,128)S(1)}, u32[]{:S(2)}, u32[]{:S(2)}) collective-permute-start(f32[328,640]{1,0:T(8,128)S(1)} %shard_map.96), channel_id=1, source_target_pairs={{0,1},{1,0},{2,3},{3,2},{4,5},{5,4},{6,7},{7,6},{8,9},{9,8},{10,11... | collective-permute-start | bytes 2519048 | tf_op jit(solution)/shard_map/ppermute | solution.py:349
  124.2 4.7 %collective-permute-start.15 = (f32[8,320]{1,0:T(8,128)S(1)}, f32[8,320]{1,0:T(8,128)S(1)}, u32[]{:S(2)}, u32[]{:S(2)}) collective-permute-start(f32[8,320]{1,0:T(8,128)S(1)} %slice_add_fusion.1), channel_id=1, source_target_pairs={{0,24},{1,25},{2,26},{3,27},{4,28},{5,29},{6,30},{7,31},{8,16},{9,... | collective-permute-start | bytes 30728 | tf_op jit(solution)/shard_map/ppermute | solution.py:346
  124.8 4.0 %collective-permute-start.14 = (f32[8,320]{1,0:T(8,128)S(1)}, f32[8,320]{1,0:T(8,128)S(1)}, u32[]{:S(2)}, u32[]{:S(2)}) collective-permute-start(f32[8,320]{1,0:T(8,128)S(1)} %slice_add_fusion.1), channel_id=1, source_target_pairs={{0,16},{1,17},{2,18},{3,19},{4,20},{5,21},{6,22},{7,23},{8,24},{9,... | collective-permute-start | bytes 30728 | tf_op jit(solution)/shard_map/ppermute | solution.py:346
  125.7 3.7 %collective-permute-start.13 = (f32[8,320]{1,0:T(8,128)S(1)}, f32[8,320]{1,0:T(8,128)S(1)}, u32[]{:S(2)}, u32[]{:S(2)}) collective-permute-start(f32[8,320]{1,0:T(8,128)S(1)} %slice_add_fusion.1), channel_id=1, source_target_pairs={{0,8},{1,9},{2,10},{3,11},{4,12},{5,13},{6,14},{7,15},{8,0},{9,1},... | collective-permute-start | bytes 30728 | tf_op jit(solution)/shard_map/ppermute | solution.py:346
